TPU v7x, 32 devices: a whole 2x2x4 slice. The times are simulated.
32 devices in a mesh: loop: 16 (over z, x, core), tensor: 2 (over y).
Axes of the slice: x: 2, y: 2, z: 4, core: 2. Of those that a mesh axis runs over, the one named last changes fastest.
Arguments:
- grad_out: bfloat16 [2048, 4096], P('loop', 'tensor'), may hold values from -6 to 6
- saved_hidden: bfloat16 [416, 32768], P('tensor', 'loop'), may hold values from -6 to 6
- picked_tokens: int32 [2, 416], replicated, may hold values from 0 to 2047, as said below
- gate_values: float32 [2, 416], replicated, may hold values from 0.25 to 1
- in_weight: bfloat16 [4096, 32768], P(None, 'loop'), may hold values from -0.09375 to 0.09375
- out_weight: bfloat16 [32768, 4096], P('loop'), may hold values from -0.046875 to 0.046875
Outputs:
- input_grad: bfloat16 [2048, 4096], P('loop', 'tensor')
Inputs may be any that keep to these rules, and one draw needn't show every extreme that they name: Each row picked_tokens[e] lists 416 distinct token indices in ascending order; among the 128 tokens of one loop index (an aligned block) it names at most 28, and in every row some block holds exactly 28.
All inputs are finite; a program needn't handle non-finite values.
Results may differ from a plain program's by a relative error of at most 0.0032.
Values may be sent and summed in bfloat16 or wider, within the bound.
No kernel may reach another device: no remote copies, remote signals or barrier semaphores. Data moves between devices by JAX's collectives and lax.ppermute only.
A program may use at most 128 MiB of HBM per device.

v0:
```python
import math

import jax
import jax.numpy as jnp
from jax import lax
from jax.sharding import PartitionSpec as P

MOST = 28


slope_scale = math.sqrt(2.0 / math.pi)


def gelu_slope(values):
    inner = slope_scale * (values + 0.044715 * values * values * values)
    bent = jnp.tanh(inner)
    return 0.5 * (1.0 + bent) + 0.5 * values * (1.0 - bent * bent) * slope_scale * (
        1.0 + 0.134145 * values * values
    )


def block_slots(ordered, offset, length, slot_count):
    list_length = ordered.shape[-1]
    first_slot = jnp.sum((ordered < offset).astype(jnp.int32), axis=-1, keepdims=True)
    positions = first_slot + jnp.arange(slot_count, dtype=jnp.int32)
    clamped = jnp.minimum(positions, list_length - 1)
    local_rows = jnp.take_along_axis(ordered, clamped, axis=-1) - offset
    inside = (positions < list_length) & (local_rows < length)
    return (clamped, local_rows, inside)


def shards(grad_out, saved_hidden, picked_tokens, gate_values, in_weight, out_weight):
    home_rows, feature_cols = grad_out.shape
    loop_size = lax.axis_size("loop")
    expert_count = picked_tokens.shape[0]
    capacity = picked_tokens.shape[1]
    group_size = loop_size // expert_count
    loop_index = lax.axis_index("loop")
    expert_id = loop_index // group_size
    home_start = loop_index * home_rows
    own_picks = lax.dynamic_index_in_dim(picked_tokens, expert_id, 0, keepdims=False)
    block_starts = jnp.arange(loop_size, dtype=jnp.int32) * home_rows
    first_mine = jnp.sum((own_picks[None, :] < block_starts[:, None]).astype(jnp.int32), axis=1)
    clamped, local_rows, inside = block_slots(picked_tokens, home_start, home_rows, MOST)
    fetched = jnp.take(grad_out, jnp.clip(local_rows, 0, home_rows - 1), axis=0)
    slot_gates = jnp.take_along_axis(gate_values, clamped, axis=1)
    outgoing = jnp.where(
        inside[:, :, None], slot_gates[:, :, None] * fetched.astype(jnp.float32), 0.0
    ).astype(jnp.bfloat16)
    outgoing = jnp.repeat(outgoing, group_size, axis=0)
    arrived = lax.all_to_all(outgoing, "loop", split_axis=0, concat_axis=0, tiled=True)
    source_block = own_picks // home_rows
    matches = source_block[:, None] == jnp.arange(loop_size, dtype=jnp.int32)[None, :]
    block_first = jnp.sum(jnp.where(matches, first_mine[None, :], 0), axis=1)
    slot_index = source_block * MOST + jnp.arange(capacity, dtype=jnp.int32) - block_first
    scaled = jnp.take(arrived.reshape(loop_size * MOST, feature_cols), slot_index, axis=0)
    wide_rows = lax.all_to_all(scaled, "tensor", split_axis=0, concat_axis=1, tiled=True)
    act_grad = lax.dot_general(
        wide_rows, out_weight, (((1,), (1,)), ((), ())), preferred_element_type=jnp.float32
    )
    pre_grad = (act_grad * gelu_slope(saved_hidden.astype(jnp.float32))).astype(jnp.bfloat16)
    partial_grad = lax.dot_general(
        pre_grad, in_weight, (((1,), (1,)), ((), ())), preferred_element_type=jnp.float32
    )
    returned = lax.all_to_all(partial_grad, "tensor", split_axis=1, concat_axis=0, tiled=True)
    last_mine = jnp.sum(
        (own_picks[None, :] < block_starts[:, None] + home_rows).astype(jnp.int32), axis=1
    )
    positions = first_mine[:, None] + jnp.arange(MOST, dtype=jnp.int32)[None, :]
    inside_out = positions < last_mine[:, None]
    fetched_back = jnp.take(returned, jnp.minimum(positions, capacity - 1), axis=0)
    sending = jnp.where(inside_out[:, :, None], fetched_back, 0.0)
    landed = lax.all_to_all(sending, "loop", split_axis=0, concat_axis=0, tiled=True)
    home_clamped, home_local, home_inside = block_slots(picked_tokens, home_start, home_rows, MOST)
    target = jnp.repeat(jnp.where(home_inside, home_local, home_rows), group_size, axis=0)
    summed = (
        jnp.zeros((home_rows, feature_cols), jnp.float32)
        .at[target.reshape(-1)]
        .add(landed.reshape(-1, feature_cols), mode="drop")
    )
    return (grad_out.astype(jnp.float32) + summed).astype(jnp.bfloat16)


def solution(mesh):
    placed = (P("loop", "tensor"), P("tensor", "loop"), P(), P(), P(None, "loop"), P("loop", None))
    return jax.shard_map(
        shards, mesh=mesh, in_specs=placed, out_specs=P("loop", "tensor"), check_vma=False
    )
```

profile of v0, /device:TPU:11, one launch (start us, length us, event | category | flops | bytes accessed | tf_op | source)
XLA Modules:
  0.0 279.9 jit_solution(3408133938625639556)
XLA Ops:
  0.0 0.0 copy-start
  0.0 0.0 copy-start.3
  0.0 0.9 fusion.12
  0.9 0.1 fusion.17
  1.0 0.1 reshape.413
  1.0 1.8 gather_fusion.4
  2.8 0.1 reshape.416
  2.9 0.1 compare_and_fusion.2
  3.0 0.1 broadcast_select_fusion.2
  3.1 0.1 reshape.368
  3.2 0.0 copy-done.3
  3.2 0.7 gather_fusion
  3.9 0.1 reshape.367
  3.9 0.1 reshape.390
  4.0 0.0 copy-done
  4.0 1.1 gather_fusion.3
  5.1 0.1 reshape.393
  5.2 0.1 broadcast_select_fusion.1
  5.3 0.2 select_convert_fusion
  5.5 1.6 broadcast_in_dim.114
  7.1 0.0 copy-start.2
  7.1 6.7 %all-to-all-start = ((bf16[16,28,2048]{2,1,0:T(8,128)(2,1)}), bf16[16,28,2048]{2,1,0:T(8,128)(2,1)}, u32[]{:S(2)}, u32[]{:S(2)}) async-start(bf16[16,28,2048]{2,1,0:T(8,128)(2,1)} %bitcast.3), calls=%async_computation | async-start | bytes 4194304 | tf_op jit(solution)/shard_map/all_to_all | solution.py:51
  13.8 0.5 broadcast.491
  14.3 0.0 copy-done.2
  14.3 0.7 fusion.18
  15.0 0.7 convert_reduce_fusion
  15.7 0.1 select_reduce_fusion
  15.8 0.1 reduce_sum.48
  15.8 0.1 lt.165
  16.0 45.3 %all-to-all-done = bf16[16,28,2048]{2,1,0:T(8,128)(2,1)} async-done(((bf16[16,28,2048]{2,1,0:T(8,128)(2,1)}), bf16[16,28,2048]{2,1,0:T(8,128)(2,1)}, u32[]{:S(2)}, u32[]{:S(2)}) %all-to-all-start) | async-done | bytes 1835040 | tf_op jit(solution)/shard_map/all_to_all | solution.py:51
  61.3 2.5 reshape.358
  63.8 2.5 gather_fusion.1
  66.2 0.2 broadcast_select_fusion
  66.5 23.0 %all_to_all.45 = bf16[2,208,2048]{2,1,0:T(8,128)(2,1)S(1)} all-to-all(bf16[2,208,2048]{2,1,0:T(8,128)(2,1)S(1)} %broadcast_select_fusion), channel_id=1, replica_groups=mesh['loop'=16,'tensor'=2] {'tensor'}, dimensions={0} | all-to-all | bytes 3407872 | tf_op jit(solution)/shard_map/all_to_all | solution.py:57
  89.5 1.3 copy.18
  90.8 19.7 %fusion.19 = f32[208,4096]{1,0:T(8,128)S(1)} fusion(bf16[4096,2048]{1,0:T(8,128)(2,1)} %param.12, bf16[208,4096]{1,0:T(8,128)(2,1)} %bitcast.51, bf16[2048,4096]{1,0:T(8,128)(2,1)} %param.13, bf16[208,2048]{1,0:T(8,128)(2,1)} %param.9), kind=kOutput, calls=%fused_computation.81 | convolution fusion | flops 6987841536 | bytes 39518208 | tf_op jit(solution)/shard_map/dot_general | solution.py:62
  110.5 2.0 copy.20
  112.4 0.0 copy-start.5
  112.5 4.1 %all-to-all-start.2 = ((f32[208,2,2048]{2,0,1:T(8,128)}), f32[208,2,2048]{2,0,1:T(8,128)S(1)}, u32[]{:S(2)}, u32[]{:S(2)}) async-start(f32[208,2,2048]{2,0,1:T(8,128)} %bitcast.47), calls=%async_computation.2 | async-start | bytes 6815744 | tf_op jit(solution)/shard_map/all_to_all | solution.py:65
  116.6 0.1 compare_select_fusion
  116.7 0.1 reshape.384
  116.8 0.0 copy-done.5
  116.8 0.1 fusion.8
  116.8 37.5 %all-to-all-done.2 = f32[208,2,2048]{2,0,1:T(8,128)S(1)} async-done(((f32[208,2,2048]{2,0,1:T(8,128)}), f32[208,2,2048]{2,0,1:T(8,128)S(1)}, u32[]{:S(2)}, u32[]{:S(2)}) %all-to-all-start.2) | async-done | bytes 3407904 | tf_op jit(solution)/shard_map/all_to_all | solution.py:65
  154.4 3.4 %gather_fusion.2 = f32[448,2048]{1,0:T(8,128)} fusion(f32[416,2048]{1,0:T(8,128)S(1)} %bitcast.46, s32[1024]{0:T(1024)S(1)} %pad_clamp_fusion), kind=kCustom, calls=%fused_computation.3 | custom fusion | bytes 7341824 | tf_op jit(solution)/shard_map/jit(_take)/gather | solution.py:71
  157.8 4.5 %reshape.383 = f32[16,28,2048]{2,1,0:T(8,128)} reshape(f32[448,2048]{1,0:T(8,128)} %gather_fusion.2) | data formatting | bytes 7340032 | tf_op jit(solution)/shard_map/jit(_take)/gather | solution.py:71
  162.3 4.6 %select_select_fusion = f32[16,28,2048]{2,1,0:T(8,128)} fusion(f32[16,28,2048]{2,1,0:T(8,128)} %reshape.383, pred[16,28]{1,0:T(8,128)(4,1)S(1)} %get-tuple-element.16, pred[16,28]{1,0:T(8,128)(4,1)S(1)} %get-tuple-element.15), kind=kLoop, calls=%fused_computation.13 | loop fusion | flops 1835008 | bytes 7340928 | tf_op jit(solution)/shard_map/jit(_where)/select_n | solution.py:72
  166.9 0.0 copy-start.4
  166.9 6.9 %all-to-all-start.3 = ((f32[16,28,2048]{2,1,0:T(8,128)}), f32[16,28,2048]{2,1,0:T(8,128)}, u32[]{:S(2)}, u32[]{:S(2)}) async-start(f32[16,28,2048]{2,1,0:T(8,128)} %select_select_fusion), calls=%async_computation.3 | async-start | bytes 8388608 | tf_op jit(solution)/shard_map/all_to_all | solution.py:73
  173.8 0.0 copy-done.4
  173.8 0.1 convert_element_type.28
  173.9 0.1 reshape_reshape.3
  174.0 92.2 %all-to-all-done.3 = f32[16,28,2048]{2,1,0:T(8,128)} async-done(((f32[16,28,2048]{2,1,0:T(8,128)}), f32[16,28,2048]{2,1,0:T(8,128)}, u32[]{:S(2)}, u32[]{:S(2)}) %all-to-all-start.3) | async-done | bytes 3670048 | tf_op jit(solution)/shard_map/all_to_all | solution.py:73
  266.3 4.7 %reshape.400 = f32[448,2048]{1,0:T(8,128)} reshape(f32[16,28,2048]{2,1,0:T(8,128)} %all-to-all-done.3) | data formatting | bytes 7340032 | tf_op jit(solution)/shard_map/reshape | solution.py:79
  270.9 0.0 copy-start.1
  270.9 8.1 %scatter_fusion = f32[128,2048]{1,0:T(8,128)S(1)} fusion(f32[128,2048]{1,0:T(8,128)S(1)} %convert_element_type.28, s32[448]{0:T(512)S(1)} %bitcast.55, f32[448,2048]{1,0:T(8,128)} %reshape.400), kind=kCustom, calls=%fused_computation.5 | custom fusion | flops 917504 | bytes 11011840 | tf_op jit(solution)/shard_map/scatter-add | solution.py:79
  279.0 0.9 convert_element_type.36
  279.9 0.0 copy-done.1
  (9 shorter events, 0.1 us)
Async XLA Ops:
  0.0 4.0 %copy-start = (f32[2,416]{1,0:T(2,128)S(1)}, f32[2,416]{1,0:T(2,128)}, u32[]{:S(2)}) copy-start(f32[2,416]{1,0:T(2,128)} %param.11) | copy-start | bytes 9988
  0.0 3.2 %copy-start.3 = (bf16[128,2048]{1,0:T(8,128)(2,1)S(1)}, bf16[128,2048]{1,0:T(8,128)(2,1)}, u32[]{:S(2)}) copy-start(bf16[128,2048]{1,0:T(8,128)(2,1)} %param.8) | copy-start | bytes 1572868
  7.1 7.2 %copy-start.2 = (s32[2,416]{1,0:T(2,128)S(1)}, s32[2,416]{1,0:T(2,128)}, u32[]{:S(2)}) copy-start(s32[2,416]{1,0:T(2,128)} %param.10) | copy-start | bytes 9988
  7.1 54.2 %all-to-all-start = ((bf16[16,28,2048]{2,1,0:T(8,128)(2,1)}), bf16[16,28,2048]{2,1,0:T(8,128)(2,1)}, u32[]{:S(2)}, u32[]{:S(2)}) async-start(bf16[16,28,2048]{2,1,0:T(8,128)(2,1)} %bitcast.3), calls=%async_computation | async-start | bytes 4194304 | tf_op jit(solution)/shard_map/all_to_all | solution.py:51
  112.4 4.3 %copy-start.5 = (s32[16]{0:T(128)S(1)}, s32[16]{0:T(128)}, u32[]{:S(2)}) copy-start(s32[16]{0:T(128)} %get-tuple-element.6) | copy-start | bytes 196
  112.5 41.9 %all-to-all-start.2 = ((f32[208,2,2048]{2,0,1:T(8,128)}), f32[208,2,2048]{2,0,1:T(8,128)S(1)}, u32[]{:S(2)}, u32[]{:S(2)}) async-start(f32[208,2,2048]{2,0,1:T(8,128)} %bitcast.47), calls=%async_computation.2 | async-start | bytes 6815744 | tf_op jit(solution)/shard_map/all_to_all | solution.py:65
  166.9 6.9 %copy-start.4 = (bf16[128,2048]{1,0:T(8,128)(2,1)S(1)}, bf16[128,2048]{1,0:T(8,128)(2,1)}, u32[]{:S(2)}) copy-start(bf16[128,2048]{1,0:T(8,128)(2,1)} %param.8) | copy-start | bytes 1572868
  166.9 99.3 %all-to-all-start.3 = ((f32[16,28,2048]{2,1,0:T(8,128)}), f32[16,28,2048]{2,1,0:T(8,128)}, u32[]{:S(2)}, u32[]{:S(2)}) async-start(f32[16,28,2048]{2,1,0:T(8,128)} %select_select_fusion), calls=%async_computation.3 | async-start | bytes 8388608 | tf_op jit(solution)/shard_map/all_to_all | solution.py:73
  270.9 9.0 %copy-start.1 = (f32[2,416]{1,0:T(2,128)S(1)}, f32[2,416]{1,0:T(2,128)}, u32[]{:S(2)}) copy-start(f32[2,416]{1,0:T(2,128)} %param.11) | copy-start | bytes 9988
where the time goes:
time: 281 us; the launch traced here: 280 us
  waiting for transfers between devices  175 us (62%)
  local copies, waits for them, and re-layouts  27.9 us (10%)
  blocking collectives  23 us (8%)
  matrix products  19.7 us (7%)
  starting transfers between devices  17.7 us (6%)
  other arithmetic  16.4 us (6%)
    all_to_all x1, waiting for transfers between devices, shards(): lax.all_to_all(sending, 'loop', split_axis=0, concat_axis=0, tiled=True)  92.2 us
    all_to_all x1, waiting for transfers between devices, shards(): lax.all_to_all(outgoing, 'loop', split_axis=0, concat_axis=0, tiled=True)  45.3 us
    all_to_all x1, waiting for transfers between devices, shards(): lax.all_to_all(partial_grad, 'tensor', split_axis=1, concat_axis=0, tiled...  37.5 us
    all_to_all x1, blocking collectives, shards(): lax.all_to_all(scaled, 'tensor', split_axis=0, concat_axis=1, tiled=True)  23 us
    dot_general x1, matrix products, shards(): lax.dot_general(pre_grad, in_weight, (((1,), (1,)), ((), ())), preferred_...  19.7 us
    scatter-add x1, other arithmetic, shards(): summed = jnp.zeros((home_rows, feature_cols), jnp.float32).at[target.resh...  8.1 us
    gather x2, local copies, waits for them, and re-layouts, shards(): jnp.take(returned, jnp.minimum(positions, capacity - 1), axis=0)  7.92 us
    all_to_all x1, starting transfers between devices, shards(): lax.all_to_all(sending, 'loop', split_axis=0, concat_axis=0, tiled=True)  6.86 us
  transfers between devices with their start and end apart: 3, of which 3 were waited for; matrix products, arithmetic and copies ran while one was open for 1% of the time, Pallas kernels for 0%

commit v1 on v0

v1 whole, which is shorter than its diff:
```python
import math

import jax
import jax.numpy as jnp
from jax import lax
from jax.sharding import PartitionSpec as P

MOST = 28
BOTH = ("loop", "tensor")

slope_scale = math.sqrt(2.0 / math.pi)


def gelu_slope(values):
    inner = slope_scale * (values + 0.044715 * values * values * values)
    bent = jnp.tanh(inner)
    return 0.5 * (1.0 + bent) + 0.5 * values * (1.0 - bent * bent) * slope_scale * (
        1.0 + 0.134145 * values * values
    )


def rows_dot(left, right, out_type=jnp.float32):
    return lax.dot_general(
        left, right, (((1,), (1,)), ((), ())), preferred_element_type=jnp.float32
    ).astype(out_type)


def swap(values, distance):
    pairs = [(source, source ^ distance) for source in range(lax.axis_size("loop"))]
    return lax.ppermute(values, "loop", pairs)


def home_routes(expert_count):
    loop_size, tensor_size = lax.axis_size("loop"), lax.axis_size("tensor")
    blocks = loop_size // tensor_size
    group_size = loop_size // expert_count
    splits = group_size // blocks
    routes = []
    for turn in range(expert_count):
        pairs = []
        for loop_at in range(loop_size):
            for tensor_at in range(tensor_size):
                expert = (tensor_at + turn) % expert_count
                place = (loop_at % blocks) * splits + tensor_at // expert_count
                target = (expert * group_size + place) * tensor_size + loop_at // blocks
                pairs.append((loop_at * tensor_size + tensor_at, target))
        routes.append(pairs)
    return routes


def widen_rows(saved, halo):
    row_count = saved.shape[0]
    size = lax.axis_size("tensor")
    before, after = [], []
    for hop in range(1, -(-halo // row_count) + 1):
        part = min(row_count, halo - (hop - 1) * row_count)
        up = [(at, at + hop) for at in range(size - hop)]
        before.insert(0, lax.ppermute(saved[row_count - part :], "tensor", up))
        after.append(lax.ppermute(saved[:part], "tensor", [(b, a) for a, b in up]))
    return jnp.concatenate(before + [saved] + after, axis=0)


def shards(grad_out, saved_hidden, picked_tokens, gate_values, in_weight, out_weight):
    home_rows, feature_cols = grad_out.shape
    width = in_weight.shape[0]
    loop_size, tensor_size = lax.axis_size("loop"), lax.axis_size("tensor")
    expert_count, capacity = picked_tokens.shape
    blocks = loop_size // tensor_size
    group_size = loop_size // expert_count
    splits = group_size // blocks
    loop_index, tensor_index = lax.axis_index("loop"), lax.axis_index("tensor")
    expert_id, place = loop_index // group_size, loop_index % group_size
    routes = home_routes(expert_count)

    tokens = loop_index * home_rows + jnp.arange(home_rows, dtype=jnp.int32)
    same = picked_tokens[:, None, :] == tokens[None, :, None]
    picked_here = jnp.any(same, axis=2)
    gates = jnp.sum(jnp.where(same, gate_values[:, None, :], 0.0), axis=2)
    rank = jnp.cumsum(picked_here.astype(jnp.int32), axis=1) - 1
    slots = jnp.arange(MOST, dtype=jnp.int32)
    chosen = picked_here[:, None, :] & (rank[:, None, :] == slots[None, :, None])
    chosen = chosen.astype(jnp.bfloat16)
    wide = grad_out.astype(jnp.float32)

    arrived = []
    for turn in range(expert_count):
        expert = (tensor_index + turn) % expert_count
        gate = lax.dynamic_index_in_dim(gates, expert, 0, keepdims=False)
        pick = lax.dynamic_index_in_dim(chosen, expert, 0, keepdims=False)
        scaled = (gate[:, None] * wide).astype(jnp.bfloat16)
        outgoing = jnp.dot(pick, scaled, preferred_element_type=jnp.float32)
        arrived.append(lax.ppermute(outgoing.astype(jnp.bfloat16), BOTH, routes[turn]))
    arrived = jnp.stack(arrived)
    turns = (expert_id - jnp.arange(expert_count)) % expert_count
    mine = jnp.concatenate(
        [lax.dynamic_index_in_dim(arrived, turns[s], 0, keepdims=False) for s in range(expert_count)],
        axis=1,
    )

    cross = [mine] + [swap(mine, 2 * m) for m in range(1, group_size // 2)]
    pieces = []
    for piece in cross:
        pieces += [piece, swap(piece, 1)]
    if splits > 1:
        order = (place % splits) ^ jnp.arange(splits)
        rows = jnp.stack(pieces).reshape(blocks, splits, MOST, width // splits)
        rows = jnp.take(rows, order, axis=1).swapaxes(1, 2).reshape(blocks * MOST, width)
    else:
        rows = jnp.concatenate(pieces, axis=0)

    per_tensor = capacity // tensor_size
    halo = max(
        max(MOST * cut * blocks - cut * per_tensor, cut * per_tensor - capacity + MOST * (tensor_size - cut) * blocks)
        for cut in range(1, tensor_size)
    )
    window = widen_rows(saved_hidden, halo)
    own_picks = lax.dynamic_index_in_dim(picked_tokens, expert_id, 0, keepdims=False)
    block_ids = tensor_index * blocks + ((place // splits) ^ jnp.arange(blocks, dtype=jnp.int32))
    first = jnp.sum((own_picks[None, :] < (block_ids * home_rows)[:, None]).astype(jnp.int32), axis=1)
    offsets = (first[:, None] + slots[None, :]).reshape(-1) - tensor_index * per_tensor + halo
    take = offsets[:, None] == jnp.arange(window.shape[0], dtype=jnp.int32)[None, :]
    hidden = jnp.dot(take.astype(jnp.bfloat16), window, preferred_element_type=jnp.float32)

    act_grad = rows_dot(rows, out_weight)
    pre_grad = (act_grad * gelu_slope(hidden)).astype(jnp.bfloat16)
    partial = rows_dot(pre_grad, in_weight)

    if splits > 1:
        partial = partial.reshape(blocks, MOST, splits, width // splits).swapaxes(1, 2)
        partial = jnp.take(partial, order, axis=1)
    partial = partial.reshape(group_size // 2, 2, MOST, width // splits)
    got = swap(partial[:, 1].astype(jnp.bfloat16), 1)
    paired = partial[:, 0] + got.astype(jnp.float32)
    total = paired[0]
    for m in range(1, group_size // 2):
        total = total + swap(paired[m].astype(jnp.bfloat16), 2 * m).astype(jnp.float32)
    total = total.astype(jnp.bfloat16).reshape(MOST, expert_count, feature_cols)

    summed = wide
    for turn in range(expert_count):
        sending = lax.dynamic_index_in_dim(total, turns[turn], 1, keepdims=False)
        back = [(target, source) for source, target in routes[turn]]
        landed = lax.ppermute(sending, BOTH, back)
        expert = (tensor_index + turn) % expert_count
        pick = lax.dynamic_index_in_dim(chosen, expert, 0, keepdims=False)
        summed = summed + lax.dot_general(
            pick, landed, (((0,), (0,)), ((), ())), preferred_element_type=jnp.float32
        )
    return summed.astype(jnp.bfloat16)


def solution(mesh):
    placed = (P("loop", "tensor"), P("tensor", "loop"), P(), P(), P(None, "loop"), P("loop", None))
    return jax.shard_map(
        shards, mesh=mesh, in_specs=placed, out_specs=P("loop", "tensor"), check_vma=False
    )
```

time: 281 us -> 106 us (0.38)
  the two profiles are of different devices: /device:TPU:11 before, /device:TPU:0 now
where the time goes in v1:
time: 106 us
  waiting for transfers between devices  33.5 us (32%)
  starting transfers between devices  24.1 us (23%)
  matrix products  23.7 us (22%)
  local copies, waits for them, and re-layouts  15.1 us (14%)
  other arithmetic  5.07 us (5%)
  between operations  4.07 us (4%)
    ppermute x11, waiting for transfers between devices, swap(): return lax.ppermute(values, 'loop', pairs)  23.8 us
    dot_general x1, matrix products, rows_dot(): lax.dot_general(left, right, (((1,), (1,)), ((), ())), preferred_element_...  17.8 us
    ppermute x2, waiting for transfers between devices, shards(): landed = lax.ppermute(sending, BOTH, back)  9.74 us
    ppermute x11, starting transfers between devices, swap(): return lax.ppermute(values, 'loop', pairs)  7.77 us
    ppermute x2, starting transfers between devices, shards(): lax.ppermute(outgoing.astype(jnp.bfloat16), BOTH, routes[turn])  6.96 us
    concatenate x1, local copies, waits for them, and re-layouts, shards(): rows = jnp.concatenate(pieces, axis=0)  5.16 us
    ppermute x1, starting transfers between devices, widen_rows(): before.insert(0, lax.ppermute(saved[row_count - part:], 'tensor', up))  4.87 us
    reshape x1, local copies, waits for them, and re-layouts, shards(): partial = partial.reshape(group_size // 2, 2, MOST, width // splits)  3.64 us
  transfers between devices with their start and end apart: 17, of which 6 were waited for; matrix products, arithmetic and copies ran while one was open for 8% of the time, Pallas kernels for 0%

profile of v1, /device:TPU:0, one launch (start us, length us, event | category | flops | bytes accessed | tf_op | source)
XLA Modules:
  0.0 105.6 jit_solution(3796515867783487203)
XLA Ops:
  0.0 1.0 fusion.52
  1.0 4.9 %collective-permute-start.9 = (bf16[16,2048]{1,0:T(8,128)(2,1)S(1)}, bf16[16,2048]{1,0:T(8,128)(2,1)S(1)}, u32[]{:S(2)}, u32[]{:S(2)}) collective-permute-start(bf16[16,2048]{1,0:T(8,128)(2,1)S(1)} %get-tuple-element.10), channel_id=1, source_target_pairs={{0,1},{2,3},{4,5},{6,7},{8,9},{10,11},{12,13},{14,15},{16,17},{18,... | collective-permute-start | bytes 196616 | tf_op jit(solution)/shard_map/ppermute | solution.py:58
  5.8 1.3 %collective-permute-start.10 = (bf16[16,2048]{1,0:T(8,128)(2,1)S(1)}, bf16[16,2048]{1,0:T(8,128)(2,1)S(1)}, u32[]{:S(2)}, u32[]{:S(2)}) collective-permute-start(bf16[16,2048]{1,0:T(8,128)(2,1)S(1)} %get-tuple-element.11), channel_id=1, source_target_pairs={{1,0},{3,2},{5,4},{7,6},{9,8},{11,10},{13,12},{15,14},{17,16},{19,... | collective-permute-start | bytes 196616 | tf_op jit(solution)/shard_map/ppermute | solution.py:59
  7.2 0.9 compare_reduce_fusion
  8.1 1.0 fusion.26
  9.1 0.3 reduce_window_sum.11
  9.4 1.3 %convolution_convert_fusion.1 = bf16[28,2048]{1,0:T(8,128)(2,1)S(1)} fusion(bf16[128,2048]{1,0:T(8,128)(2,1)} %param.6, f32[128]{0:T(128)S(1)} %get-tuple-element.17, pred[2,28,128]{2,1,0:T(8,128)(4,1)S(1)} %fusion.32, s32[]{:T(128)S(6)} %select_n.61), kind=kOutput, calls=%fused_computation.8 | convolution fusion | flops 15523840 | bytes 643588 | tf_op jit(solution)/shard_map/dot_general | solution.py:91
  10.8 0.7 collective-permute-start
  11.4 1.3 %convolution_convert_fusion = bf16[28,2048]{1,0:T(8,128)(2,1)S(1)} fusion(bf16[128,2048]{1,0:T(8,128)(2,1)} %param.6, f32[128]{0:T(128)S(1)} %get-tuple-element.16, pred[2,28,128]{2,1,0:T(8,128)(4,1)S(1)} %fusion.32, s32[]{:T(128)S(6)} %select_n.64), kind=kOutput, calls=%fused_computation.7 | convolution fusion | flops 15523840 | bytes 643588 | tf_op jit(solution)/shard_map/dot_general | solution.py:91
  12.8 6.3 %collective-permute-start.1 = (bf16[28,2048]{1,0:T(8,128)(2,1)S(1)}, bf16[28,2048]{1,0:T(8,128)(2,1)S(1)}, u32[]{:S(2)}, u32[]{:S(2)}) collective-permute-start(bf16[28,2048]{1,0:T(8,128)(2,1)S(1)} %convolution_convert_fusion), channel_id=1, source_target_pairs={{0,16},{1,0},{2,18},{3,2},{4,20},{5,4},{6,22},{7,6},{8,24},{9,8},{... | collective-permute-start | bytes 344072 | tf_op jit(solution)/shard_map/ppermute | solution.py:92
  19.1 0.6 fusion.53
  23.5 0.7 constant_dynamic-slice_fusion.2
  24.2 0.0 collective-permute-done
  24.2 0.0 collective-permute-done.1
  24.3 0.1 fusion.30
  24.4 2.6 %collective-permute-start.7 = (bf16[28,4096]{1,0:T(8,128)(2,1)S(1)}, bf16[28,4096]{1,0:T(8,128)(2,1)S(1)}, u32[]{:S(2)}, u32[]{:S(2)}) collective-permute-start(bf16[28,4096]{1,0:T(8,128)(2,1)S(1)} %pad_maximum_fusion), channel_id=1, source_target_pairs={{0,12},{2,14},{4,8},{6,10},{8,4},{10,6},{12,0},{14,2},{16,28},{18,... | collective-permute-start | bytes 688136 | tf_op jit(solution)/shard_map/ppermute | solution.py:30
  27.0 0.4 collective-permute-start.5
  27.4 0.5 collective-permute-start.3
  28.0 0.2 convert_reduce_fusion
  28.1 0.1 subtract_add_fusion
  28.2 0.1 add.156
  28.3 0.0 collective-permute-done.9
  28.3 0.1 collective-permute-start.2
  28.4 6.3 %collective-permute-done.7 = bf16[28,4096]{1,0:T(8,128)(2,1)S(1)} collective-permute-done((bf16[28,4096]{1,0:T(8,128)(2,1)S(1)}, bf16[28,4096]{1,0:T(8,128)(2,1)S(1)}, u32[]{:S(2)}, u32[]{:S(2)}) %collective-permute-start.7) | collective-permute-done | bytes 229408 | tf_op jit(solution)/shard_map/ppermute | solution.py:30
  34.7 0.0 collective-permute-start.8
  34.7 3.3 %collective-permute-done.5 = bf16[28,4096]{1,0:T(8,128)(2,1)S(1)} collective-permute-done((bf16[28,4096]{1,0:T(8,128)(2,1)S(1)}, bf16[28,4096]{1,0:T(8,128)(2,1)S(1)}, u32[]{:S(2)}, u32[]{:S(2)}) %collective-permute-start.5) | collective-permute-done | bytes 229408 | tf_op jit(solution)/shard_map/ppermute | solution.py:30
  38.0 0.0 collective-permute-start.6
  38.0 0.0 collective-permute-done.3
  38.0 0.5 collective-permute-start.4
  38.5 0.0 collective-permute-done.10
  38.5 1.7 %fusion.12 = f32[224,2048]{1,0:T(8,128)} fusion(bf16[16,2048]{1,0:T(8,128)(2,1)S(1)} %collective-permute-done.10, bf16[208,2048]{1,0:T(8,128)(2,1)S(1)} %copy-done.2, bf16[16,2048]{1,0:T(8,128)(2,1)S(1)} %collective-permute-done.9, s32[224]{0:T(256)S(1)} %add.156), kind=kOutput, calls=%fused_computation.22 | convolution fusion | flops 223203840 | bytes 2818944 | tf_op jit(solution)/shard_map/dot_general | solution.py:122
  40.2 0.0 collective-permute-done.2
  40.2 0.0 collective-permute-done.8
  40.2 0.0 collective-permute-done.6
  40.2 0.0 copy-start.1
  40.3 0.7 copy-done.1
  41.0 0.0 collective-permute-done.4
  41.0 5.2 %concatenate.10 = bf16[224,4096]{1,0:T(8,128)(2,1)S(1)} concatenate(bf16[28,4096]{1,0:T(8,128)(2,1)S(1)} %pad_maximum_fusion, bf16[28,4096]{1,0:T(8,128)(2,1)S(1)} %collective-permute-done.2, bf16[28,4096]{1,0:T(8,128)(2,1)S(1)} %collective-permute-done.3, bf16[28,4096]{1,0:T(8,128)(2,1)} %collective-permute-done.4, bf16[28,4096]{1,0:T(8,128)(2,1)S(1)} %collective-permute-done.5, ...), dimensions={0} | concatenate | bytes 3670016 | tf_op jit(solution)/shard_map/concatenate | solution.py:109
  46.1 17.8 %fusion.54 = f32[224,4096]{1,0:T(8,128)} fusion(bf16[4096,2048]{1,0:T(8,128)(2,1)} %param.10, bf16[224,4096]{1,0:T(8,128)(2,1)S(1)} %concatenate.10, bf16[2048,4096]{1,0:T(8,128)(2,1)} %param.11, f32[224,2048]{1,0:T(8,128)} %fusion.12), kind=kOutput, calls=%fused_computation.89 | convolution fusion | flops 7524909056 | bytes 40894464 | tf_op jit(solution)/shard_map/dot_general | solution.py:23
  64.0 3.6 %reshape.56 = f32[4,2,28,4096]{3,2,1,0:T(8,128)} reshape(f32[224,4096]{1,0:T(8,128)} %fusion.54) | data formatting | bytes 7340032 | tf_op jit(solution)/shard_map/reshape | solution.py:131
  67.6 1.7 %fusion.11 = bf16[4,28,4096]{2,1,0:T(8,128)(2,1)S(1)} fusion(f32[4,2,28,4096]{3,2,1,0:T(8,128)} %reshape.56), kind=kLoop, calls=%fused_computation.21 | loop fusion | bytes 1835008 | tf_op jit(solution)/shard_map/convert_element_type | solution.py:132
  69.3 0.7 copy.15
  70.0 0.1 collective-permute-start.11
  70.1 2.5 %collective-permute-done.11 = bf16[4,28,4096]{2,0,1:T(4,128)(2,1)S(1)} collective-permute-done((bf16[4,28,4096]{2,0,1:T(4,128)(2,1)S(1)}, bf16[4,28,4096]{2,0,1:T(4,128)(2,1)S(1)}, u32[]{:S(2)}, u32[]{:S(2)}) %collective-permute-start.11) | collective-permute-done | bytes 917536 | tf_op jit(solution)/shard_map/ppermute | solution.py:30
  72.6 2.3 %fusion.50 = (bf16[4,28,4096]{2,1,0:T(8,128)(2,1)S(1)}, f32[4,28,4096]{2,1,0:T(8,128)S(1)}) fusion(bf16[4,28,4096]{2,0,1:T(4,128)(2,1)S(1)} %collective-permute-done.11, f32[4,2,28,4096]{3,2,1,0:T(8,128)} %reshape.56), kind=kLoop, calls=%fused_computation.86 | loop fusion | flops 1376256 | bytes 5505024 | tf_op jit(solution)/shard_map/convert.2
  74.9 0.1 slice_bitcast_fusion.4
  74.9 1.1 %collective-permute-start.12 = (bf16[28,4096]{1,0:T(8,128)(2,1)S(1)}, bf16[28,4096]{1,0:T(8,128)(2,1)S(1)}, u32[]{:S(2)}, u32[]{:S(2)}) collective-permute-start(bf16[28,4096]{1,0:T(8,128)(2,1)S(1)} %get-tuple-element.7), channel_id=1, source_target_pairs={{0,4},{2,6},{4,0},{6,2},{8,12},{10,14},{12,8},{14,10},{16,20},{18,... | collective-permute-start | bytes 688136 | tf_op jit(solution)/shard_map/ppermute | solution.py:30
  76.1 2.1 %collective-permute-start.14 = (bf16[28,4096]{1,0:T(8,128)(2,1)S(1)}, bf16[28,4096]{1,0:T(8,128)(2,1)S(1)}, u32[]{:S(2)}, u32[]{:S(2)}) collective-permute-start(bf16[28,4096]{1,0:T(8,128)(2,1)S(1)} %get-tuple-element.8), channel_id=1, source_target_pairs={{0,12},{2,14},{4,8},{6,10},{8,4},{10,6},{12,0},{14,2},{16,28},{18,... | collective-permute-start | bytes 688136 | tf_op jit(solution)/shard_map/ppermute | solution.py:30
  78.1 0.4 collective-permute-start.13
  78.5 10.5 %collective-permute-done.12 = bf16[28,4096]{1,0:T(8,128)(2,1)S(1)} collective-permute-done((bf16[28,4096]{1,0:T(8,128)(2,1)S(1)}, bf16[28,4096]{1,0:T(8,128)(2,1)S(1)}, u32[]{:S(2)}, u32[]{:S(2)}) %collective-permute-start.12) | collective-permute-done | bytes 229408 | tf_op jit(solution)/shard_map/ppermute | solution.py:30
  89.0 0.0 collective-permute-done.14
  89.0 1.2 %collective-permute-done.13 = bf16[28,4096]{1,0:T(8,128)(2,1)S(1)} collective-permute-done((bf16[28,4096]{1,0:T(8,128)(2,1)S(1)}, bf16[28,4096]{1,0:T(8,128)(2,1)S(1)}, u32[]{:S(2)}, u32[]{:S(2)}) %collective-permute-start.13) | collective-permute-done | bytes 229408 | tf_op jit(solution)/shard_map/ppermute | solution.py:30
  90.2 0.1 fusion.23
  90.3 0.0 copy-start
  90.4 0.1 reshape.57
  90.5 0.5 constant_dynamic-slice_fusion.1
  91.0 0.1 copy.25
  91.1 2.5 %collective-permute-start.16 = (bf16[28,2048]{1,0:T(8,128)(2,1)S(1)}, bf16[28,2048]{1,0:T(8,128)(2,1)S(1)}, u32[]{:S(2)}, u32[]{:S(2)}) collective-permute-start(bf16[28,2048]{1,0:T(8,128)(2,1)S(1)} %bitcast.68), channel_id=1, source_target_pairs={{16,0},{0,1},{18,2},{2,3},{20,4},{4,5},{22,6},{6,7},{24,8},{8,9},{... | collective-permute-start | bytes 344072 | tf_op jit(solution)/shard_map/ppermute | solution.py:143
  93.6 0.1 copy.26
  93.7 0.7 collective-permute-start.15
  94.3 9.7 %collective-permute-done.16 = bf16[28,2048]{1,0:T(8,128)(2,1)S(1)} collective-permute-done((bf16[28,2048]{1,0:T(8,128)(2,1)S(1)}, bf16[28,2048]{1,0:T(8,128)(2,1)S(1)}, u32[]{:S(2)}, u32[]{:S(2)}) %collective-permute-start.16) | collective-permute-done | bytes 114720 | tf_op jit(solution)/shard_map/ppermute | solution.py:143
  104.1 0.3 fusion.33
  104.4 0.0 collective-permute-done.15
  104.4 1.2 %fusion.2 = bf16[128,2048]{1,0:T(8,128)(2,1)} fusion(f32[128,2048]{1,0:T(8,128)S(1)} %fusion.33, bf16[28,2048]{1,0:T(8,128)(2,1)S(1)} %collective-permute-done.15, bf16[128,2048]{1,0:T(8,128)(2,1)S(1)} %copy-done, pred[2,28,128]{2,1,0:T(8,128)(4,1)S(1)} %fusion.32, s32[]{:T(128)S(6)} %select_n.61), kind=kOutput, calls=%fused_computation.6 | convolution fusion | flops 15728640 | bytes 2232324 | tf_op jit(solution)/shard_map/dot_general | solution.py:146
  (11 shorter events, 0.1 us)
Async XLA Ops:
  0.0 38.5 %copy-start.2 = (bf16[208,2048]{1,0:T(8,128)(2,1)S(1)}, bf16[208,2048]{1,0:T(8,128)(2,1)}, u32[]{:S(2)}) copy-start(bf16[208,2048]{1,0:T(8,128)(2,1)} %param.7) | copy-start | bytes 2555908
  1.0 27.3 %collective-permute-start.9 = (bf16[16,2048]{1,0:T(8,128)(2,1)S(1)}, bf16[16,2048]{1,0:T(8,128)(2,1)S(1)}, u32[]{:S(2)}, u32[]{:S(2)}) collective-permute-start(bf16[16,2048]{1,0:T(8,128)(2,1)S(1)} %get-tuple-element.10), channel_id=1, source_target_pairs={{0,1},{2,3},{4,5},{6,7},{8,9},{10,11},{12,13},{14,15},{16,17},{18,... | collective-permute-start | bytes 196616 | tf_op jit(solution)/shard_map/ppermute | solution.py:58
  5.8 32.7 %collective-permute-start.10 = (bf16[16,2048]{1,0:T(8,128)(2,1)S(1)}, bf16[16,2048]{1,0:T(8,128)(2,1)S(1)}, u32[]{:S(2)}, u32[]{:S(2)}) collective-permute-start(bf16[16,2048]{1,0:T(8,128)(2,1)S(1)} %get-tuple-element.11), channel_id=1, source_target_pairs={{1,0},{3,2},{5,4},{7,6},{9,8},{11,10},{13,12},{15,14},{17,16},{19,... | collective-permute-start | bytes 196616 | tf_op jit(solution)/shard_map/ppermute | solution.py:59
  10.8 13.5 %collective-permute-start = (bf16[28,2048]{1,0:T(8,128)(2,1)S(1)}, bf16[28,2048]{1,0:T(8,128)(2,1)S(1)}, u32[]{:S(2)}, u32[]{:S(2)}) collective-permute-start(bf16[28,2048]{1,0:T(8,128)(2,1)S(1)} %convolution_convert_fusion.1), channel_id=1, source_target_pairs={{0,0},{1,16},{2,2},{3,18},{4,4},{5,20},{6,6},{7,22},{8,8},{9,24},{... | collective-permute-start | bytes 344072 | tf_op jit(solution)/shard_map/ppermute | solution.py:92
  12.8 11.5 %collective-permute-start.1 = (bf16[28,2048]{1,0:T(8,128)(2,1)S(1)}, bf16[28,2048]{1,0:T(8,128)(2,1)S(1)}, u32[]{:S(2)}, u32[]{:S(2)}) collective-permute-start(bf16[28,2048]{1,0:T(8,128)(2,1)S(1)} %convolution_convert_fusion), channel_id=1, source_target_pairs={{0,16},{1,0},{2,18},{3,2},{4,20},{5,4},{6,22},{7,6},{8,24},{9,8},{... | collective-permute-start | bytes 344072 | tf_op jit(solution)/shard_map/ppermute | solution.py:92
  24.4 10.2 %collective-permute-start.7 = (bf16[28,4096]{1,0:T(8,128)(2,1)S(1)}, bf16[28,4096]{1,0:T(8,128)(2,1)S(1)}, u32[]{:S(2)}, u32[]{:S(2)}) collective-permute-start(bf16[28,4096]{1,0:T(8,128)(2,1)S(1)} %pad_maximum_fusion), channel_id=1, source_target_pairs={{0,12},{2,14},{4,8},{6,10},{8,4},{10,6},{12,0},{14,2},{16,28},{18,... | collective-permute-start | bytes 688136 | tf_op jit(solution)/shard_map/ppermute | solution.py:30
  27.0 11.0 %collective-permute-start.5 = (bf16[28,4096]{1,0:T(8,128)(2,1)S(1)}, bf16[28,4096]{1,0:T(8,128)(2,1)S(1)}, u32[]{:S(2)}, u32[]{:S(2)}) collective-permute-start(bf16[28,4096]{1,0:T(8,128)(2,1)S(1)} %pad_maximum_fusion), channel_id=1, source_target_pairs={{0,8},{2,10},{4,12},{6,14},{8,0},{10,2},{12,4},{14,6},{16,24},{18,... | collective-permute-start | bytes 688136 | tf_op jit(solution)/shard_map/ppermute | solution.py:30
  27.4 10.6 %collective-permute-start.3 = (bf16[28,4096]{1,0:T(8,128)(2,1)S(1)}, bf16[28,4096]{1,0:T(8,128)(2,1)S(1)}, u32[]{:S(2)}, u32[]{:S(2)}) collective-permute-start(bf16[28,4096]{1,0:T(8,128)(2,1)S(1)} %pad_maximum_fusion), channel_id=1, source_target_pairs={{0,4},{2,6},{4,0},{6,2},{8,12},{10,14},{12,8},{14,10},{16,20},{18,... | collective-permute-start | bytes 688136 | tf_op jit(solution)/shard_map/ppermute | solution.py:30
  28.3 11.9 %collective-permute-start.2 = (bf16[28,4096]{1,0:T(8,128)(2,1)S(1)}, bf16[28,4096]{1,0:T(8,128)(2,1)S(1)}, u32[]{:S(2)}, u32[]{:S(2)}) collective-permute-start(bf16[28,4096]{1,0:T(8,128)(2,1)S(1)} %pad_maximum_fusion), channel_id=1, source_target_pairs={{0,2},{2,0},{4,6},{6,4},{8,10},{10,8},{12,14},{14,12},{16,18},{18,... | collective-permute-start | bytes 688136 | tf_op jit(solution)/shard_map/ppermute | solution.py:30
  34.7 5.6 %collective-permute-start.8 = (bf16[28,4096]{1,0:T(8,128)(2,1)S(1)}, bf16[28,4096]{1,0:T(8,128)(2,1)S(1)}, u32[]{:S(2)}, u32[]{:S(2)}) collective-permute-start(bf16[28,4096]{1,0:T(8,128)(2,1)S(1)} %collective-permute-done.7), channel_id=1, source_target_pairs={{0,2},{2,0},{4,6},{6,4},{8,10},{10,8},{12,14},{14,12},{16,18},{18,... | collective-permute-start | bytes 688136 | tf_op jit(solution)/shard_map/ppermute | solution.py:30
  38.0 2.3 %collective-permute-start.6 = (bf16[28,4096]{1,0:T(8,128)(2,1)S(1)}, bf16[28,4096]{1,0:T(8,128)(2,1)S(1)}, u32[]{:S(2)}, u32[]{:S(2)}) collective-permute-start(bf16[28,4096]{1,0:T(8,128)(2,1)S(1)} %collective-permute-done.5), channel_id=1, source_target_pairs={{0,2},{2,0},{4,6},{6,4},{8,10},{10,8},{12,14},{14,12},{16,18},{18,... | collective-permute-start | bytes 688136 | tf_op jit(solution)/shard_map/ppermute | solution.py:30
  38.0 3.0 %collective-permute-start.4 = (bf16[28,4096]{1,0:T(8,128)(2,1)S(1)}, bf16[28,4096]{1,0:T(8,128)(2,1)}, u32[]{:S(2)}, u32[]{:S(2)}) collective-permute-start(bf16[28,4096]{1,0:T(8,128)(2,1)S(1)} %collective-permute-done.3), channel_id=1, source_target_pairs={{0,2},{2,0},{4,6},{6,4},{8,10},{10,8},{12,14},{14,12},{16,18},{18,... | collective-permute-start | bytes 688136 | tf_op jit(solution)/shard_map/ppermute | solution.py:30
  40.2 0.7 copy-start.1
  70.0 2.5 %collective-permute-start.11 = (bf16[4,28,4096]{2,0,1:T(4,128)(2,1)S(1)}, bf16[4,28,4096]{2,0,1:T(4,128)(2,1)S(1)}, u32[]{:S(2)}, u32[]{:S(2)}) collective-permute-start(bf16[4,28,4096]{2,0,1:T(4,128)(2,1)S(1)} %copy.15), channel_id=1, source_target_pairs={{0,2},{2,0},{4,6},{6,4},{8,10},{10,8},{12,14},{14,12},{16,18},{18,... | collective-permute-start | bytes 2752520 | tf_op jit(solution)/shard_map/ppermute | solution.py:30
  74.9 14.0 %collective-permute-start.12 = (bf16[28,4096]{1,0:T(8,128)(2,1)S(1)}, bf16[28,4096]{1,0:T(8,128)(2,1)S(1)}, u32[]{:S(2)}, u32[]{:S(2)}) collective-permute-start(bf16[28,4096]{1,0:T(8,128)(2,1)S(1)} %get-tuple-element.7), channel_id=1, source_target_pairs={{0,4},{2,6},{4,0},{6,2},{8,12},{10,14},{12,8},{14,10},{16,20},{18,... | collective-permute-start | bytes 688136 | tf_op jit(solution)/shard_map/ppermute | solution.py:30
  76.1 12.9 %collective-permute-start.14 = (bf16[28,4096]{1,0:T(8,128)(2,1)S(1)}, bf16[28,4096]{1,0:T(8,128)(2,1)S(1)}, u32[]{:S(2)}, u32[]{:S(2)}) collective-permute-start(bf16[28,4096]{1,0:T(8,128)(2,1)S(1)} %get-tuple-element.8), channel_id=1, source_target_pairs={{0,12},{2,14},{4,8},{6,10},{8,4},{10,6},{12,0},{14,2},{16,28},{18,... | collective-permute-start | bytes 688136 | tf_op jit(solution)/shard_map/ppermute | solution.py:30
  78.1 12.1 %collective-permute-start.13 = (bf16[28,4096]{1,0:T(8,128)(2,1)S(1)}, bf16[28,4096]{1,0:T(8,128)(2,1)S(1)}, u32[]{:S(2)}, u32[]{:S(2)}) collective-permute-start(bf16[28,4096]{1,0:T(8,128)(2,1)S(1)} %get-tuple-element.9), channel_id=1, source_target_pairs={{0,8},{2,10},{4,12},{6,14},{8,0},{10,2},{12,4},{14,6},{16,24},{18,... | collective-permute-start | bytes 688136 | tf_op jit(solution)/shard_map/ppermute | solution.py:30
  90.3 14.1 %copy-start = (bf16[128,2048]{1,0:T(8,128)(2,1)S(1)}, bf16[128,2048]{1,0:T(8,128)(2,1)}, u32[]{:S(2)}) copy-start(bf16[128,2048]{1,0:T(8,128)(2,1)} %param.6) | copy-start | bytes 1572868
  91.1 13.0 %collective-permute-start.16 = (bf16[28,2048]{1,0:T(8,128)(2,1)S(1)}, bf16[28,2048]{1,0:T(8,128)(2,1)S(1)}, u32[]{:S(2)}, u32[]{:S(2)}) collective-permute-start(bf16[28,2048]{1,0:T(8,128)(2,1)S(1)} %bitcast.68), channel_id=1, source_target_pairs={{16,0},{0,1},{18,2},{2,3},{20,4},{4,5},{22,6},{6,7},{24,8},{8,9},{... | collective-permute-start | bytes 344072 | tf_op jit(solution)/shard_map/ppermute | solution.py:143
  93.7 10.8 %collective-permute-start.15 = (bf16[28,2048]{1,0:T(8,128)(2,1)S(1)}, bf16[28,2048]{1,0:T(8,128)(2,1)S(1)}, u32[]{:S(2)}, u32[]{:S(2)}) collective-permute-start(bf16[28,2048]{1,0:T(8,128)(2,1)S(1)} %bitcast.69), channel_id=1, source_target_pairs={{0,0},{16,1},{2,2},{18,3},{4,4},{20,5},{6,6},{22,7},{8,8},{24,9},{... | collective-permute-start | bytes 344072 | tf_op jit(solution)/shard_map/ppermute | solution.py:143

commit v2 on v0

v2 whole, which is shorter than its diff:
```python
import functools
import math

import jax
import jax.numpy as jnp
from jax import lax
from jax.experimental import pallas as pl
from jax.experimental.pallas import tpu as pltpu
from jax.sharding import PartitionSpec as P

MOST = 28
PADDED = 32
BOTH = ("loop", "tensor")
VMEM = pl.BlockSpec(memory_space=pltpu.VMEM)
LEFT = pl.BlockSpec(memory_space=pl.ANY)

slope_scale = math.sqrt(2.0 / math.pi)


def gelu_slope(values):
    inner = slope_scale * (values + 0.044715 * values * values * values)
    bent = jnp.tanh(inner)
    return 0.5 * (1.0 + bent) + 0.5 * values * (1.0 - bent * bent) * slope_scale * (
        1.0 + 0.134145 * values * values
    )


def rows_dot(left, right):
    return lax.dot_general(left, right, (((1,), (1,)), ((), ())), preferred_element_type=jnp.float32)


def kernel_call(body, out_shape, operands, scratch=(), flops=0, vmem=4, left=0):
    nbytes = sum(o.size * o.dtype.itemsize for o in operands)
    operands = [
        pltpu.with_memory_space_constraint(o, pltpu.HBM) if at < left else o
        for at, o in enumerate(operands)
    ]
    return pl.pallas_call(
        body,
        out_shape=out_shape,
        in_specs=[LEFT] * left + [VMEM] * (len(operands) - left),
        out_specs=jax.tree.map(lambda _: VMEM, out_shape),
        scratch_shapes=scratch,
        cost_estimate=pl.CostEstimate(flops=flops, bytes_accessed=nbytes, transcendentals=0),
        compiler_params=pltpu.CompilerParams(vmem_limit_bytes=vmem << 20),
    )(*operands)


def after_all(values, others):
    values = tuple(values)
    return lax.optimization_barrier((values, tuple(others)))[0]


def swap(values, distance):
    pairs = [(source, source ^ distance) for source in range(lax.axis_size("loop"))]
    return lax.ppermute(values, "loop", pairs)


def home_routes(expert_count):
    loop_size, tensor_size = lax.axis_size("loop"), lax.axis_size("tensor")
    blocks = loop_size // tensor_size
    group_size = loop_size // expert_count
    splits = group_size // blocks
    routes = []
    for turn in range(expert_count):
        pairs = []
        for loop_at in range(loop_size):
            for tensor_at in range(tensor_size):
                expert = (tensor_at + turn) % expert_count
                place = (loop_at % blocks) * splits + tensor_at // expert_count
                target = (expert * group_size + place) * tensor_size + loop_at // blocks
                pairs.append((loop_at * tensor_size + tensor_at, target))
        routes.append(pairs)
    return routes


def home_slots(picks, start, home_rows):
    capacity = picks.shape[1]
    first = jnp.sum((picks < start).astype(jnp.int32), axis=1, keepdims=True)
    slot = lax.broadcasted_iota(jnp.int32, (PADDED, capacity), 0)
    listed = lax.broadcasted_iota(jnp.int32, (PADDED, capacity), 1) == first + slot
    local = jnp.sum(jnp.where(listed, picks - start + 1, 0), axis=1, keepdims=True) - 1
    tokens = lax.broadcasted_iota(jnp.int32, (PADDED, home_rows), 1)
    return listed, (tokens == local).astype(jnp.bfloat16)


def prepare_kernel(grad_from, picked_from, gates_from, saved_from, *refs):
    outs, edge, (grad, picked, gates, arrived) = refs[:-5], refs[-5], refs[-4:]
    expert_count = len(outs)
    spare = saved_from.shape[0] - edge.shape[0]
    first = jnp.where(lax.axis_index("tensor") == 0, spare, 0)
    saved_rows = saved_from.at[pl.ds(pl.multiple_of(first, 16), edge.shape[0]), :]
    copies = [
        pltpu.make_async_copy(source, target, arrived.at[at])
        for at, (source, target) in enumerate(
            ((picked_from, picked), (gates_from, gates), (grad_from, grad), (saved_rows, edge))
        )
    ]
    for copy in copies:
        copy.start()
    home_rows = grad.shape[0]
    start = lax.axis_index("loop") * home_rows
    copies[0].wait()
    copies[1].wait()
    rows = []
    for turn in range(expert_count):
        expert = lax.rem(lax.axis_index("tensor") + turn, expert_count)
        listed, chosen = home_slots(picked[pl.ds(expert, 1), :], start, home_rows)
        gate = jnp.sum(jnp.where(listed, gates[pl.ds(expert, 1), :], 0.0), axis=1, keepdims=True)
        rows.append((gate, chosen))
    copies[2].wait()
    for (gate, chosen), out in zip(rows, outs):
        taken = jnp.dot(chosen, grad[...], preferred_element_type=jnp.float32)
        out[...] = (gate * taken).astype(jnp.bfloat16)[:MOST]
    copies[3].wait()


def finish_kernel(expert_count, grad, picked, *refs):
    landed, out, held = refs[:expert_count], refs[expert_count], refs[expert_count + 1]
    home_rows = grad.shape[0]
    start = lax.axis_index("loop") * home_rows
    total = grad[...].astype(jnp.float32)
    for turn in range(expert_count):
        expert = lax.rem(lax.axis_index("tensor") + turn, expert_count)
        _, chosen = home_slots(picked[pl.ds(expert, 1), :], start, home_rows)
        held[...] = jnp.zeros_like(held)
        held[:MOST, :] = landed[turn][...]
        total += lax.dot_general(
            chosen, held[...], (((0,), (0,)), ((), ())), preferred_element_type=jnp.float32
        )
    out[...] = total.astype(jnp.bfloat16)


def part_start(turn, split, splits, expert_count, group_size, features):
    loop_index = lax.axis_index("loop")
    mine = lax.rem(lax.rem(loop_index, group_size), splits) ^ split
    share = lax.rem(loop_index // group_size - turn + expert_count, expert_count)
    return pl.multiple_of((mine * expert_count + share) * features, 128)


def weight_copies(turn, sizes, axis, weight, out, arrived):
    _, splits, expert_count, group_size = sizes
    features = out.shape[1 + axis]
    parts = arrived.shape[1]
    step = out.shape[1] // parts
    copies = []
    for split in range(splits):
        start = part_start(turn, split, splits, expert_count, group_size, features)
        for at in range(parts):
            rows = pl.ds(at * step, step)
            if axis == 1:
                source = weight.at[rows, pl.ds(start, features)]
            else:
                source = weight.at[pl.ds(pl.multiple_of(start + at * step, 16), step), :]
            copies.append(pltpu.make_async_copy(source, out.at[split, rows], arrived.at[split, at]))
            copies[-1].start()
    return copies


def fetch_kernel(wanted, sizes, out_weight, in_weight, *refs):
    outs, arrived = refs[:-1], refs[-1]
    copies = []
    for at, (turn, axis) in enumerate(wanted):
        weight = out_weight if axis == 1 else in_weight
        copies += weight_copies(turn, sizes, axis, weight, outs[at], arrived.at[at])
    for copy in copies:
        copy.wait()


def slope_kernel(turns, sizes, home_rows, halo, in_weight, picked, *refs):
    blocks, splits, _, group_size = sizes
    refs, arrived = refs[:-1], refs[-1]
    refs, brought = refs[: len(refs) - len(turns)], refs[len(refs) - len(turns) :]
    parts, out = refs[:-1], refs[-1]
    copies = []
    for at, turn in enumerate(turns):
        copies += weight_copies(turn, sizes, 0, in_weight, brought[at], arrived.at[at])
    loop_index, tensor_index = lax.axis_index("loop"), lax.axis_index("tensor")
    picks = picked[pl.ds(loop_index // group_size, 1), :]
    place = lax.rem(loop_index, group_size) // splits
    per_tensor = parts[len(parts) // 2].shape[0]
    window = jnp.concatenate([part[...] for part in parts], axis=0)
    for at in range(blocks):
        block = tensor_index * blocks + (place ^ at)
        first = jnp.sum((picks < block * home_rows).astype(jnp.int32), axis=1, keepdims=True)
        wanted = first + lax.broadcasted_iota(jnp.int32, (MOST, window.shape[0]), 0)
        wanted = wanted - tensor_index * per_tensor + halo
        held = lax.broadcasted_iota(jnp.int32, (MOST, window.shape[0]), 1)
        hidden = jnp.dot(
            (held == wanted).astype(jnp.bfloat16), window, preferred_element_type=jnp.float32
        )
        out[at * MOST : (at + 1) * MOST, :] = gelu_slope(hidden)
    for copy in copies:
        copy.wait()


def join_kernel(*refs):
    for at, part in enumerate(refs[:-1]):
        refs[-1][at] = part[...]


def up_product(sizes, slope, weights, pieces, gathered, pre_grad):
    blocks, splits = sizes[:2]
    hidden = slope.shape[1]
    step = min(512, hidden)
    for turn in range(len(weights)):
        for split in range(splits):
            for at in range(blocks):
                rows = slice(at * MOST, (at + 1) * MOST)
                gathered[turn, split, rows, :] = pieces[at * splits + split][turn]
    for low in range(0, hidden, step):
        columns = slice(low, low + step)
        total = 0.0
        for turn, weight in enumerate(weights):
            for split in range(splits):
                total += rows_dot(gathered[turn, split], weight[split, columns])
        pre_grad[:, columns] = (total * slope[:, columns]).astype(jnp.bfloat16)


def down_product(sizes, pre_grad, weight, keep, give):
    blocks, splits = sizes[:2]
    features = weight.shape[1]
    step = min(512, features)
    for split in range(splits):
        for low in range(0, features, step):
            columns = slice(low, low + step)
            product = rows_dot(pre_grad[...], weight[split, columns]).astype(jnp.bfloat16)
            for at in range(blocks):
                index = at * splits + split
                target = give if index % 2 else keep
                target[index // 2, :, columns] = product[at * MOST : (at + 1) * MOST]


def both_kernel(sizes, *refs):
    expert_count = sizes[2]
    weights, down_weight, slope = refs[:expert_count], refs[expert_count], refs[expert_count + 1]
    pieces, (pre_grad, keep, give, gathered) = refs[expert_count + 2 : -4], refs[-4:]
    up_product(sizes, slope, weights, pieces, gathered, pre_grad)
    down_product(sizes, pre_grad, down_weight, keep, give)


def down_kernel(sizes, weight, pre_grad, keep, give):
    down_product(sizes, pre_grad, weight, keep, give)


def shards(grad_out, saved_hidden, picked_tokens, gate_values, in_weight, out_weight):
    home_rows, features = grad_out.shape
    width, hidden = in_weight.shape
    loop_size, tensor_size = lax.axis_size("loop"), lax.axis_size("tensor")
    expert_count, capacity = picked_tokens.shape
    blocks = loop_size // tensor_size
    group_size = loop_size // expert_count
    splits = group_size // blocks
    sizes = (blocks, splits, expert_count, group_size)
    row_count = blocks * MOST
    routes = home_routes(expert_count)
    bf16, f32 = jnp.bfloat16, jnp.float32

    order = list(range(expert_count))[::-1]
    back_order = order[::-1]
    per_tensor = capacity // tensor_size
    halo = max(
        (
            max(MOST * cut * blocks - cut * per_tensor, cut * per_tensor - capacity + MOST * (tensor_size - cut) * blocks)
            for cut in range(1, tensor_size)
        ),
        default=0,
    )
    halo = -(-halo // 16) * 16
    *outgoing, edge = kernel_call(
        prepare_kernel,
        [jax.ShapeDtypeStruct((MOST, features), bf16)] * expert_count
        + [jax.ShapeDtypeStruct((min(halo, per_tensor // 16 * 16), hidden), bf16)],
        (grad_out, picked_tokens, gate_values, saved_hidden),
        [
            pltpu.VMEM(grad_out.shape, bf16),
            pltpu.VMEM(picked_tokens.shape, jnp.int32),
            pltpu.VMEM(gate_values.shape, f32),
            pltpu.SemaphoreType.DMA((4,)),
        ],
        left=4,
    )
    arrived = {turn: lax.ppermute(outgoing[turn], BOTH, routes[turn]) for turn in order}

    parts = 4
    up_shape = pltpu.VMEM((splits, hidden, features), bf16)
    down_shape = pltpu.VMEM((splits, features, hidden), bf16)
    wanted = [(turn, 1) for turn in order] + [(back_order[0], 0)]
    sources = after_all((out_weight, in_weight), outgoing)
    fetched = kernel_call(
        functools.partial(fetch_kernel, wanted, sizes),
        [up_shape if axis == 1 else down_shape for _, axis in wanted],
        sources,
        [pltpu.SemaphoreType.DMA((len(wanted), splits, parts))],
        left=2,
    )
    arrived = after_all([arrived[turn] for turn in order], fetched)
    up_weight, down_weight = fetched[:-1], {back_order[0]: fetched[-1]}

    mine = kernel_call(join_kernel, jax.ShapeDtypeStruct((expert_count, MOST, features), bf16), arrived)
    cross = [swap(mine, 2 * m) for m in range(1, group_size // 2)]
    beside = swap(mine, 1)

    saved, edge, down_source = after_all((saved_hidden, edge, in_weight), [beside])
    before, after = [], []
    if tensor_size == 2 and halo <= per_tensor:
        before = after = [lax.ppermute(edge, "tensor", [(0, 1), (1, 0)])]
    else:
        for hop in range(1, -(-halo // per_tensor) + 1):
            part = min(per_tensor, halo - (hop - 1) * per_tensor)
            up = [(at, at + hop) for at in range(tensor_size - hop)]
            before.insert(0, lax.ppermute(saved[per_tensor - part :], "tensor", up))
            after.append(lax.ppermute(saved[:part], "tensor", [(b, a) for a, b in up]))
    slope, *fetched = kernel_call(
        functools.partial(slope_kernel, back_order[1:], sizes, home_rows, halo),
        [jax.ShapeDtypeStruct((row_count, hidden), f32)] + [down_shape] * (expert_count - 1),
        (down_source, picked_tokens, *before, saved, *after),
        [pltpu.SemaphoreType.DMA((max(1, expert_count - 1), splits, parts))],
        flops=2 * row_count * hidden * (per_tensor + 2 * halo),
        left=1,
    )
    down_weight.update(zip(back_order[1:], fetched))
    gathered = [mine, beside]
    gathered += [piece for got in after_all(cross, [slope]) for piece in (got, swap(got, 1))]

    half = 2 * row_count * hidden * features * splits
    halves = [jax.ShapeDtypeStruct((group_size // 2, MOST, features), bf16)] * 2
    made = {}
    pre_grad, *made[back_order[0]] = kernel_call(
        functools.partial(both_kernel, sizes),
        [jax.ShapeDtypeStruct((row_count, hidden), bf16)] + halves,
        (*up_weight, down_weight[back_order[0]], slope, *gathered),
        [pltpu.VMEM((expert_count, splits, row_count, features), bf16)],
        flops=(expert_count + 1) * half,
        vmem=6,
    )
    for turn in back_order[1:]:
        made[turn] = kernel_call(
            functools.partial(down_kernel, sizes),
            halves,
            (down_weight[turn], pre_grad),
            flops=half,
        )

    landed = []
    for turn in back_order:
        keep, give = made[turn]
        paired = keep.astype(f32) + swap(give, 1).astype(f32)
        summed = paired[0]
        for m in reversed(range(1, group_size // 2)):
            summed = summed + swap(paired[m].astype(bf16), 2 * m).astype(f32)
        back = [(target, source) for source, target in routes[turn]]
        landed.append(lax.ppermute(summed.astype(bf16), BOTH, back))

    return kernel_call(
        functools.partial(finish_kernel, expert_count),
        jax.ShapeDtypeStruct((home_rows, features), bf16),
        (grad_out, picked_tokens, *landed),
        [pltpu.VMEM((PADDED, features), bf16)],
    )


def solution(mesh):
    placed = (P("loop", "tensor"), P("tensor", "loop"), P(), P(), P(None, "loop"), P("loop", None))
    return jax.shard_map(
        shards, mesh=mesh, in_specs=placed, out_specs=P("loop", "tensor"), check_vma=False
    )
```

time: 281 us -> 74.2 us (0.26)
  the two profiles are of different devices: /device:TPU:11 before, /device:TPU:0 now
where the time goes in v2:
time: 74.2 us; the launch traced here: 74 us
  Pallas kernels  26.2 us (35%)
  waiting for transfers between devices  24.7 us (33%)
  starting transfers between devices  22.5 us (30%)
    pallas_call x7, Pallas kernels, kernel_call(): pl.pallas_call(body, out_shape=out_shape, in_specs=[LEFT] * left + [VMEM]...  26.2 us
    ppermute x15, starting transfers between devices, swap(): return lax.ppermute(values, 'loop', pairs)  13.5 us
    ppermute x2, waiting for transfers between devices, shards(): landed.append(lax.ppermute(summed.astype(bf16), BOTH, back))  11.2 us
    ppermute x15, waiting for transfers between devices, swap(): return lax.ppermute(values, 'loop', pairs)  9.72 us
    ppermute x2, starting transfers between devices, shards(): lax.ppermute(outgoing[turn], BOTH, routes[turn])  7.29 us
    ppermute x1, waiting for transfers between devices, shards(): before = after = [lax.ppermute(edge, 'tensor', [(0, 1), (1, 0)])]  3.81 us
  transfers between devices with their start and end apart: 20, of which 9 were waited for; matrix products, arithmetic and copies ran while one was open for 1% of the time, Pallas kernels for 21%

profile of v2, /device:TPU:0, one launch (start us, length us, event | category | flops | bytes accessed | tf_op | source)
XLA Modules:
  0.0 74.0 jit_solution(3270834760465739013)
XLA Ops:
  0.0 1.4 %shard_map.64 = (bf16[28,2048]{1,0:T(8,128)(2,1)S(1)}, bf16[28,2048]{1,0:T(8,128)(2,1)S(1)}, bf16[16,2048]{1,0:T(8,128)(2,1)S(1)}) custom-call(bf16[128,2048]{1,0:T(8,128)(2,1)} %grad.1, s32[2,416]{1,0:T(2,128)} %picked.3, f32[2,416]{1,0:T(2,128)} %gates_from.1, bf16[208,2048]{1,0:T(8,128)(2,1)} %refs_1_), custom_call_target="tpu_custom_call" | custom-call | bytes 1382912 | tf_op jit(solution)/shard_map/pallas_call | solution.py:38
  1.4 0.7 collective-permute-start.1
  2.1 0.0 copy-start
  2.1 0.0 copy-start.2
  2.1 6.6 %collective-permute-start = (bf16[28,2048]{1,0:T(8,128)(2,1)S(1)}, bf16[28,2048]{1,0:T(8,128)(2,1)S(1)}, u32[]{:S(2)}, u32[]{:S(2)}) collective-permute-start(bf16[28,2048]{1,0:T(8,128)(2,1)S(1)} %get-tuple-element.29), channel_id=1, source_target_pairs={{0,16},{1,0},{2,18},{3,2},{4,20},{5,4},{6,22},{7,6},{8,24},{9,8},{... | collective-permute-start | bytes 344072 | tf_op jit(solution)/shard_map/ppermute | solution.py:283
  8.7 8.3 %shard_map.65 = (bf16[1,2048,2048]{2,1,0:T(8,128)(2,1)S(1)}, bf16[1,2048,2048]{2,1,0:T(8,128)(2,1)S(1)}, bf16[1,2048,2048]{2,1,0:T(8,128)(2,1)S(1)}) custom-call(bf16[2048,4096]{1,0:T(8,128)(2,1)} %out_weight, bf16[4096,2048]{1,0:T(8,128)(2,1)} %in_weight.1), custom_call_target="tpu_custom_call" | custom-call | bytes 33554432 | tf_op jit(solution)/shard_map/pallas_call | solution.py:38
  17.1 0.0 collective-permute-done.1.refs_1_
  17.1 0.0 collective-permute-done.refs_0_
  17.1 0.1 collective-permute-start.2
  17.2 2.6 %collective-permute-start.6 = (bf16[2,28,2048]{2,1,0:T(8,128)(2,1)S(1)}, bf16[2,28,2048]{2,1,0:T(8,128)(2,1)S(1)}, u32[]{:S(2)}, u32[]{:S(2)}) collective-permute-start(bf16[2,28,2048]{2,1,0:T(8,128)(2,1)S(1)} %shard_map.66.refs_4_), channel_id=1, source_target_pairs={{0,12},{2,14},{4,8},{6,10},{8,4},{10,6},{12,0},{14,2},{16,28},{18,... | collective-permute-start | bytes 688136 | tf_op jit(solution)/shard_map/ppermute | solution.py:56
  19.8 0.4 collective-permute-start.5
  20.2 0.5 collective-permute-start.4
  20.8 0.0 collective-permute-done.2.refs_5_
  20.8 0.5 collective-permute-start.3
  21.2 3.8 %collective-permute-done.3.refs_0_.refs_2_ = bf16[16,2048]{1,0:T(8,128)(2,1)S(1)} collective-permute-done((bf16[16,2048]{1,0:T(8,128)(2,1)S(1)}, bf16[16,2048]{1,0:T(8,128)(2,1)S(1)}, u32[]{:S(2)}, u32[]{:S(2)}) %collective-permute-start.3) | collective-permute-done | bytes 65568 | tf_op jit(solution)/shard_map/ppermute | solution.py:307
  25.0 0.0 copy-done
  25.0 0.0 copy-done.2
  25.0 4.8 %shard_map.67 = (f32[224,2048]{1,0:T(8,128)S(1)}, bf16[1,2048,2048]{2,1,0:T(8,128)(2,1)S(1)}) custom-call(bf16[4096,2048]{1,0:T(8,128)(2,1)} %in_weight.1, s32[2,416]{1,0:T(2,128)S(1)} %copy-done.2, bf16[16,2048]{1,0:T(8,128)(2,1)S(1)} %collective-permute-done.3.refs_0_.refs_2_, bf16[208,2048]{1,0:T(8,128)(2,1)S(1)} %copy-done, ...), custom_call_target="tpu_custom_call" | custom-call | flops 220200960 | bytes 17763584 | tf_op jit(solution)/shard_map/pallas_call | solution.py:38
  29.8 0.0 collective-permute-done.6.refs_10_
  29.8 2.7 %collective-permute-done.5.refs_8_ = bf16[2,28,2048]{2,1,0:T(8,128)(2,1)S(1)} collective-permute-done((bf16[2,28,2048]{2,1,0:T(8,128)(2,1)S(1)}, bf16[2,28,2048]{2,1,0:T(8,128)(2,1)S(1)}, u32[]{:S(2)}, u32[]{:S(2)}) %collective-permute-start.5) | collective-permute-done | bytes 229408 | tf_op jit(solution)/shard_map/ppermute | solution.py:56
  32.5 0.0 collective-permute-done.4.refs_6_
  32.5 0.0 collective-permute-start.7
  32.5 0.5 collective-permute-start.8
  33.0 0.0 collective-permute-start.9
  33.0 1.0 %collective-permute-done.7.refs_7_ = bf16[2,28,2048]{2,1,0:T(8,128)(2,1)S(1)} collective-permute-done((bf16[2,28,2048]{2,1,0:T(8,128)(2,1)S(1)}, bf16[2,28,2048]{2,1,0:T(8,128)(2,1)S(1)}, u32[]{:S(2)}, u32[]{:S(2)}) %collective-permute-start.7) | collective-permute-done | bytes 229408 | tf_op jit(solution)/shard_map/ppermute | solution.py:56
  34.1 0.4 collective-permute-done.8.refs_9_
  34.4 0.4 collective-permute-done.9.refs_11_
  34.8 7.6 %shard_map.68 = (bf16[224,2048]{1,0:T(8,128)(2,1)S(1)}, bf16[4,28,2048]{2,1,0:T(8,128)(2,1)S(1)}, bf16[4,28,2048]{2,1,0:T(8,128)(2,1)S(1)}) custom-call(bf16[1,2048,2048]{2,1,0:T(8,128)(2,1)S(1)} %get-tuple-element.32.refs_0_, bf16[1,2048,2048]{2,1,0:T(8,128)(2,1)S(1)} %get-tuple-element.33.refs_1_, bf16[1,2048,2048]{2,1,0:T(8,128)(2,1)S(1)} %get-tuple-element.34.refs_2_, ...), custom_call_target="tpu_custom_call" | custom-call | flops 5637144576 | bytes 28835840 | tf_op jit(solution)/shard_map/pallas_call | solution.py:38
  42.4 0.2 collective-permute-start.10
  42.6 0.0 copy-start.1
  42.6 2.6 %shard_map.69 = (bf16[4,28,2048]{2,1,0:T(8,128)(2,1)S(1)}, bf16[4,28,2048]{2,1,0:T(8,128)(2,1)S(1)}) custom-call(bf16[1,2048,2048]{2,1,0:T(8,128)(2,1)S(1)} %get-tuple-element.47.weight, bf16[224,2048]{1,0:T(8,128)(2,1)S(1)} %get-tuple-element.48.pre_grad), custom_call_target="tpu_custom_call" | custom-call | flops 1879048192 | bytes 9306112 | tf_op jit(solution)/shard_map/pallas_call | solution.py:38
  45.2 0.5 collective-permute-start.15
  45.7 0.0 collective-permute-done.10
  45.7 0.1 fusion.8
  45.9 2.5 %collective-permute-start.11 = (bf16[28,2048]{1,0:T(8,128)(2,1)S(1)}, bf16[28,2048]{1,0:T(8,128)(2,1)S(1)}, u32[]{:S(2)}, u32[]{:S(2)}) collective-permute-start(bf16[28,2048]{1,0:T(8,128)(2,1)S(1)} %get-tuple-element.58), channel_id=1, source_target_pairs={{0,12},{2,14},{4,8},{6,10},{8,4},{10,6},{12,0},{14,2},{16,28},{18,... | collective-permute-start | bytes 344072 | tf_op jit(solution)/shard_map/ppermute | solution.py:56
  48.3 0.6 collective-permute-start.13
  49.0 0.4 collective-permute-start.12
  49.4 0.0 collective-permute-done.15
  49.4 0.1 fusion.9
  49.6 2.5 %collective-permute-start.16 = (bf16[28,2048]{1,0:T(8,128)(2,1)S(1)}, bf16[28,2048]{1,0:T(8,128)(2,1)S(1)}, u32[]{:S(2)}, u32[]{:S(2)}) collective-permute-start(bf16[28,2048]{1,0:T(8,128)(2,1)S(1)} %get-tuple-element.55), channel_id=1, source_target_pairs={{0,12},{2,14},{4,8},{6,10},{8,4},{10,6},{12,0},{14,2},{16,28},{18,... | collective-permute-start | bytes 344072 | tf_op jit(solution)/shard_map/ppermute | solution.py:56
  52.1 0.6 collective-permute-start.18
  52.7 0.0 collective-permute-done.11
  52.7 2.1 %collective-permute-start.17 = (bf16[28,2048]{1,0:T(8,128)(2,1)S(1)}, bf16[28,2048]{1,0:T(8,128)(2,1)S(1)}, u32[]{:S(2)}, u32[]{:S(2)}) collective-permute-start(bf16[28,2048]{1,0:T(8,128)(2,1)S(1)} %get-tuple-element.57), channel_id=1, source_target_pairs={{0,8},{2,10},{4,12},{6,14},{8,0},{10,2},{12,4},{14,6},{16,24},{18,... | collective-permute-start | bytes 344072 | tf_op jit(solution)/shard_map/ppermute | solution.py:56
  54.8 1.6 %collective-permute-done.13 = bf16[28,2048]{1,0:T(8,128)(2,1)S(1)} collective-permute-done((bf16[28,2048]{1,0:T(8,128)(2,1)S(1)}, bf16[28,2048]{1,0:T(8,128)(2,1)S(1)}, u32[]{:S(2)}, u32[]{:S(2)}) %collective-permute-start.13) | collective-permute-done | bytes 114720 | tf_op jit(solution)/shard_map/ppermute | solution.py:56
  56.3 0.0 collective-permute-done.12
  56.3 0.1 fusion.7
  56.4 0.7 collective-permute-start.14
  57.1 1.9 %collective-permute-done.16 = bf16[28,2048]{1,0:T(8,128)(2,1)S(1)} collective-permute-done((bf16[28,2048]{1,0:T(8,128)(2,1)S(1)}, bf16[28,2048]{1,0:T(8,128)(2,1)S(1)}, u32[]{:S(2)}, u32[]{:S(2)}) %collective-permute-start.16) | collective-permute-done | bytes 114720 | tf_op jit(solution)/shard_map/ppermute | solution.py:56
  59.0 1.7 %collective-permute-done.18 = bf16[28,2048]{1,0:T(8,128)(2,1)S(1)} collective-permute-done((bf16[28,2048]{1,0:T(8,128)(2,1)S(1)}, bf16[28,2048]{1,0:T(8,128)(2,1)S(1)}, u32[]{:S(2)}, u32[]{:S(2)}) %collective-permute-start.18) | collective-permute-done | bytes 114720 | tf_op jit(solution)/shard_map/ppermute | solution.py:56
  60.8 0.0 collective-permute-done.17
  60.8 0.1 fusion.3
  60.9 0.5 collective-permute-start.19
  61.4 0.0 collective-permute-done.14.refs_0_
  61.4 11.2 %collective-permute-done.19.refs_1_ = bf16[28,2048]{1,0:T(8,128)(2,1)S(1)} collective-permute-done((bf16[28,2048]{1,0:T(8,128)(2,1)S(1)}, bf16[28,2048]{1,0:T(8,128)(2,1)S(1)}, u32[]{:S(2)}, u32[]{:S(2)}) %collective-permute-start.19) | collective-permute-done | bytes 114720 | tf_op jit(solution)/shard_map/ppermute | solution.py:353
  72.5 0.0 copy-done.1
  72.5 1.4 %shard_map.70 = bf16[128,2048]{1,0:T(8,128)(2,1)} custom-call(bf16[128,2048]{1,0:T(8,128)(2,1)S(1)} %copy-done.1, s32[2,416]{1,0:T(2,128)S(1)} %copy-done.2, bf16[28,2048]{1,0:T(8,128)(2,1)S(1)} %collective-permute-done.14.refs_0_, bf16[28,2048]{1,0:T(8,128)(2,1)S(1)} %collective-permute-done.19.refs_1_), custom_call_target="tpu_custom_call" | custom-call | bytes 756992 | tf_op jit(solution)/shard_map/pallas_call | solution.py:38
  (3 shorter events, 0.1 us)
Async XLA Ops:
  1.4 15.7 %collective-permute-start.1 = (bf16[28,2048]{1,0:T(8,128)(2,1)S(1)}, bf16[28,2048]{1,0:T(8,128)(2,1)S(1)}, u32[]{:S(2)}, u32[]{:S(2)}) collective-permute-start(bf16[28,2048]{1,0:T(8,128)(2,1)S(1)} %get-tuple-element.28), channel_id=1, source_target_pairs={{0,0},{1,16},{2,2},{3,18},{4,4},{5,20},{6,6},{7,22},{8,8},{9,24},{... | collective-permute-start | bytes 344072 | tf_op jit(solution)/shard_map/ppermute | solution.py:283
  2.1 23.0 %copy-start = (bf16[208,2048]{1,0:T(8,128)(2,1)S(1)}, bf16[208,2048]{1,0:T(8,128)(2,1)}, u32[]{:S(2)}) copy-start(bf16[208,2048]{1,0:T(8,128)(2,1)} %refs_1_) | copy-start | bytes 2555908
  2.1 22.9 %copy-start.2 = (s32[2,416]{1,0:T(2,128)S(1)}, s32[2,416]{1,0:T(2,128)}, u32[]{:S(2)}) copy-start(s32[2,416]{1,0:T(2,128)} %picked.3) | copy-start | bytes 9988
  2.1 15.0 %collective-permute-start = (bf16[28,2048]{1,0:T(8,128)(2,1)S(1)}, bf16[28,2048]{1,0:T(8,128)(2,1)S(1)}, u32[]{:S(2)}, u32[]{:S(2)}) collective-permute-start(bf16[28,2048]{1,0:T(8,128)(2,1)S(1)} %get-tuple-element.29), channel_id=1, source_target_pairs={{0,16},{1,0},{2,18},{3,2},{4,20},{5,4},{6,22},{7,6},{8,24},{9,8},{... | collective-permute-start | bytes 344072 | tf_op jit(solution)/shard_map/ppermute | solution.py:283
  17.1 3.6 %collective-permute-start.2 = (bf16[2,28,2048]{2,1,0:T(8,128)(2,1)S(1)}, bf16[2,28,2048]{2,1,0:T(8,128)(2,1)S(1)}, u32[]{:S(2)}, u32[]{:S(2)}) collective-permute-start(bf16[2,28,2048]{2,1,0:T(8,128)(2,1)S(1)} %shard_map.66.refs_4_), channel_id=1, source_target_pairs={{0,2},{2,0},{4,6},{6,4},{8,10},{10,8},{12,14},{14,12},{16,18},{18,... | collective-permute-start | bytes 688136 | tf_op jit(solution)/shard_map/ppermute | solution.py:56
  17.2 12.6 %collective-permute-start.6 = (bf16[2,28,2048]{2,1,0:T(8,128)(2,1)S(1)}, bf16[2,28,2048]{2,1,0:T(8,128)(2,1)S(1)}, u32[]{:S(2)}, u32[]{:S(2)}) collective-permute-start(bf16[2,28,2048]{2,1,0:T(8,128)(2,1)S(1)} %shard_map.66.refs_4_), channel_id=1, source_target_pairs={{0,12},{2,14},{4,8},{6,10},{8,4},{10,6},{12,0},{14,2},{16,28},{18,... | collective-permute-start | bytes 688136 | tf_op jit(solution)/shard_map/ppermute | solution.py:56
  19.8 12.7 %collective-permute-start.5 = (bf16[2,28,2048]{2,1,0:T(8,128)(2,1)S(1)}, bf16[2,28,2048]{2,1,0:T(8,128)(2,1)S(1)}, u32[]{:S(2)}, u32[]{:S(2)}) collective-permute-start(bf16[2,28,2048]{2,1,0:T(8,128)(2,1)S(1)} %shard_map.66.refs_4_), channel_id=1, source_target_pairs={{0,8},{2,10},{4,12},{6,14},{8,0},{10,2},{12,4},{14,6},{16,24},{18,... | collective-permute-start | bytes 688136 | tf_op jit(solution)/shard_map/ppermute | solution.py:56
  20.2 12.3 %collective-permute-start.4 = (bf16[2,28,2048]{2,1,0:T(8,128)(2,1)S(1)}, bf16[2,28,2048]{2,1,0:T(8,128)(2,1)S(1)}, u32[]{:S(2)}, u32[]{:S(2)}) collective-permute-start(bf16[2,28,2048]{2,1,0:T(8,128)(2,1)S(1)} %shard_map.66.refs_4_), channel_id=1, source_target_pairs={{0,4},{2,6},{4,0},{6,2},{8,12},{10,14},{12,8},{14,10},{16,20},{18,... | collective-permute-start | bytes 688136 | tf_op jit(solution)/shard_map/ppermute | solution.py:56
  20.8 4.3 %collective-permute-start.3 = (bf16[16,2048]{1,0:T(8,128)(2,1)S(1)}, bf16[16,2048]{1,0:T(8,128)(2,1)S(1)}, u32[]{:S(2)}, u32[]{:S(2)}) collective-permute-start(bf16[16,2048]{1,0:T(8,128)(2,1)S(1)} %get-tuple-element.39), channel_id=1, source_target_pairs={{0,1},{1,0},{2,3},{3,2},{4,5},{5,4},{6,7},{7,6},{8,9},{9,8},{10,11... | collective-permute-start | bytes 196616 | tf_op jit(solution)/shard_map/ppermute | solution.py:307
  32.5 1.5 %collective-permute-start.7 = (bf16[2,28,2048]{2,1,0:T(8,128)(2,1)S(1)}, bf16[2,28,2048]{2,1,0:T(8,128)(2,1)S(1)}, u32[]{:S(2)}, u32[]{:S(2)}) collective-permute-start(bf16[2,28,2048]{2,1,0:T(8,128)(2,1)S(1)} %collective-permute-done.4.refs_6_), channel_id=1, source_target_pairs={{0,2},{2,0},{4,6},{6,4},{8,10},{10,8},{12,14},{14,12},{16,18},{18,... | collective-permute-start | bytes 688136 | tf_op jit(solution)/shard_map/ppermute | solution.py:56
  32.5 1.9 %collective-permute-start.8 = (bf16[2,28,2048]{2,1,0:T(8,128)(2,1)S(1)}, bf16[2,28,2048]{2,1,0:T(8,128)(2,1)S(1)}, u32[]{:S(2)}, u32[]{:S(2)}) collective-permute-start(bf16[2,28,2048]{2,1,0:T(8,128)(2,1)S(1)} %collective-permute-done.5.refs_8_), channel_id=1, source_target_pairs={{0,2},{2,0},{4,6},{6,4},{8,10},{10,8},{12,14},{14,12},{16,18},{18,... | collective-permute-start | bytes 688136 | tf_op jit(solution)/shard_map/ppermute | solution.py:56
  33.0 1.8 %collective-permute-start.9 = (bf16[2,28,2048]{2,1,0:T(8,128)(2,1)S(1)}, bf16[2,28,2048]{2,1,0:T(8,128)(2,1)S(1)}, u32[]{:S(2)}, u32[]{:S(2)}) collective-permute-start(bf16[2,28,2048]{2,1,0:T(8,128)(2,1)S(1)} %collective-permute-done.6.refs_10_), channel_id=1, source_target_pairs={{0,2},{2,0},{4,6},{6,4},{8,10},{10,8},{12,14},{14,12},{16,18},{18,... | collective-permute-start | bytes 688136 | tf_op jit(solution)/shard_map/ppermute | solution.py:56
  42.4 3.2 %collective-permute-start.10 = (bf16[4,28,2048]{2,1,0:T(8,128)(2,1)S(1)}, bf16[4,28,2048]{2,1,0:T(8,128)(2,1)S(1)}, u32[]{:S(2)}, u32[]{:S(2)}) collective-permute-start(bf16[4,28,2048]{2,1,0:T(8,128)(2,1)S(1)} %get-tuple-element.46), channel_id=1, source_target_pairs={{0,2},{2,0},{4,6},{6,4},{8,10},{10,8},{12,14},{14,12},{16,18},{18,... | collective-permute-start | bytes 1376264 | tf_op jit(solution)/shard_map/ppermute | solution.py:56
  42.6 29.9 %copy-start.1 = (bf16[128,2048]{1,0:T(8,128)(2,1)S(1)}, bf16[128,2048]{1,0:T(8,128)(2,1)}, u32[]{:S(2)}) copy-start(bf16[128,2048]{1,0:T(8,128)(2,1)} %grad.1) | copy-start | bytes 1572868
  45.2 4.2 %collective-permute-start.15 = (bf16[4,28,2048]{2,1,0:T(8,128)(2,1)S(1)}, bf16[4,28,2048]{2,1,0:T(8,128)(2,1)S(1)}, u32[]{:S(2)}, u32[]{:S(2)}) collective-permute-start(bf16[4,28,2048]{2,1,0:T(8,128)(2,1)S(1)} %get-tuple-element.50), channel_id=1, source_target_pairs={{0,2},{2,0},{4,6},{6,4},{8,10},{10,8},{12,14},{14,12},{16,18},{18,... | collective-permute-start | bytes 1376264 | tf_op jit(solution)/shard_map/ppermute | solution.py:56
  45.9 6.9 %collective-permute-start.11 = (bf16[28,2048]{1,0:T(8,128)(2,1)S(1)}, bf16[28,2048]{1,0:T(8,128)(2,1)S(1)}, u32[]{:S(2)}, u32[]{:S(2)}) collective-permute-start(bf16[28,2048]{1,0:T(8,128)(2,1)S(1)} %get-tuple-element.58), channel_id=1, source_target_pairs={{0,12},{2,14},{4,8},{6,10},{8,4},{10,6},{12,0},{14,2},{16,28},{18,... | collective-permute-start | bytes 344072 | tf_op jit(solution)/shard_map/ppermute | solution.py:56
  48.3 8.0 %collective-permute-start.13 = (bf16[28,2048]{1,0:T(8,128)(2,1)S(1)}, bf16[28,2048]{1,0:T(8,128)(2,1)S(1)}, u32[]{:S(2)}, u32[]{:S(2)}) collective-permute-start(bf16[28,2048]{1,0:T(8,128)(2,1)S(1)} %get-tuple-element.59), channel_id=1, source_target_pairs={{0,4},{2,6},{4,0},{6,2},{8,12},{10,14},{12,8},{14,10},{16,20},{18,... | collective-permute-start | bytes 344072 | tf_op jit(solution)/shard_map/ppermute | solution.py:56
  49.0 7.4 %collective-permute-start.12 = (bf16[28,2048]{1,0:T(8,128)(2,1)S(1)}, bf16[28,2048]{1,0:T(8,128)(2,1)S(1)}, u32[]{:S(2)}, u32[]{:S(2)}) collective-permute-start(bf16[28,2048]{1,0:T(8,128)(2,1)S(1)} %get-tuple-element.60), channel_id=1, source_target_pairs={{0,8},{2,10},{4,12},{6,14},{8,0},{10,2},{12,4},{14,6},{16,24},{18,... | collective-permute-start | bytes 344072 | tf_op jit(solution)/shard_map/ppermute | solution.py:56
  49.6 9.4 %collective-permute-start.16 = (bf16[28,2048]{1,0:T(8,128)(2,1)S(1)}, bf16[28,2048]{1,0:T(8,128)(2,1)S(1)}, u32[]{:S(2)}, u32[]{:S(2)}) collective-permute-start(bf16[28,2048]{1,0:T(8,128)(2,1)S(1)} %get-tuple-element.55), channel_id=1, source_target_pairs={{0,12},{2,14},{4,8},{6,10},{8,4},{10,6},{12,0},{14,2},{16,28},{18,... | collective-permute-start | bytes 344072 | tf_op jit(solution)/shard_map/ppermute | solution.py:56
  52.1 8.7 %collective-permute-start.18 = (bf16[28,2048]{1,0:T(8,128)(2,1)S(1)}, bf16[28,2048]{1,0:T(8,128)(2,1)S(1)}, u32[]{:S(2)}, u32[]{:S(2)}) collective-permute-start(bf16[28,2048]{1,0:T(8,128)(2,1)S(1)} %get-tuple-element.56), channel_id=1, source_target_pairs={{0,4},{2,6},{4,0},{6,2},{8,12},{10,14},{12,8},{14,10},{16,20},{18,... | collective-permute-start | bytes 344072 | tf_op jit(solution)/shard_map/ppermute | solution.py:56
  52.7 8.1 %collective-permute-start.17 = (bf16[28,2048]{1,0:T(8,128)(2,1)S(1)}, bf16[28,2048]{1,0:T(8,128)(2,1)S(1)}, u32[]{:S(2)}, u32[]{:S(2)}) collective-permute-start(bf16[28,2048]{1,0:T(8,128)(2,1)S(1)} %get-tuple-element.57), channel_id=1, source_target_pairs={{0,8},{2,10},{4,12},{6,14},{8,0},{10,2},{12,4},{14,6},{16,24},{18,... | collective-permute-start | bytes 344072 | tf_op jit(solution)/shard_map/ppermute | solution.py:56
  56.4 5.0 %collective-permute-start.14 = (bf16[28,2048]{1,0:T(8,128)(2,1)S(1)}, bf16[28,2048]{1,0:T(8,128)(2,1)S(1)}, u32[]{:S(2)}, u32[]{:S(2)}) collective-permute-start(bf16[28,2048]{1,0:T(8,128)(2,1)S(1)} %fusion.7), channel_id=1, source_target_pairs={{0,0},{16,1},{2,2},{18,3},{4,4},{20,5},{6,6},{22,7},{8,8},{24,9},{... | collective-permute-start | bytes 344072 | tf_op jit(solution)/shard_map/ppermute | solution.py:353
  60.9 11.7 %collective-permute-start.19 = (bf16[28,2048]{1,0:T(8,128)(2,1)S(1)}, bf16[28,2048]{1,0:T(8,128)(2,1)S(1)}, u32[]{:S(2)}, u32[]{:S(2)}) collective-permute-start(bf16[28,2048]{1,0:T(8,128)(2,1)S(1)} %fusion.3), channel_id=1, source_target_pairs={{16,0},{0,1},{18,2},{2,3},{20,4},{4,5},{22,6},{6,7},{24,8},{8,9},{... | collective-permute-start | bytes 344072 | tf_op jit(solution)/shard_map/ppermute | solution.py:353

commit v3 on v2

--- a/solution.py
+++ b/solution.py
@@ -61,6 +61,7 @@
     blocks = loop_size // tensor_size
     group_size = loop_size // expert_count
     splits = group_size // blocks
+    mirror = blocks // 2 if splits == 1 else 0
     routes = []
     for turn in range(expert_count):
         pairs = []
@@ -68,6 +69,7 @@
             for tensor_at in range(tensor_size):
                 expert = (tensor_at + turn) % expert_count
                 place = (loop_at % blocks) * splits + tensor_at // expert_count
+                place ^= mirror if expert != loop_at // blocks else 0
                 target = (expert * group_size + place) * tensor_size + loop_at // blocks
                 pairs.append((loop_at * tensor_size + tensor_at, target))
         routes.append(pairs)
@@ -115,13 +117,19 @@
     copies[3].wait()
 
 
-def finish_kernel(expert_count, grad, picked, *refs):
-    landed, out, held = refs[:expert_count], refs[expert_count], refs[expert_count + 1]
+def finish_kernel(blocks, grad, picked, *refs):
+    landed, out, held = refs[:-2], refs[-2], refs[-1]
+    expert_count = len(landed)
     home_rows = grad.shape[0]
     start = lax.axis_index("loop") * home_rows
+    direct = lax.axis_size("tensor") != expert_count
+    half = lax.axis_index("loop") // blocks
     total = grad[...].astype(jnp.float32)
     for turn in range(expert_count):
-        expert = lax.rem(lax.axis_index("tensor") + turn, expert_count)
+        if direct:
+            expert = lax.rem(lax.axis_index("tensor") + turn, expert_count)
+        else:
+            expert = lax.rem(half - turn + expert_count, expert_count)
         _, chosen = home_slots(picked[pl.ds(expert, 1), :], start, home_rows)
         held[...] = jnp.zeros_like(held)
         held[:MOST, :] = landed[turn][...]
@@ -131,10 +139,13 @@
     out[...] = total.astype(jnp.bfloat16)
 
 
-def part_start(turn, split, splits, expert_count, group_size, features):
+def part_start(turn, axis, split, splits, expert_count, group_size, features):
     loop_index = lax.axis_index("loop")
     mine = lax.rem(lax.rem(loop_index, group_size), splits) ^ split
-    share = lax.rem(loop_index // group_size - turn + expert_count, expert_count)
+    if axis == 0 and splits == 1:
+        share = lax.rem(lax.axis_index("tensor") + turn, expert_count)
+    else:
+        share = lax.rem(loop_index // group_size - turn + expert_count, expert_count)
     return pl.multiple_of((mine * expert_count + share) * features, 128)
 
 
@@ -145,7 +156,7 @@
     step = out.shape[1] // parts
     copies = []
     for split in range(splits):
-        start = part_start(turn, split, splits, expert_count, group_size, features)
+        start = part_start(turn, axis, split, splits, expert_count, group_size, features)
         for at in range(parts):
             rows = pl.ds(at * step, step)
             if axis == 1:
@@ -157,27 +168,23 @@
     return copies
 
 
-def fetch_kernel(wanted, sizes, out_weight, in_weight, *refs):
+def fetch_kernel(turns, axis, sizes, weight, *refs):
     outs, arrived = refs[:-1], refs[-1]
     copies = []
-    for at, (turn, axis) in enumerate(wanted):
-        weight = out_weight if axis == 1 else in_weight
+    for at, turn in enumerate(turns):
         copies += weight_copies(turn, sizes, axis, weight, outs[at], arrived.at[at])
     for copy in copies:
         copy.wait()
 
 
-def slope_kernel(turns, sizes, home_rows, halo, in_weight, picked, *refs):
+def slope_kernel(sizes, home_rows, halo, picked, *refs):
     blocks, splits, _, group_size = sizes
-    refs, arrived = refs[:-1], refs[-1]
-    refs, brought = refs[: len(refs) - len(turns)], refs[len(refs) - len(turns) :]
     parts, out = refs[:-1], refs[-1]
-    copies = []
-    for at, turn in enumerate(turns):
-        copies += weight_copies(turn, sizes, 0, in_weight, brought[at], arrived.at[at])
     loop_index, tensor_index = lax.axis_index("loop"), lax.axis_index("tensor")
     picks = picked[pl.ds(loop_index // group_size, 1), :]
     place = lax.rem(loop_index, group_size) // splits
+    if splits == 1:
+        place = jnp.where(loop_index // group_size != tensor_index, place ^ (blocks // 2), place)
     per_tensor = parts[len(parts) // 2].shape[0]
     window = jnp.concatenate([part[...] for part in parts], axis=0)
     for at in range(blocks):
@@ -190,8 +197,6 @@
             (held == wanted).astype(jnp.bfloat16), window, preferred_element_type=jnp.float32
         )
         out[at * MOST : (at + 1) * MOST, :] = gelu_slope(hidden)
-    for copy in copies:
-        copy.wait()
 
 
 def join_kernel(*refs):
@@ -257,7 +262,7 @@
     bf16, f32 = jnp.bfloat16, jnp.float32
 
     order = list(range(expert_count))[::-1]
-    back_order = order[::-1]
+    back_order = order if splits == 1 else order[::-1]
     per_tensor = capacity // tensor_size
     halo = max(
         (
@@ -282,20 +287,18 @@
     )
     arrived = {turn: lax.ppermute(outgoing[turn], BOTH, routes[turn]) for turn in order}
 
-    parts = 4
-    up_shape = pltpu.VMEM((splits, hidden, features), bf16)
-    down_shape = pltpu.VMEM((splits, features, hidden), bf16)
-    wanted = [(turn, 1) for turn in order] + [(back_order[0], 0)]
-    sources = after_all((out_weight, in_weight), outgoing)
-    fetched = kernel_call(
-        functools.partial(fetch_kernel, wanted, sizes),
-        [up_shape if axis == 1 else down_shape for _, axis in wanted],
-        sources,
-        [pltpu.SemaphoreType.DMA((len(wanted), splits, parts))],
-        left=2,
-    )
-    arrived = after_all([arrived[turn] for turn in order], fetched)
-    up_weight, down_weight = fetched[:-1], {back_order[0]: fetched[-1]}
+    def fetched(turns, axis, weight):
+        shape = (splits, hidden, features) if axis == 1 else (splits, features, hidden)
+        return kernel_call(
+            functools.partial(fetch_kernel, turns, axis, sizes),
+            [pltpu.VMEM(shape, bf16)] * expert_count,
+            (weight,),
+            [pltpu.SemaphoreType.DMA((expert_count, splits, 4))],
+            left=1,
+        )
+
+    up_weight = fetched(order, 1, *after_all((out_weight,), outgoing))
+    arrived = after_all([arrived[turn] for turn in order], up_weight)
 
     mine = kernel_call(join_kernel, jax.ShapeDtypeStruct((expert_count, MOST, features), bf16), arrived)
     cross = [swap(mine, 2 * m) for m in range(1, group_size // 2)]
@@ -311,17 +314,17 @@
             up = [(at, at + hop) for at in range(tensor_size - hop)]
             before.insert(0, lax.ppermute(saved[per_tensor - part :], "tensor", up))
             after.append(lax.ppermute(saved[:part], "tensor", [(b, a) for a, b in up]))
-    slope, *fetched = kernel_call(
-        functools.partial(slope_kernel, back_order[1:], sizes, home_rows, halo),
-        [jax.ShapeDtypeStruct((row_count, hidden), f32)] + [down_shape] * (expert_count - 1),
-        (down_source, picked_tokens, *before, saved, *after),
-        [pltpu.SemaphoreType.DMA((max(1, expert_count - 1), splits, parts))],
+    slope = kernel_call(
+        functools.partial(slope_kernel, sizes, home_rows, halo),
+        jax.ShapeDtypeStruct((row_count, hidden), f32),
+        (picked_tokens, *before, saved, *after),
         flops=2 * row_count * hidden * (per_tensor + 2 * halo),
-        left=1,
-    )
-    down_weight.update(zip(back_order[1:], fetched))
+    )
+    down_weight = fetched(back_order, 0, down_source)
+    cross = after_all(cross, [slope, *down_weight])
+    down_weight = dict(zip(back_order, down_weight))
     gathered = [mine, beside]
-    gathered += [piece for got in after_all(cross, [slope]) for piece in (got, swap(got, 1))]
+    gathered += [piece for got in cross for piece in (got, swap(got, 1))]
 
     half = 2 * row_count * hidden * features * splits
     halves = [jax.ShapeDtypeStruct((group_size // 2, MOST, features), bf16)] * 2
@@ -342,18 +345,39 @@
             flops=half,
         )
 
-    landed = []
+    totals = {}
     for turn in back_order:
         keep, give = made[turn]
         paired = keep.astype(f32) + swap(give, 1).astype(f32)
         summed = paired[0]
-        for m in reversed(range(1, group_size // 2)):
+        for m in range(1, group_size // 2):
             summed = summed + swap(paired[m].astype(bf16), 2 * m).astype(f32)
-        back = [(target, source) for source, target in routes[turn]]
-        landed.append(lax.ppermute(summed.astype(bf16), BOTH, back))
+        totals[turn] = summed.astype(bf16)
+        if splits == 1 and turn:
+            pairs = [(at, (at + turn) % tensor_size) for at in range(tensor_size)]
+            totals[turn] = lax.ppermute(totals[turn], "tensor", pairs)
+
+    if splits == 1:
+        expert_id, tensor_index = lax.axis_index("loop") // group_size, lax.axis_index("tensor")
+        landed = []
+        for turn in range(expert_count):
+            half_at = (expert_id + turn) % expert_count
+            sending = totals[0]
+            for other in range(1, expert_count):
+                sending = jnp.where((tensor_index - half_at) % tensor_size == other, totals[other], sending)
+            pairs = [
+                (at, (at // group_size + turn) % expert_count * group_size + (at % group_size ^ (blocks // 2)))
+                for at in range(loop_size)
+            ]
+            landed.append(lax.ppermute(sending, "loop", pairs) if turn else sending)
+    else:
+        landed = [
+            lax.ppermute(totals[turn], BOTH, [(target, source) for source, target in routes[turn]])
+            for turn in range(expert_count)
+        ]
 
     return kernel_call(
-        functools.partial(finish_kernel, expert_count),
+        functools.partial(finish_kernel, blocks),
         jax.ShapeDtypeStruct((home_rows, features), bf16),
         (grad_out, picked_tokens, *landed),
         [pltpu.VMEM((PADDED, features), bf16)],

time: 74.2 us -> 70.2 us (0.946)
  waiting for transfers between devices: 24.7 us -> 13.1 us
  starting transfers between devices: 22.5 us -> 29.3 us
    ppermute x2, starting transfers between devices: 1.19 us -> 6.4 us  [the longest x1 4 us: shards(): totals[turn] = lax.ppermute(totals[turn], 'tensor', pairs)]
    ppermute x15, waiting for transfers between devices: 9.72 us -> 5.7 us  [swap(): return lax.ppermute(values, 'loop', pairs)]
    ppermute x2, waiting for transfers between devices: 11.2 us -> 7.35 us  [the longest x1 4.41 us: shards(): landed.append(lax.ppermute(sending, 'loop', pairs) if turn else sending)]
    ppermute x1, waiting for transfers between devices: 3.81 us -> 0.01 us  [shards(): before = after = [lax.ppermute(edge, 'tensor', [(0, 1), (1, 0)])]]
    ppermute x1, starting transfers between devices: 0.46 us -> 4.22 us  [shards(): before = after = [lax.ppermute(edge, 'tensor', [(0, 1), (1, 0)])]]
    ppermute x2, starting transfers between devices: 7.29 us -> 5.76 us  [shards(): lax.ppermute(outgoing[turn], BOTH, routes[turn])]
    pallas_call x7 -> x8, Pallas kernels: 26.2 us -> 26.8 us  [kernel_call(): pl.pallas_call(body, out_shape=out_shape, in_specs=[LEFT] * left + [VMEM]...]
  transfers between devices with their start and end apart: 20 -> 20, of which waited for: 9 -> 8; matrix products, arithmetic and copies ran while one was open for 1% -> 1% of each run, Pallas kernels for 21% -> 23%
where the time goes in v3:
time: 70.2 us; the launch traced here: 70 us
  starting transfers between devices  29.3 us (42%)
  Pallas kernels  26.8 us (38%)
  waiting for transfers between devices  13.1 us (19%)
    pallas_call x8, Pallas kernels, kernel_call(): pl.pallas_call(body, out_shape=out_shape, in_specs=[LEFT] * left + [VMEM]...  26.8 us
    ppermute x15, starting transfers between devices, swap(): return lax.ppermute(values, 'loop', pairs)  13 us
    ppermute x2, starting transfers between devices, shards(): lax.ppermute(outgoing[turn], BOTH, routes[turn])  5.76 us
    ppermute x15, waiting for transfers between devices, swap(): return lax.ppermute(values, 'loop', pairs)  5.7 us
    ppermute x1, waiting for transfers between devices, shards(): landed.append(lax.ppermute(sending, 'loop', pairs) if turn else sending)  4.41 us
    ppermute x1, starting transfers between devices, shards(): before = after = [lax.ppermute(edge, 'tensor', [(0, 1), (1, 0)])]  4.22 us
    ppermute x1, starting transfers between devices, shards(): totals[turn] = lax.ppermute(totals[turn], 'tensor', pairs)  4 us
    ppermute x1, waiting for transfers between devices, shards(): totals[turn] = lax.ppermute(totals[turn], 'tensor', pairs)  2.94 us
  transfers between devices with their start and end apart: 20, of which 8 were waited for; matrix products, arithmetic and copies ran while one was open for 1% of the time, Pallas kernels for 23%

profile of v3, /device:TPU:0, one launch (start us, length us, event | category | flops | bytes accessed | tf_op | source)
XLA Modules:
  0.0 70.0 jit_solution(15018656161810862551)
XLA Ops:
  0.0 1.4 %shard_map.64 = (bf16[28,2048]{1,0:T(8,128)(2,1)S(1)}, bf16[28,2048]{1,0:T(8,128)(2,1)S(1)}, bf16[16,2048]{1,0:T(8,128)(2,1)S(1)}) custom-call(bf16[128,2048]{1,0:T(8,128)(2,1)} %grad.1, s32[2,416]{1,0:T(2,128)} %picked.3, f32[2,416]{1,0:T(2,128)} %gates_from.1, bf16[208,2048]{1,0:T(8,128)(2,1)} %refs_1_), custom_call_target="tpu_custom_call" | custom-call | bytes 1382912 | tf_op jit(solution)/shard_map/pallas_call | solution.py:38
  1.4 5.1 %collective-permute-start = (bf16[28,2048]{1,0:T(8,128)(2,1)S(1)}, bf16[28,2048]{1,0:T(8,128)(2,1)S(1)}, u32[]{:S(2)}, u32[]{:S(2)}) collective-permute-start(bf16[28,2048]{1,0:T(8,128)(2,1)S(1)} %get-tuple-element.27), channel_id=1, source_target_pairs={{0,24},{1,0},{2,26},{3,2},{4,28},{5,4},{6,30},{7,6},{8,16},{9,8},{... | collective-permute-start | bytes 344072 | tf_op jit(solution)/shard_map/ppermute | solution.py:288
  6.5 0.7 collective-permute-start.1
  7.2 5.9 %shard_map.65 = (bf16[1,2048,2048]{2,1,0:T(8,128)(2,1)S(1)}, bf16[1,2048,2048]{2,1,0:T(8,128)(2,1)S(1)}) custom-call(bf16[2048,4096]{1,0:T(8,128)(2,1)} %weight), custom_call_target="tpu_custom_call" | custom-call | bytes 16777216 | tf_op jit(solution)/shard_map/pallas_call | solution.py:38
  13.1 0.0 collective-permute-done.refs_0_
  13.1 0.0 collective-permute-done.1.refs_1_
  13.2 0.1 collective-permute-start.2
  13.3 1.6 %collective-permute-start.4 = (bf16[2,28,2048]{2,1,0:T(8,128)(2,1)S(1)}, bf16[2,28,2048]{2,1,0:T(8,128)(2,1)S(1)}, u32[]{:S(2)}, u32[]{:S(2)}) collective-permute-start(bf16[2,28,2048]{2,1,0:T(8,128)(2,1)S(1)} %shard_map.66.refs_4_), channel_id=1, source_target_pairs={{0,4},{2,6},{4,0},{6,2},{8,12},{10,14},{12,8},{14,10},{16,20},{18,... | collective-permute-start | bytes 688136 | tf_op jit(solution)/shard_map/ppermute | solution.py:56
  14.8 0.0 collective-permute-start.5
  14.8 2.0 %collective-permute-start.6 = (bf16[2,28,2048]{2,1,0:T(8,128)(2,1)S(1)}, bf16[2,28,2048]{2,1,0:T(8,128)(2,1)S(1)}, u32[]{:S(2)}, u32[]{:S(2)}) collective-permute-start(bf16[2,28,2048]{2,1,0:T(8,128)(2,1)S(1)} %shard_map.66.refs_4_), channel_id=1, source_target_pairs={{0,12},{2,14},{4,8},{6,10},{8,4},{10,6},{12,0},{14,2},{16,28},{18,... | collective-permute-start | bytes 688136 | tf_op jit(solution)/shard_map/ppermute | solution.py:56
  16.8 0.0 collective-permute-done.2.refs_5_
  16.8 0.0 copy-start
  16.8 0.0 copy-start.2
  16.8 4.2 %collective-permute-start.3 = (bf16[16,2048]{1,0:T(8,128)(2,1)S(1)}, bf16[16,2048]{1,0:T(8,128)(2,1)S(1)}, u32[]{:S(2)}, u32[]{:S(2)}) collective-permute-start(bf16[16,2048]{1,0:T(8,128)(2,1)S(1)} %get-tuple-element.36), channel_id=1, source_target_pairs={{0,1},{1,0},{2,3},{3,2},{4,5},{5,4},{6,7},{7,6},{8,9},{9,8},{10,11... | collective-permute-start | bytes 196616 | tf_op jit(solution)/shard_map/ppermute | solution.py:310
  21.0 5.9 %shard_map.67 = (bf16[1,2048,2048]{2,1,0:T(8,128)(2,1)S(1)}, bf16[1,2048,2048]{2,1,0:T(8,128)(2,1)S(1)}) custom-call(bf16[4096,2048]{1,0:T(8,128)(2,1)} %weight.1), custom_call_target="tpu_custom_call" | custom-call | bytes 16777216 | tf_op jit(solution)/shard_map/pallas_call | solution.py:38
  27.0 0.0 collective-permute-done.3.refs_0_.refs_2_
  27.0 0.0 copy-done
  27.0 0.0 copy-done.2
  27.0 2.0 %shard_map.68.refs_3_ = f32[224,2048]{1,0:T(8,128)S(1)} custom-call(s32[2,416]{1,0:T(2,128)S(1)} %copy-done.2, bf16[16,2048]{1,0:T(8,128)(2,1)S(1)} %collective-permute-done.3.refs_0_.refs_2_, bf16[208,2048]{1,0:T(8,128)(2,1)S(1)} %copy-done, bf16[16,2048]{1,0:T(8,128)(2,1)S(1)} %collective-permute-done.3.refs_0_.refs_2_), custom_call_target="tpu_custom_call" | custom-call | flops 220200960 | bytes 986368 | tf_op jit(solution)/shard_map/pallas_call | solution.py:38
  29.0 0.0 collective-permute-done.4.refs_6_
  29.0 0.0 collective-permute-done.5.refs_8_
  29.0 0.0 collective-permute-done.6.refs_10_
  29.0 0.1 collective-permute-start.7
  29.1 0.5 collective-permute-start.8
  29.6 0.1 collective-permute-start.9
  29.6 0.9 %collective-permute-done.7.refs_7_ = bf16[2,28,2048]{2,1,0:T(8,128)(2,1)S(1)} collective-permute-done((bf16[2,28,2048]{2,1,0:T(8,128)(2,1)S(1)}, bf16[2,28,2048]{2,1,0:T(8,128)(2,1)S(1)}, u32[]{:S(2)}, u32[]{:S(2)}) %collective-permute-start.7) | collective-permute-done | bytes 229408 | tf_op jit(solution)/shard_map/ppermute | solution.py:56
  30.6 0.4 collective-permute-done.8.refs_9_
  31.0 0.4 collective-permute-done.9.refs_11_
  31.3 7.6 %shard_map.69 = (bf16[224,2048]{1,0:T(8,128)(2,1)S(1)}, bf16[4,28,2048]{2,1,0:T(8,128)(2,1)S(1)}, bf16[4,28,2048]{2,1,0:T(8,128)(2,1)S(1)}) custom-call(bf16[1,2048,2048]{2,1,0:T(8,128)(2,1)S(1)} %get-tuple-element.29.refs_0_, bf16[1,2048,2048]{2,1,0:T(8,128)(2,1)S(1)} %get-tuple-element.30.refs_1_, bf16[1,2048,2048]{2,1,0:T(8,128)(2,1)S(1)} %get-tuple-element.35.refs_2_, ...), custom_call_target="tpu_custom_call" | custom-call | flops 5637144576 | bytes 28835840 | tf_op jit(solution)/shard_map/pallas_call | solution.py:38
  38.9 0.2 collective-permute-start.10
  39.1 0.0 copy-start.1
  39.1 2.6 %shard_map.70 = (bf16[4,28,2048]{2,1,0:T(8,128)(2,1)S(1)}, bf16[4,28,2048]{2,1,0:T(8,128)(2,1)S(1)}) custom-call(bf16[1,2048,2048]{2,1,0:T(8,128)(2,1)S(1)} %get-tuple-element.38.weight, bf16[224,2048]{1,0:T(8,128)(2,1)S(1)} %get-tuple-element.44.pre_grad), custom_call_target="tpu_custom_call" | custom-call | flops 1879048192 | bytes 9306112 | tf_op jit(solution)/shard_map/pallas_call | solution.py:38
  41.7 0.4 collective-permute-start.15
  42.2 0.0 collective-permute-done.10
  42.2 0.2 fusion.8
  42.4 1.0 %collective-permute-start.13 = (bf16[28,2048]{1,0:T(8,128)(2,1)S(1)}, bf16[28,2048]{1,0:T(8,128)(2,1)S(1)}, u32[]{:S(2)}, u32[]{:S(2)}) collective-permute-start(bf16[28,2048]{1,0:T(8,128)(2,1)S(1)} %get-tuple-element.57), channel_id=1, source_target_pairs={{0,12},{2,14},{4,8},{6,10},{8,4},{10,6},{12,0},{14,2},{16,28},{18,... | collective-permute-start | bytes 344072 | tf_op jit(solution)/shard_map/ppermute | solution.py:56
  43.4 2.0 %collective-permute-start.12 = (bf16[28,2048]{1,0:T(8,128)(2,1)S(1)}, bf16[28,2048]{1,0:T(8,128)(2,1)S(1)}, u32[]{:S(2)}, u32[]{:S(2)}) collective-permute-start(bf16[28,2048]{1,0:T(8,128)(2,1)S(1)} %get-tuple-element.58), channel_id=1, source_target_pairs={{0,8},{2,10},{4,12},{6,14},{8,0},{10,2},{12,4},{14,6},{16,24},{18,... | collective-permute-start | bytes 344072 | tf_op jit(solution)/shard_map/ppermute | solution.py:56
  45.4 0.5 collective-permute-start.11
  45.9 0.0 collective-permute-done.15
  45.9 0.2 convert_add_fusion
  46.1 1.0 %collective-permute-start.18 = (bf16[28,2048]{1,0:T(8,128)(2,1)S(1)}, bf16[28,2048]{1,0:T(8,128)(2,1)S(1)}, u32[]{:S(2)}, u32[]{:S(2)}) collective-permute-start(bf16[28,2048]{1,0:T(8,128)(2,1)S(1)} %get-tuple-element.54), channel_id=1, source_target_pairs={{0,12},{2,14},{4,8},{6,10},{8,4},{10,6},{12,0},{14,2},{16,28},{18,... | collective-permute-start | bytes 344072 | tf_op jit(solution)/shard_map/ppermute | solution.py:56
  47.1 2.0 %collective-permute-start.17 = (bf16[28,2048]{1,0:T(8,128)(2,1)S(1)}, bf16[28,2048]{1,0:T(8,128)(2,1)S(1)}, u32[]{:S(2)}, u32[]{:S(2)}) collective-permute-start(bf16[28,2048]{1,0:T(8,128)(2,1)S(1)} %get-tuple-element.55), channel_id=1, source_target_pairs={{0,8},{2,10},{4,12},{6,14},{8,0},{10,2},{12,4},{14,6},{16,24},{18,... | collective-permute-start | bytes 344072 | tf_op jit(solution)/shard_map/ppermute | solution.py:56
  49.1 0.5 collective-permute-done.13
  49.7 1.5 %collective-permute-start.16 = (bf16[28,2048]{1,0:T(8,128)(2,1)S(1)}, bf16[28,2048]{1,0:T(8,128)(2,1)S(1)}, u32[]{:S(2)}, u32[]{:S(2)}) collective-permute-start(bf16[28,2048]{1,0:T(8,128)(2,1)S(1)} %get-tuple-element.53), channel_id=1, source_target_pairs={{0,4},{2,6},{4,0},{6,2},{8,12},{10,14},{12,8},{14,10},{16,20},{18,... | collective-permute-start | bytes 344072 | tf_op jit(solution)/shard_map/ppermute | solution.py:56
  51.1 1.3 %collective-permute-done.12 = bf16[28,2048]{1,0:T(8,128)(2,1)S(1)} collective-permute-done((bf16[28,2048]{1,0:T(8,128)(2,1)S(1)}, bf16[28,2048]{1,0:T(8,128)(2,1)S(1)}, u32[]{:S(2)}, u32[]{:S(2)}) %collective-permute-start.12) | collective-permute-done | bytes 114720 | tf_op jit(solution)/shard_map/ppermute | solution.py:56
  52.5 2.1 %collective-permute-done.11 = bf16[28,2048]{1,0:T(8,128)(2,1)S(1)} collective-permute-done((bf16[28,2048]{1,0:T(8,128)(2,1)S(1)}, bf16[28,2048]{1,0:T(8,128)(2,1)S(1)}, u32[]{:S(2)}, u32[]{:S(2)}) %collective-permute-start.11) | collective-permute-done | bytes 114720 | tf_op jit(solution)/shard_map/ppermute | solution.py:56
  54.6 0.1 fusion.7
  54.7 4.0 %collective-permute-start.14 = (bf16[28,2048]{1,0:T(8,128)(2,1)S(1)}, bf16[28,2048]{1,0:T(8,128)(2,1)S(1)}, u32[]{:S(2)}, u32[]{:S(2)}) collective-permute-start(bf16[28,2048]{1,0:T(8,128)(2,1)S(1)} %fusion.7), channel_id=1, source_target_pairs={{0,1},{1,0},{2,3},{3,2},{4,5},{5,4},{6,7},{7,6},{8,9},{9,8},{10,11... | collective-permute-start | bytes 344072 | tf_op jit(solution)/shard_map/ppermute | solution.py:358
  58.7 0.0 collective-permute-done.18
  58.7 0.0 collective-permute-done.17
  58.7 0.0 collective-permute-done.16
  58.7 2.9 %collective-permute-done.14 = bf16[28,2048]{1,0:T(8,128)(2,1)S(1)} collective-permute-done((bf16[28,2048]{1,0:T(8,128)(2,1)S(1)}, bf16[28,2048]{1,0:T(8,128)(2,1)S(1)}, u32[]{:S(2)}, u32[]{:S(2)}) %collective-permute-start.14) | collective-permute-done | bytes 114720 | tf_op jit(solution)/shard_map/ppermute | solution.py:358
  61.6 0.1 broadcast_select_fusion
  61.7 2.4 %collective-permute-start.19 = (bf16[28,2048]{1,0:T(8,128)(2,1)S(1)}, bf16[28,2048]{1,0:T(8,128)(2,1)S(1)}, u32[]{:S(2)}, u32[]{:S(2)}) collective-permute-start(bf16[28,2048]{1,0:T(8,128)(2,1)S(1)} %get-tuple-element.47), channel_id=1, source_target_pairs={{0,24},{2,26},{4,28},{6,30},{8,16},{10,18},{12,20},{14,22},{16,8},... | collective-permute-start | bytes 344072 | tf_op jit(solution)/shard_map/ppermute | solution.py:372
  64.1 4.4 %collective-permute-done.19.refs_1_ = bf16[28,2048]{1,0:T(8,128)(2,1)S(1)} collective-permute-done((bf16[28,2048]{1,0:T(8,128)(2,1)S(1)}, bf16[28,2048]{1,0:T(8,128)(2,1)S(1)}, u32[]{:S(2)}, u32[]{:S(2)}) %collective-permute-start.19) | collective-permute-done | bytes 114720 | tf_op jit(solution)/shard_map/ppermute | solution.py:372
  68.5 0.0 copy-done.1
  68.5 1.4 %shard_map.71 = bf16[128,2048]{1,0:T(8,128)(2,1)} custom-call(bf16[128,2048]{1,0:T(8,128)(2,1)S(1)} %copy-done.1, s32[2,416]{1,0:T(2,128)S(1)} %copy-done.2, bf16[28,2048]{1,0:T(8,128)(2,1)S(1)} %broadcast_select_fusion.1.refs_0_, bf16[28,2048]{1,0:T(8,128)(2,1)S(1)} %collective-permute-done.19.refs_1_), custom_call_target="tpu_custom_call" | custom-call | bytes 756992 | tf_op jit(solution)/shard_map/pallas_call | solution.py:38
  (4 shorter events, 0.1 us)
Async XLA Ops:
  1.4 11.7 %collective-permute-start = (bf16[28,2048]{1,0:T(8,128)(2,1)S(1)}, bf16[28,2048]{1,0:T(8,128)(2,1)S(1)}, u32[]{:S(2)}, u32[]{:S(2)}) collective-permute-start(bf16[28,2048]{1,0:T(8,128)(2,1)S(1)} %get-tuple-element.27), channel_id=1, source_target_pairs={{0,24},{1,0},{2,26},{3,2},{4,28},{5,4},{6,30},{7,6},{8,16},{9,8},{... | collective-permute-start | bytes 344072 | tf_op jit(solution)/shard_map/ppermute | solution.py:288
  6.5 6.6 %collective-permute-start.1 = (bf16[28,2048]{1,0:T(8,128)(2,1)S(1)}, bf16[28,2048]{1,0:T(8,128)(2,1)S(1)}, u32[]{:S(2)}, u32[]{:S(2)}) collective-permute-start(bf16[28,2048]{1,0:T(8,128)(2,1)S(1)} %get-tuple-element.26), channel_id=1, source_target_pairs={{0,0},{1,24},{2,2},{3,26},{4,4},{5,28},{6,6},{7,30},{8,8},{9,16},{... | collective-permute-start | bytes 344072 | tf_op jit(solution)/shard_map/ppermute | solution.py:288
  13.2 3.6 %collective-permute-start.2 = (bf16[2,28,2048]{2,1,0:T(8,128)(2,1)S(1)}, bf16[2,28,2048]{2,1,0:T(8,128)(2,1)S(1)}, u32[]{:S(2)}, u32[]{:S(2)}) collective-permute-start(bf16[2,28,2048]{2,1,0:T(8,128)(2,1)S(1)} %shard_map.66.refs_4_), channel_id=1, source_target_pairs={{0,2},{2,0},{4,6},{6,4},{8,10},{10,8},{12,14},{14,12},{16,18},{18,... | collective-permute-start | bytes 688136 | tf_op jit(solution)/shard_map/ppermute | solution.py:56
  13.3 15.7 %collective-permute-start.4 = (bf16[2,28,2048]{2,1,0:T(8,128)(2,1)S(1)}, bf16[2,28,2048]{2,1,0:T(8,128)(2,1)S(1)}, u32[]{:S(2)}, u32[]{:S(2)}) collective-permute-start(bf16[2,28,2048]{2,1,0:T(8,128)(2,1)S(1)} %shard_map.66.refs_4_), channel_id=1, source_target_pairs={{0,4},{2,6},{4,0},{6,2},{8,12},{10,14},{12,8},{14,10},{16,20},{18,... | collective-permute-start | bytes 688136 | tf_op jit(solution)/shard_map/ppermute | solution.py:56
  14.8 14.2 %collective-permute-start.5 = (bf16[2,28,2048]{2,1,0:T(8,128)(2,1)S(1)}, bf16[2,28,2048]{2,1,0:T(8,128)(2,1)S(1)}, u32[]{:S(2)}, u32[]{:S(2)}) collective-permute-start(bf16[2,28,2048]{2,1,0:T(8,128)(2,1)S(1)} %shard_map.66.refs_4_), channel_id=1, source_target_pairs={{0,8},{2,10},{4,12},{6,14},{8,0},{10,2},{12,4},{14,6},{16,24},{18,... | collective-permute-start | bytes 688136 | tf_op jit(solution)/shard_map/ppermute | solution.py:56
  14.8 14.2 %collective-permute-start.6 = (bf16[2,28,2048]{2,1,0:T(8,128)(2,1)S(1)}, bf16[2,28,2048]{2,1,0:T(8,128)(2,1)S(1)}, u32[]{:S(2)}, u32[]{:S(2)}) collective-permute-start(bf16[2,28,2048]{2,1,0:T(8,128)(2,1)S(1)} %shard_map.66.refs_4_), channel_id=1, source_target_pairs={{0,12},{2,14},{4,8},{6,10},{8,4},{10,6},{12,0},{14,2},{16,28},{18,... | collective-permute-start | bytes 688136 | tf_op jit(solution)/shard_map/ppermute | solution.py:56
  16.8 10.2 %copy-start = (bf16[208,2048]{1,0:T(8,128)(2,1)S(1)}, bf16[208,2048]{1,0:T(8,128)(2,1)}, u32[]{:S(2)}) copy-start(bf16[208,2048]{1,0:T(8,128)(2,1)} %refs_1_) | copy-start | bytes 2555908
  16.8 10.2 %copy-start.2 = (s32[2,416]{1,0:T(2,128)S(1)}, s32[2,416]{1,0:T(2,128)}, u32[]{:S(2)}) copy-start(s32[2,416]{1,0:T(2,128)} %picked.3) | copy-start | bytes 9988
  16.8 10.2 %collective-permute-start.3 = (bf16[16,2048]{1,0:T(8,128)(2,1)S(1)}, bf16[16,2048]{1,0:T(8,128)(2,1)S(1)}, u32[]{:S(2)}, u32[]{:S(2)}) collective-permute-start(bf16[16,2048]{1,0:T(8,128)(2,1)S(1)} %get-tuple-element.36), channel_id=1, source_target_pairs={{0,1},{1,0},{2,3},{3,2},{4,5},{5,4},{6,7},{7,6},{8,9},{9,8},{10,11... | collective-permute-start | bytes 196616 | tf_op jit(solution)/shard_map/ppermute | solution.py:310
  29.0 1.6 %collective-permute-start.7 = (bf16[2,28,2048]{2,1,0:T(8,128)(2,1)S(1)}, bf16[2,28,2048]{2,1,0:T(8,128)(2,1)S(1)}, u32[]{:S(2)}, u32[]{:S(2)}) collective-permute-start(bf16[2,28,2048]{2,1,0:T(8,128)(2,1)S(1)} %collective-permute-done.4.refs_6_), channel_id=1, source_target_pairs={{0,2},{2,0},{4,6},{6,4},{8,10},{10,8},{12,14},{14,12},{16,18},{18,... | collective-permute-start | bytes 688136 | tf_op jit(solution)/shard_map/ppermute | solution.py:56
  29.1 1.9 %collective-permute-start.8 = (bf16[2,28,2048]{2,1,0:T(8,128)(2,1)S(1)}, bf16[2,28,2048]{2,1,0:T(8,128)(2,1)S(1)}, u32[]{:S(2)}, u32[]{:S(2)}) collective-permute-start(bf16[2,28,2048]{2,1,0:T(8,128)(2,1)S(1)} %collective-permute-done.5.refs_8_), channel_id=1, source_target_pairs={{0,2},{2,0},{4,6},{6,4},{8,10},{10,8},{12,14},{14,12},{16,18},{18,... | collective-permute-start | bytes 688136 | tf_op jit(solution)/shard_map/ppermute | solution.py:56
  29.6 1.8 %collective-permute-start.9 = (bf16[2,28,2048]{2,1,0:T(8,128)(2,1)S(1)}, bf16[2,28,2048]{2,1,0:T(8,128)(2,1)S(1)}, u32[]{:S(2)}, u32[]{:S(2)}) collective-permute-start(bf16[2,28,2048]{2,1,0:T(8,128)(2,1)S(1)} %collective-permute-done.6.refs_10_), channel_id=1, source_target_pairs={{0,2},{2,0},{4,6},{6,4},{8,10},{10,8},{12,14},{14,12},{16,18},{18,... | collective-permute-start | bytes 688136 | tf_op jit(solution)/shard_map/ppermute | solution.py:56
  38.9 3.2 %collective-permute-start.10 = (bf16[4,28,2048]{2,1,0:T(8,128)(2,1)S(1)}, bf16[4,28,2048]{2,1,0:T(8,128)(2,1)S(1)}, u32[]{:S(2)}, u32[]{:S(2)}) collective-permute-start(bf16[4,28,2048]{2,1,0:T(8,128)(2,1)S(1)} %get-tuple-element.43), channel_id=1, source_target_pairs={{0,2},{2,0},{4,6},{6,4},{8,10},{10,8},{12,14},{14,12},{16,18},{18,... | collective-permute-start | bytes 1376264 | tf_op jit(solution)/shard_map/ppermute | solution.py:56
  39.1 29.4 %copy-start.1 = (bf16[128,2048]{1,0:T(8,128)(2,1)S(1)}, bf16[128,2048]{1,0:T(8,128)(2,1)}, u32[]{:S(2)}) copy-start(bf16[128,2048]{1,0:T(8,128)(2,1)} %grad.1) | copy-start | bytes 1572868
  41.7 4.2 %collective-permute-start.15 = (bf16[4,28,2048]{2,1,0:T(8,128)(2,1)S(1)}, bf16[4,28,2048]{2,1,0:T(8,128)(2,1)S(1)}, u32[]{:S(2)}, u32[]{:S(2)}) collective-permute-start(bf16[4,28,2048]{2,1,0:T(8,128)(2,1)S(1)} %get-tuple-element.46), channel_id=1, source_target_pairs={{0,2},{2,0},{4,6},{6,4},{8,10},{10,8},{12,14},{14,12},{16,18},{18,... | collective-permute-start | bytes 1376264 | tf_op jit(solution)/shard_map/ppermute | solution.py:56
  42.4 7.3 %collective-permute-start.13 = (bf16[28,2048]{1,0:T(8,128)(2,1)S(1)}, bf16[28,2048]{1,0:T(8,128)(2,1)S(1)}, u32[]{:S(2)}, u32[]{:S(2)}) collective-permute-start(bf16[28,2048]{1,0:T(8,128)(2,1)S(1)} %get-tuple-element.57), channel_id=1, source_target_pairs={{0,12},{2,14},{4,8},{6,10},{8,4},{10,6},{12,0},{14,2},{16,28},{18,... | collective-permute-start | bytes 344072 | tf_op jit(solution)/shard_map/ppermute | solution.py:56
  43.4 9.1 %collective-permute-start.12 = (bf16[28,2048]{1,0:T(8,128)(2,1)S(1)}, bf16[28,2048]{1,0:T(8,128)(2,1)S(1)}, u32[]{:S(2)}, u32[]{:S(2)}) collective-permute-start(bf16[28,2048]{1,0:T(8,128)(2,1)S(1)} %get-tuple-element.58), channel_id=1, source_target_pairs={{0,8},{2,10},{4,12},{6,14},{8,0},{10,2},{12,4},{14,6},{16,24},{18,... | collective-permute-start | bytes 344072 | tf_op jit(solution)/shard_map/ppermute | solution.py:56
  45.4 9.2 %collective-permute-start.11 = (bf16[28,2048]{1,0:T(8,128)(2,1)S(1)}, bf16[28,2048]{1,0:T(8,128)(2,1)S(1)}, u32[]{:S(2)}, u32[]{:S(2)}) collective-permute-start(bf16[28,2048]{1,0:T(8,128)(2,1)S(1)} %get-tuple-element.56), channel_id=1, source_target_pairs={{0,4},{2,6},{4,0},{6,2},{8,12},{10,14},{12,8},{14,10},{16,20},{18,... | collective-permute-start | bytes 344072 | tf_op jit(solution)/shard_map/ppermute | solution.py:56
  46.1 12.6 %collective-permute-start.18 = (bf16[28,2048]{1,0:T(8,128)(2,1)S(1)}, bf16[28,2048]{1,0:T(8,128)(2,1)S(1)}, u32[]{:S(2)}, u32[]{:S(2)}) collective-permute-start(bf16[28,2048]{1,0:T(8,128)(2,1)S(1)} %get-tuple-element.54), channel_id=1, source_target_pairs={{0,12},{2,14},{4,8},{6,10},{8,4},{10,6},{12,0},{14,2},{16,28},{18,... | collective-permute-start | bytes 344072 | tf_op jit(solution)/shard_map/ppermute | solution.py:56
  47.1 11.6 %collective-permute-start.17 = (bf16[28,2048]{1,0:T(8,128)(2,1)S(1)}, bf16[28,2048]{1,0:T(8,128)(2,1)S(1)}, u32[]{:S(2)}, u32[]{:S(2)}) collective-permute-start(bf16[28,2048]{1,0:T(8,128)(2,1)S(1)} %get-tuple-element.55), channel_id=1, source_target_pairs={{0,8},{2,10},{4,12},{6,14},{8,0},{10,2},{12,4},{14,6},{16,24},{18,... | collective-permute-start | bytes 344072 | tf_op jit(solution)/shard_map/ppermute | solution.py:56
  49.7 9.0 %collective-permute-start.16 = (bf16[28,2048]{1,0:T(8,128)(2,1)S(1)}, bf16[28,2048]{1,0:T(8,128)(2,1)S(1)}, u32[]{:S(2)}, u32[]{:S(2)}) collective-permute-start(bf16[28,2048]{1,0:T(8,128)(2,1)S(1)} %get-tuple-element.53), channel_id=1, source_target_pairs={{0,4},{2,6},{4,0},{6,2},{8,12},{10,14},{12,8},{14,10},{16,20},{18,... | collective-permute-start | bytes 344072 | tf_op jit(solution)/shard_map/ppermute | solution.py:56
  54.7 7.0 %collective-permute-start.14 = (bf16[28,2048]{1,0:T(8,128)(2,1)S(1)}, bf16[28,2048]{1,0:T(8,128)(2,1)S(1)}, u32[]{:S(2)}, u32[]{:S(2)}) collective-permute-start(bf16[28,2048]{1,0:T(8,128)(2,1)S(1)} %fusion.7), channel_id=1, source_target_pairs={{0,1},{1,0},{2,3},{3,2},{4,5},{5,4},{6,7},{7,6},{8,9},{9,8},{10,11... | collective-permute-start | bytes 344072 | tf_op jit(solution)/shard_map/ppermute | solution.py:358
  61.7 6.8 %collective-permute-start.19 = (bf16[28,2048]{1,0:T(8,128)(2,1)S(1)}, bf16[28,2048]{1,0:T(8,128)(2,1)S(1)}, u32[]{:S(2)}, u32[]{:S(2)}) collective-permute-start(bf16[28,2048]{1,0:T(8,128)(2,1)S(1)} %get-tuple-element.47), channel_id=1, source_target_pairs={{0,24},{2,26},{4,28},{6,30},{8,16},{10,18},{12,20},{14,22},{16,8},... | collective-permute-start | bytes 344072 | tf_op jit(solution)/shard_map/ppermute | solution.py:372

commit v4 on v3

--- a/solution.py
+++ b/solution.py
@@ -321,7 +321,7 @@
         flops=2 * row_count * hidden * (per_tensor + 2 * halo),
     )
     down_weight = fetched(back_order, 0, down_source)
-    cross = after_all(cross, [slope, *down_weight])
+    cross = [after_all((piece,), [slope, *down_weight])[0] for piece in cross]
     down_weight = dict(zip(back_order, down_weight))
     gathered = [mine, beside]
     gathered += [piece for got in cross for piece in (got, swap(got, 1))]
@@ -350,7 +350,7 @@
         keep, give = made[turn]
         paired = keep.astype(f32) + swap(give, 1).astype(f32)
         summed = paired[0]
-        for m in range(1, group_size // 2):
+        for m in [group_size // 2 - 1, *range(1, group_size // 2 - 1)]:
             summed = summed + swap(paired[m].astype(bf16), 2 * m).astype(f32)
         totals[turn] = summed.astype(bf16)
         if splits == 1 and turn:

time: 70.2 us -> 67.5 us (0.962)
  starting transfers between devices: 29.3 us -> 26.7 us
    ppermute x15, starting transfers between devices: 13 us -> 11 us  [swap(): return lax.ppermute(values, 'loop', pairs)]
    ppermute x1, waiting for transfers between devices: 2.94 us -> 1.49 us  [shards(): totals[turn] = lax.ppermute(totals[turn], 'tensor', pairs)]
    ppermute x15, waiting for transfers between devices: 5.7 us -> 7.05 us  [swap(): return lax.ppermute(values, 'loop', pairs)]
    ppermute x1, starting transfers between devices: 4 us -> 3.3 us  [shards(): totals[turn] = lax.ppermute(totals[turn], 'tensor', pairs)]
  transfers between devices with their start and end apart: 20 -> 20, of which waited for: 8 -> 8; matrix products, arithmetic and copies ran while one was open for 1% -> 1% of each run, Pallas kernels for 23% -> 24%
where the time goes in v4:
time: 67.5 us; the launch traced here: 67.3 us
  Pallas kernels  26.9 us (40%)
  starting transfers between devices  26.7 us (40%)
  waiting for transfers between devices  13 us (19%)
    pallas_call x8, Pallas kernels, kernel_call(): pl.pallas_call(body, out_shape=out_shape, in_specs=[LEFT] * left + [VMEM]...  26.9 us
    ppermute x15, starting transfers between devices, swap(): return lax.ppermute(values, 'loop', pairs)  11 us
    ppermute x15, waiting for transfers between devices, swap(): return lax.ppermute(values, 'loop', pairs)  7.05 us
    ppermute x2, starting transfers between devices, shards(): lax.ppermute(outgoing[turn], BOTH, routes[turn])  5.76 us
    ppermute x1, waiting for transfers between devices, shards(): landed.append(lax.ppermute(sending, 'loop', pairs) if turn else sending)  4.44 us
    ppermute x1, starting transfers between devices, shards(): before = after = [lax.ppermute(edge, 'tensor', [(0, 1), (1, 0)])]  4.22 us
    ppermute x1, starting transfers between devices, shards(): totals[turn] = lax.ppermute(totals[turn], 'tensor', pairs)  3.3 us
    ppermute x1, starting transfers between devices, shards(): landed.append(lax.ppermute(sending, 'loop', pairs) if turn else sending)  2.48 us
  transfers between devices with their start and end apart: 20, of which 8 were waited for; matrix products, arithmetic and copies ran while one was open for 1% of the time, Pallas kernels for 24%

profile of v4, /device:TPU:0, one launch (start us, length us, event | category | flops | bytes accessed | tf_op | source)
XLA Modules:
  0.0 67.3 jit_solution(17947371672672440103)
XLA Ops:
  0.0 1.4 %shard_map.64 = (bf16[28,2048]{1,0:T(8,128)(2,1)S(1)}, bf16[28,2048]{1,0:T(8,128)(2,1)S(1)}, bf16[16,2048]{1,0:T(8,128)(2,1)S(1)}) custom-call(bf16[128,2048]{1,0:T(8,128)(2,1)} %grad.1, s32[2,416]{1,0:T(2,128)} %picked.3, f32[2,416]{1,0:T(2,128)} %gates_from.1, bf16[208,2048]{1,0:T(8,128)(2,1)} %refs_1_), custom_call_target="tpu_custom_call" | custom-call | bytes 1382912 | tf_op jit(solution)/shard_map/pallas_call | solution.py:38
  1.4 5.1 %collective-permute-start = (bf16[28,2048]{1,0:T(8,128)(2,1)S(1)}, bf16[28,2048]{1,0:T(8,128)(2,1)S(1)}, u32[]{:S(2)}, u32[]{:S(2)}) collective-permute-start(bf16[28,2048]{1,0:T(8,128)(2,1)S(1)} %get-tuple-element.27), channel_id=1, source_target_pairs={{0,24},{1,0},{2,26},{3,2},{4,28},{5,4},{6,30},{7,6},{8,16},{9,8},{... | collective-permute-start | bytes 344072 | tf_op jit(solution)/shard_map/ppermute | solution.py:288
  6.5 0.7 collective-permute-start.1
  7.2 5.9 %shard_map.65 = (bf16[1,2048,2048]{2,1,0:T(8,128)(2,1)S(1)}, bf16[1,2048,2048]{2,1,0:T(8,128)(2,1)S(1)}) custom-call(bf16[2048,4096]{1,0:T(8,128)(2,1)} %weight), custom_call_target="tpu_custom_call" | custom-call | bytes 16777216 | tf_op jit(solution)/shard_map/pallas_call | solution.py:38
  13.1 0.0 collective-permute-done.refs_0_
  13.1 0.0 collective-permute-done.1.refs_1_
  13.2 0.1 collective-permute-start.2
  13.3 1.6 %collective-permute-start.4 = (bf16[2,28,2048]{2,1,0:T(8,128)(2,1)S(1)}, bf16[2,28,2048]{2,1,0:T(8,128)(2,1)S(1)}, u32[]{:S(2)}, u32[]{:S(2)}) collective-permute-start(bf16[2,28,2048]{2,1,0:T(8,128)(2,1)S(1)} %shard_map.66.refs_4_), channel_id=1, source_target_pairs={{0,4},{2,6},{4,0},{6,2},{8,12},{10,14},{12,8},{14,10},{16,20},{18,... | collective-permute-start | bytes 688136 | tf_op jit(solution)/shard_map/ppermute | solution.py:56
  14.8 0.0 collective-permute-start.6
  14.8 2.0 %collective-permute-start.8 = (bf16[2,28,2048]{2,1,0:T(8,128)(2,1)S(1)}, bf16[2,28,2048]{2,1,0:T(8,128)(2,1)S(1)}, u32[]{:S(2)}, u32[]{:S(2)}) collective-permute-start(bf16[2,28,2048]{2,1,0:T(8,128)(2,1)S(1)} %shard_map.66.refs_4_), channel_id=1, source_target_pairs={{0,12},{2,14},{4,8},{6,10},{8,4},{10,6},{12,0},{14,2},{16,28},{18,... | collective-permute-start | bytes 688136 | tf_op jit(solution)/shard_map/ppermute | solution.py:56
  16.8 0.0 collective-permute-done.2.refs_5_
  16.8 0.0 copy-start
  16.8 0.0 copy-start.2
  16.8 4.2 %collective-permute-start.3 = (bf16[16,2048]{1,0:T(8,128)(2,1)S(1)}, bf16[16,2048]{1,0:T(8,128)(2,1)S(1)}, u32[]{:S(2)}, u32[]{:S(2)}) collective-permute-start(bf16[16,2048]{1,0:T(8,128)(2,1)S(1)} %get-tuple-element.36), channel_id=1, source_target_pairs={{0,1},{1,0},{2,3},{3,2},{4,5},{5,4},{6,7},{7,6},{8,9},{9,8},{10,11... | collective-permute-start | bytes 196616 | tf_op jit(solution)/shard_map/ppermute | solution.py:310
  21.0 5.9 %shard_map.67 = (bf16[1,2048,2048]{2,1,0:T(8,128)(2,1)S(1)}, bf16[1,2048,2048]{2,1,0:T(8,128)(2,1)S(1)}) custom-call(bf16[4096,2048]{1,0:T(8,128)(2,1)} %weight.1), custom_call_target="tpu_custom_call" | custom-call | bytes 16777216 | tf_op jit(solution)/shard_map/pallas_call | solution.py:38
  27.0 0.0 collective-permute-done.3.refs_0_.refs_2_
  27.0 0.0 copy-done
  27.0 0.0 copy-done.2
  27.0 2.0 %shard_map.68.refs_3_ = f32[224,2048]{1,0:T(8,128)S(1)} custom-call(s32[2,416]{1,0:T(2,128)S(1)} %copy-done.2, bf16[16,2048]{1,0:T(8,128)(2,1)S(1)} %collective-permute-done.3.refs_0_.refs_2_, bf16[208,2048]{1,0:T(8,128)(2,1)S(1)} %copy-done, bf16[16,2048]{1,0:T(8,128)(2,1)S(1)} %collective-permute-done.3.refs_0_.refs_2_), custom_call_target="tpu_custom_call" | custom-call | flops 220200960 | bytes 986368 | tf_op jit(solution)/shard_map/pallas_call | solution.py:38
  29.0 0.0 collective-permute-done.4.refs_6_
  29.0 0.1 collective-permute-start.5
  29.0 0.0 collective-permute-done.6.refs_8_
  29.1 0.5 collective-permute-start.7
  29.5 0.0 collective-permute-done.8.refs_10_
  29.5 0.1 collective-permute-start.9
  29.6 0.9 %collective-permute-done.5.refs_7_ = bf16[2,28,2048]{2,1,0:T(8,128)(2,1)S(1)} collective-permute-done((bf16[2,28,2048]{2,1,0:T(8,128)(2,1)S(1)}, bf16[2,28,2048]{2,1,0:T(8,128)(2,1)S(1)}, u32[]{:S(2)}, u32[]{:S(2)}) %collective-permute-start.5) | collective-permute-done | bytes 229408 | tf_op jit(solution)/shard_map/ppermute | solution.py:56
  30.6 0.4 collective-permute-done.7.refs_9_
  30.9 0.4 collective-permute-done.9.refs_11_
  31.3 7.6 %shard_map.69 = (bf16[224,2048]{1,0:T(8,128)(2,1)S(1)}, bf16[4,28,2048]{2,1,0:T(8,128)(2,1)S(1)}, bf16[4,28,2048]{2,1,0:T(8,128)(2,1)S(1)}) custom-call(bf16[1,2048,2048]{2,1,0:T(8,128)(2,1)S(1)} %get-tuple-element.29.refs_0_, bf16[1,2048,2048]{2,1,0:T(8,128)(2,1)S(1)} %get-tuple-element.30.refs_1_, bf16[1,2048,2048]{2,1,0:T(8,128)(2,1)S(1)} %get-tuple-element.35.refs_2_, ...), custom_call_target="tpu_custom_call" | custom-call | flops 5637144576 | bytes 28835840 | tf_op jit(solution)/shard_map/pallas_call | solution.py:38
  38.9 0.2 collective-permute-start.10
  39.1 0.0 copy-start.1
  39.1 2.6 %shard_map.70 = (bf16[4,28,2048]{2,1,0:T(8,128)(2,1)S(1)}, bf16[4,28,2048]{2,1,0:T(8,128)(2,1)S(1)}) custom-call(bf16[1,2048,2048]{2,1,0:T(8,128)(2,1)S(1)} %get-tuple-element.38.weight, bf16[224,2048]{1,0:T(8,128)(2,1)S(1)} %get-tuple-element.44.pre_grad), custom_call_target="tpu_custom_call" | custom-call | flops 1879048192 | bytes 9306112 | tf_op jit(solution)/shard_map/pallas_call | solution.py:38
  41.7 0.4 collective-permute-start.15
  42.1 0.0 collective-permute-done.10
  42.1 0.2 fusion.8
  42.3 0.2 collective-permute-start.13
  42.5 1.5 %collective-permute-start.12 = (bf16[28,2048]{1,0:T(8,128)(2,1)S(1)}, bf16[28,2048]{1,0:T(8,128)(2,1)S(1)}, u32[]{:S(2)}, u32[]{:S(2)}) collective-permute-start(bf16[28,2048]{1,0:T(8,128)(2,1)S(1)} %get-tuple-element.58), channel_id=1, source_target_pairs={{0,4},{2,6},{4,0},{6,2},{8,12},{10,14},{12,8},{14,10},{16,20},{18,... | collective-permute-start | bytes 344072 | tf_op jit(solution)/shard_map/ppermute | solution.py:56
  44.0 1.9 %collective-permute-start.11 = (bf16[28,2048]{1,0:T(8,128)(2,1)S(1)}, bf16[28,2048]{1,0:T(8,128)(2,1)S(1)}, u32[]{:S(2)}, u32[]{:S(2)}) collective-permute-start(bf16[28,2048]{1,0:T(8,128)(2,1)S(1)} %get-tuple-element.56), channel_id=1, source_target_pairs={{0,12},{2,14},{4,8},{6,10},{8,4},{10,6},{12,0},{14,2},{16,28},{18,... | collective-permute-start | bytes 344072 | tf_op jit(solution)/shard_map/ppermute | solution.py:56
  45.9 0.0 collective-permute-done.15
  45.9 0.2 convert_add_fusion
  46.1 0.2 collective-permute-start.18
  46.3 1.5 %collective-permute-start.17 = (bf16[28,2048]{1,0:T(8,128)(2,1)S(1)}, bf16[28,2048]{1,0:T(8,128)(2,1)S(1)}, u32[]{:S(2)}, u32[]{:S(2)}) collective-permute-start(bf16[28,2048]{1,0:T(8,128)(2,1)S(1)} %get-tuple-element.55), channel_id=1, source_target_pairs={{0,4},{2,6},{4,0},{6,2},{8,12},{10,14},{12,8},{14,10},{16,20},{18,... | collective-permute-start | bytes 344072 | tf_op jit(solution)/shard_map/ppermute | solution.py:56
  47.7 1.0 %collective-permute-done.13 = bf16[28,2048]{1,0:T(8,128)(2,1)S(1)} collective-permute-done((bf16[28,2048]{1,0:T(8,128)(2,1)S(1)}, bf16[28,2048]{1,0:T(8,128)(2,1)S(1)}, u32[]{:S(2)}, u32[]{:S(2)}) %collective-permute-start.13) | collective-permute-done | bytes 114720 | tf_op jit(solution)/shard_map/ppermute | solution.py:56
  48.8 0.9 %collective-permute-start.16 = (bf16[28,2048]{1,0:T(8,128)(2,1)S(1)}, bf16[28,2048]{1,0:T(8,128)(2,1)S(1)}, u32[]{:S(2)}, u32[]{:S(2)}) collective-permute-start(bf16[28,2048]{1,0:T(8,128)(2,1)S(1)} %get-tuple-element.53), channel_id=1, source_target_pairs={{0,12},{2,14},{4,8},{6,10},{8,4},{10,6},{12,0},{14,2},{16,28},{18,... | collective-permute-start | bytes 344072 | tf_op jit(solution)/shard_map/ppermute | solution.py:56
  49.7 0.0 collective-permute-done.12
  49.7 2.9 %collective-permute-done.11 = bf16[28,2048]{1,0:T(8,128)(2,1)S(1)} collective-permute-done((bf16[28,2048]{1,0:T(8,128)(2,1)S(1)}, bf16[28,2048]{1,0:T(8,128)(2,1)S(1)}, u32[]{:S(2)}, u32[]{:S(2)}) %collective-permute-start.11) | collective-permute-done | bytes 114720 | tf_op jit(solution)/shard_map/ppermute | solution.py:56
  52.5 0.1 fusion.7
  52.6 3.3 %collective-permute-start.14 = (bf16[28,2048]{1,0:T(8,128)(2,1)S(1)}, bf16[28,2048]{1,0:T(8,128)(2,1)S(1)}, u32[]{:S(2)}, u32[]{:S(2)}) collective-permute-start(bf16[28,2048]{1,0:T(8,128)(2,1)S(1)} %fusion.7), channel_id=1, source_target_pairs={{0,1},{1,0},{2,3},{3,2},{4,5},{5,4},{6,7},{7,6},{8,9},{9,8},{10,11... | collective-permute-start | bytes 344072 | tf_op jit(solution)/shard_map/ppermute | solution.py:358
  55.9 0.0 collective-permute-done.18
  55.9 0.0 collective-permute-done.17
  55.9 1.5 %collective-permute-done.16 = bf16[28,2048]{1,0:T(8,128)(2,1)S(1)} collective-permute-done((bf16[28,2048]{1,0:T(8,128)(2,1)S(1)}, bf16[28,2048]{1,0:T(8,128)(2,1)S(1)}, u32[]{:S(2)}, u32[]{:S(2)}) %collective-permute-start.16) | collective-permute-done | bytes 114720 | tf_op jit(solution)/shard_map/ppermute | solution.py:56
  57.3 1.5 %collective-permute-done.14 = bf16[28,2048]{1,0:T(8,128)(2,1)S(1)} collective-permute-done((bf16[28,2048]{1,0:T(8,128)(2,1)S(1)}, bf16[28,2048]{1,0:T(8,128)(2,1)S(1)}, u32[]{:S(2)}, u32[]{:S(2)}) %collective-permute-start.14) | collective-permute-done | bytes 114720 | tf_op jit(solution)/shard_map/ppermute | solution.py:358
  58.8 0.1 broadcast_select_fusion
  58.9 2.5 %collective-permute-start.19 = (bf16[28,2048]{1,0:T(8,128)(2,1)S(1)}, bf16[28,2048]{1,0:T(8,128)(2,1)S(1)}, u32[]{:S(2)}, u32[]{:S(2)}) collective-permute-start(bf16[28,2048]{1,0:T(8,128)(2,1)S(1)} %get-tuple-element.47), channel_id=1, source_target_pairs={{0,24},{2,26},{4,28},{6,30},{8,16},{10,18},{12,20},{14,22},{16,8},... | collective-permute-start | bytes 344072 | tf_op jit(solution)/shard_map/ppermute | solution.py:372
  61.4 4.4 %collective-permute-done.19.refs_1_ = bf16[28,2048]{1,0:T(8,128)(2,1)S(1)} collective-permute-done((bf16[28,2048]{1,0:T(8,128)(2,1)S(1)}, bf16[28,2048]{1,0:T(8,128)(2,1)S(1)}, u32[]{:S(2)}, u32[]{:S(2)}) %collective-permute-start.19) | collective-permute-done | bytes 114720 | tf_op jit(solution)/shard_map/ppermute | solution.py:372
  65.9 0.0 copy-done.1
  65.9 1.4 %shard_map.71 = bf16[128,2048]{1,0:T(8,128)(2,1)} custom-call(bf16[128,2048]{1,0:T(8,128)(2,1)S(1)} %copy-done.1, s32[2,416]{1,0:T(2,128)S(1)} %copy-done.2, bf16[28,2048]{1,0:T(8,128)(2,1)S(1)} %broadcast_select_fusion.1.refs_0_, bf16[28,2048]{1,0:T(8,128)(2,1)S(1)} %collective-permute-done.19.refs_1_), custom_call_target="tpu_custom_call" | custom-call | bytes 756992 | tf_op jit(solution)/shard_map/pallas_call | solution.py:38
  (4 shorter events, 0.1 us)
Async XLA Ops:
  1.4 11.7 %collective-permute-start = (bf16[28,2048]{1,0:T(8,128)(2,1)S(1)}, bf16[28,2048]{1,0:T(8,128)(2,1)S(1)}, u32[]{:S(2)}, u32[]{:S(2)}) collective-permute-start(bf16[28,2048]{1,0:T(8,128)(2,1)S(1)} %get-tuple-element.27), channel_id=1, source_target_pairs={{0,24},{1,0},{2,26},{3,2},{4,28},{5,4},{6,30},{7,6},{8,16},{9,8},{... | collective-permute-start | bytes 344072 | tf_op jit(solution)/shard_map/ppermute | solution.py:288
  6.5 6.6 %collective-permute-start.1 = (bf16[28,2048]{1,0:T(8,128)(2,1)S(1)}, bf16[28,2048]{1,0:T(8,128)(2,1)S(1)}, u32[]{:S(2)}, u32[]{:S(2)}) collective-permute-start(bf16[28,2048]{1,0:T(8,128)(2,1)S(1)} %get-tuple-element.26), channel_id=1, source_target_pairs={{0,0},{1,24},{2,2},{3,26},{4,4},{5,28},{6,6},{7,30},{8,8},{9,16},{... | collective-permute-start | bytes 344072 | tf_op jit(solution)/shard_map/ppermute | solution.py:288
  13.2 3.6 %collective-permute-start.2 = (bf16[2,28,2048]{2,1,0:T(8,128)(2,1)S(1)}, bf16[2,28,2048]{2,1,0:T(8,128)(2,1)S(1)}, u32[]{:S(2)}, u32[]{:S(2)}) collective-permute-start(bf16[2,28,2048]{2,1,0:T(8,128)(2,1)S(1)} %shard_map.66.refs_4_), channel_id=1, source_target_pairs={{0,2},{2,0},{4,6},{6,4},{8,10},{10,8},{12,14},{14,12},{16,18},{18,... | collective-permute-start | bytes 688136 | tf_op jit(solution)/shard_map/ppermute | solution.py:56
  13.3 15.7 %collective-permute-start.4 = (bf16[2,28,2048]{2,1,0:T(8,128)(2,1)S(1)}, bf16[2,28,2048]{2,1,0:T(8,128)(2,1)S(1)}, u32[]{:S(2)}, u32[]{:S(2)}) collective-permute-start(bf16[2,28,2048]{2,1,0:T(8,128)(2,1)S(1)} %shard_map.66.refs_4_), channel_id=1, source_target_pairs={{0,4},{2,6},{4,0},{6,2},{8,12},{10,14},{12,8},{14,10},{16,20},{18,... | collective-permute-start | bytes 688136 | tf_op jit(solution)/shard_map/ppermute | solution.py:56
  14.8 14.2 %collective-permute-start.6 = (bf16[2,28,2048]{2,1,0:T(8,128)(2,1)S(1)}, bf16[2,28,2048]{2,1,0:T(8,128)(2,1)S(1)}, u32[]{:S(2)}, u32[]{:S(2)}) collective-permute-start(bf16[2,28,2048]{2,1,0:T(8,128)(2,1)S(1)} %shard_map.66.refs_4_), channel_id=1, source_target_pairs={{0,8},{2,10},{4,12},{6,14},{8,0},{10,2},{12,4},{14,6},{16,24},{18,... | collective-permute-start | bytes 688136 | tf_op jit(solution)/shard_map/ppermute | solution.py:56
  14.8 14.7 %collective-permute-start.8 = (bf16[2,28,2048]{2,1,0:T(8,128)(2,1)S(1)}, bf16[2,28,2048]{2,1,0:T(8,128)(2,1)S(1)}, u32[]{:S(2)}, u32[]{:S(2)}) collective-permute-start(bf16[2,28,2048]{2,1,0:T(8,128)(2,1)S(1)} %shard_map.66.refs_4_), channel_id=1, source_target_pairs={{0,12},{2,14},{4,8},{6,10},{8,4},{10,6},{12,0},{14,2},{16,28},{18,... | collective-permute-start | bytes 688136 | tf_op jit(solution)/shard_map/ppermute | solution.py:56
  16.8 10.2 %copy-start = (bf16[208,2048]{1,0:T(8,128)(2,1)S(1)}, bf16[208,2048]{1,0:T(8,128)(2,1)}, u32[]{:S(2)}) copy-start(bf16[208,2048]{1,0:T(8,128)(2,1)} %refs_1_) | copy-start | bytes 2555908
  16.8 10.2 %copy-start.2 = (s32[2,416]{1,0:T(2,128)S(1)}, s32[2,416]{1,0:T(2,128)}, u32[]{:S(2)}) copy-start(s32[2,416]{1,0:T(2,128)} %picked.3) | copy-start | bytes 9988
  16.8 10.2 %collective-permute-start.3 = (bf16[16,2048]{1,0:T(8,128)(2,1)S(1)}, bf16[16,2048]{1,0:T(8,128)(2,1)S(1)}, u32[]{:S(2)}, u32[]{:S(2)}) collective-permute-start(bf16[16,2048]{1,0:T(8,128)(2,1)S(1)} %get-tuple-element.36), channel_id=1, source_target_pairs={{0,1},{1,0},{2,3},{3,2},{4,5},{5,4},{6,7},{7,6},{8,9},{9,8},{10,11... | collective-permute-start | bytes 196616 | tf_op jit(solution)/shard_map/ppermute | solution.py:310
  29.0 1.6 %collective-permute-start.5 = (bf16[2,28,2048]{2,1,0:T(8,128)(2,1)S(1)}, bf16[2,28,2048]{2,1,0:T(8,128)(2,1)S(1)}, u32[]{:S(2)}, u32[]{:S(2)}) collective-permute-start(bf16[2,28,2048]{2,1,0:T(8,128)(2,1)S(1)} %collective-permute-done.4.refs_6_), channel_id=1, source_target_pairs={{0,2},{2,0},{4,6},{6,4},{8,10},{10,8},{12,14},{14,12},{16,18},{18,... | collective-permute-start | bytes 688136 | tf_op jit(solution)/shard_map/ppermute | solution.py:56
  29.1 1.9 %collective-permute-start.7 = (bf16[2,28,2048]{2,1,0:T(8,128)(2,1)S(1)}, bf16[2,28,2048]{2,1,0:T(8,128)(2,1)S(1)}, u32[]{:S(2)}, u32[]{:S(2)}) collective-permute-start(bf16[2,28,2048]{2,1,0:T(8,128)(2,1)S(1)} %collective-permute-done.6.refs_8_), channel_id=1, source_target_pairs={{0,2},{2,0},{4,6},{6,4},{8,10},{10,8},{12,14},{14,12},{16,18},{18,... | collective-permute-start | bytes 688136 | tf_op jit(solution)/shard_map/ppermute | solution.py:56
  29.5 1.8 %collective-permute-start.9 = (bf16[2,28,2048]{2,1,0:T(8,128)(2,1)S(1)}, bf16[2,28,2048]{2,1,0:T(8,128)(2,1)S(1)}, u32[]{:S(2)}, u32[]{:S(2)}) collective-permute-start(bf16[2,28,2048]{2,1,0:T(8,128)(2,1)S(1)} %collective-permute-done.8.refs_10_), channel_id=1, source_target_pairs={{0,2},{2,0},{4,6},{6,4},{8,10},{10,8},{12,14},{14,12},{16,18},{18,... | collective-permute-start | bytes 688136 | tf_op jit(solution)/shard_map/ppermute | solution.py:56
  38.9 3.2 %collective-permute-start.10 = (bf16[4,28,2048]{2,1,0:T(8,128)(2,1)S(1)}, bf16[4,28,2048]{2,1,0:T(8,128)(2,1)S(1)}, u32[]{:S(2)}, u32[]{:S(2)}) collective-permute-start(bf16[4,28,2048]{2,1,0:T(8,128)(2,1)S(1)} %get-tuple-element.43), channel_id=1, source_target_pairs={{0,2},{2,0},{4,6},{6,4},{8,10},{10,8},{12,14},{14,12},{16,18},{18,... | collective-permute-start | bytes 1376264 | tf_op jit(solution)/shard_map/ppermute | solution.py:56
  39.1 26.7 %copy-start.1 = (bf16[128,2048]{1,0:T(8,128)(2,1)S(1)}, bf16[128,2048]{1,0:T(8,128)(2,1)}, u32[]{:S(2)}) copy-start(bf16[128,2048]{1,0:T(8,128)(2,1)} %grad.1) | copy-start | bytes 1572868
  41.7 4.2 %collective-permute-start.15 = (bf16[4,28,2048]{2,1,0:T(8,128)(2,1)S(1)}, bf16[4,28,2048]{2,1,0:T(8,128)(2,1)S(1)}, u32[]{:S(2)}, u32[]{:S(2)}) collective-permute-start(bf16[4,28,2048]{2,1,0:T(8,128)(2,1)S(1)} %get-tuple-element.46), channel_id=1, source_target_pairs={{0,2},{2,0},{4,6},{6,4},{8,10},{10,8},{12,14},{14,12},{16,18},{18,... | collective-permute-start | bytes 1376264 | tf_op jit(solution)/shard_map/ppermute | solution.py:56
  42.3 6.4 %collective-permute-start.13 = (bf16[28,2048]{1,0:T(8,128)(2,1)S(1)}, bf16[28,2048]{1,0:T(8,128)(2,1)S(1)}, u32[]{:S(2)}, u32[]{:S(2)}) collective-permute-start(bf16[28,2048]{1,0:T(8,128)(2,1)S(1)} %get-tuple-element.57), channel_id=1, source_target_pairs={{0,8},{2,10},{4,12},{6,14},{8,0},{10,2},{12,4},{14,6},{16,24},{18,... | collective-permute-start | bytes 344072 | tf_op jit(solution)/shard_map/ppermute | solution.py:56
  42.5 7.2 %collective-permute-start.12 = (bf16[28,2048]{1,0:T(8,128)(2,1)S(1)}, bf16[28,2048]{1,0:T(8,128)(2,1)S(1)}, u32[]{:S(2)}, u32[]{:S(2)}) collective-permute-start(bf16[28,2048]{1,0:T(8,128)(2,1)S(1)} %get-tuple-element.58), channel_id=1, source_target_pairs={{0,4},{2,6},{4,0},{6,2},{8,12},{10,14},{12,8},{14,10},{16,20},{18,... | collective-permute-start | bytes 344072 | tf_op jit(solution)/shard_map/ppermute | solution.py:56
  44.0 8.6 %collective-permute-start.11 = (bf16[28,2048]{1,0:T(8,128)(2,1)S(1)}, bf16[28,2048]{1,0:T(8,128)(2,1)S(1)}, u32[]{:S(2)}, u32[]{:S(2)}) collective-permute-start(bf16[28,2048]{1,0:T(8,128)(2,1)S(1)} %get-tuple-element.56), channel_id=1, source_target_pairs={{0,12},{2,14},{4,8},{6,10},{8,4},{10,6},{12,0},{14,2},{16,28},{18,... | collective-permute-start | bytes 344072 | tf_op jit(solution)/shard_map/ppermute | solution.py:56
  46.1 9.8 %collective-permute-start.18 = (bf16[28,2048]{1,0:T(8,128)(2,1)S(1)}, bf16[28,2048]{1,0:T(8,128)(2,1)S(1)}, u32[]{:S(2)}, u32[]{:S(2)}) collective-permute-start(bf16[28,2048]{1,0:T(8,128)(2,1)S(1)} %get-tuple-element.54), channel_id=1, source_target_pairs={{0,8},{2,10},{4,12},{6,14},{8,0},{10,2},{12,4},{14,6},{16,24},{18,... | collective-permute-start | bytes 344072 | tf_op jit(solution)/shard_map/ppermute | solution.py:56
  46.3 9.6 %collective-permute-start.17 = (bf16[28,2048]{1,0:T(8,128)(2,1)S(1)}, bf16[28,2048]{1,0:T(8,128)(2,1)S(1)}, u32[]{:S(2)}, u32[]{:S(2)}) collective-permute-start(bf16[28,2048]{1,0:T(8,128)(2,1)S(1)} %get-tuple-element.55), channel_id=1, source_target_pairs={{0,4},{2,6},{4,0},{6,2},{8,12},{10,14},{12,8},{14,10},{16,20},{18,... | collective-permute-start | bytes 344072 | tf_op jit(solution)/shard_map/ppermute | solution.py:56
  48.8 8.6 %collective-permute-start.16 = (bf16[28,2048]{1,0:T(8,128)(2,1)S(1)}, bf16[28,2048]{1,0:T(8,128)(2,1)S(1)}, u32[]{:S(2)}, u32[]{:S(2)}) collective-permute-start(bf16[28,2048]{1,0:T(8,128)(2,1)S(1)} %get-tuple-element.53), channel_id=1, source_target_pairs={{0,12},{2,14},{4,8},{6,10},{8,4},{10,6},{12,0},{14,2},{16,28},{18,... | collective-permute-start | bytes 344072 | tf_op jit(solution)/shard_map/ppermute | solution.py:56
  52.6 6.2 %collective-permute-start.14 = (bf16[28,2048]{1,0:T(8,128)(2,1)S(1)}, bf16[28,2048]{1,0:T(8,128)(2,1)S(1)}, u32[]{:S(2)}, u32[]{:S(2)}) collective-permute-start(bf16[28,2048]{1,0:T(8,128)(2,1)S(1)} %fusion.7), channel_id=1, source_target_pairs={{0,1},{1,0},{2,3},{3,2},{4,5},{5,4},{6,7},{7,6},{8,9},{9,8},{10,11... | collective-permute-start | bytes 344072 | tf_op jit(solution)/shard_map/ppermute | solution.py:358
  58.9 6.9 %collective-permute-start.19 = (bf16[28,2048]{1,0:T(8,128)(2,1)S(1)}, bf16[28,2048]{1,0:T(8,128)(2,1)S(1)}, u32[]{:S(2)}, u32[]{:S(2)}) collective-permute-start(bf16[28,2048]{1,0:T(8,128)(2,1)S(1)} %get-tuple-element.47), channel_id=1, source_target_pairs={{0,24},{2,26},{4,28},{6,30},{8,16},{10,18},{12,20},{14,22},{16,8},... | collective-permute-start | bytes 344072 | tf_op jit(solution)/shard_map/ppermute | solution.py:372

commit v5 on v4

--- a/solution.py
+++ b/solution.py
@@ -29,7 +29,7 @@
     return lax.dot_general(left, right, (((1,), (1,)), ((), ())), preferred_element_type=jnp.float32)
 
 
-def kernel_call(body, out_shape, operands, scratch=(), flops=0, vmem=4, left=0):
+def kernel_call(body, out_shape, operands, scratch=(), flops=0, vmem=4, left=0, out_left=False):
     nbytes = sum(o.size * o.dtype.itemsize for o in operands)
     operands = [
         pltpu.with_memory_space_constraint(o, pltpu.HBM) if at < left else o
@@ -39,7 +39,7 @@
         body,
         out_shape=out_shape,
         in_specs=[LEFT] * left + [VMEM] * (len(operands) - left),
-        out_specs=jax.tree.map(lambda _: VMEM, out_shape),
+        out_specs=jax.tree.map(lambda _: LEFT if out_left else VMEM, out_shape),
         scratch_shapes=scratch,
         cost_estimate=pl.CostEstimate(flops=flops, bytes_accessed=nbytes, transcendentals=0),
         compiler_params=pltpu.CompilerParams(vmem_limit_bytes=vmem << 20),
@@ -117,26 +117,47 @@
     copies[3].wait()
 
 
-def finish_kernel(blocks, grad, picked, *refs):
-    landed, out, held = refs[:-2], refs[-2], refs[-1]
-    expert_count = len(landed)
+def landed_expert(turn, blocks, expert_count):
+    if lax.axis_size("tensor") != expert_count:
+        return lax.rem(lax.axis_index("tensor") + turn, expert_count)
+    return lax.rem(lax.axis_index("loop") // blocks - turn + expert_count, expert_count)
+
+
+def place_rows(chosen, rows, held):
+    held[...] = jnp.zeros_like(held)
+    held[:MOST, :] = rows[...]
+    return lax.dot_general(chosen, held[...], (((0,), (0,)), ((), ())), preferred_element_type=jnp.float32)
+
+
+def begin_kernel(early, blocks, grad, picked, *refs):
+    landed, (total, chosen, held) = refs[:early], refs[early:]
+    expert_count = early + chosen.shape[0]
     home_rows = grad.shape[0]
     start = lax.axis_index("loop") * home_rows
-    direct = lax.axis_size("tensor") != expert_count
-    half = lax.axis_index("loop") // blocks
-    total = grad[...].astype(jnp.float32)
+    total[...] = grad[...].astype(jnp.float32)
     for turn in range(expert_count):
-        if direct:
-            expert = lax.rem(lax.axis_index("tensor") + turn, expert_count)
+        expert = landed_expert(turn, blocks, expert_count)
+        _, tokens = home_slots(picked[pl.ds(expert, 1), :], start, home_rows)
+        if turn < early:
+            total[...] += place_rows(tokens, landed[turn], held)
         else:
-            expert = lax.rem(half - turn + expert_count, expert_count)
-        _, chosen = home_slots(picked[pl.ds(expert, 1), :], start, home_rows)
-        held[...] = jnp.zeros_like(held)
-        held[:MOST, :] = landed[turn][...]
-        total += lax.dot_general(
-            chosen, held[...], (((0,), (0,)), ((), ())), preferred_element_type=jnp.float32
-        )
-    out[...] = total.astype(jnp.bfloat16)
+            chosen[turn - early] = tokens
+
+
+def finish_kernel(total, chosen, *refs):
+    landed, (out, held, ready, sent) = refs[:-4], refs[-4:]
+    parts, _, step = ready.shape
+    copies = []
+    for part in range(parts):
+        columns = pl.ds(part * step, step)
+        summed = total[:, columns]
+        for at, rows in enumerate(landed):
+            summed += place_rows(chosen[at], rows.at[:, columns], held)
+        ready[part] = summed.astype(jnp.bfloat16)
+        copies.append(pltpu.make_async_copy(ready.at[part], out.at[:, columns], sent.at[part]))
+        copies[-1].start()
+    for copy in copies:
+        copy.wait()
 
 
 def part_start(turn, axis, split, splits, expert_count, group_size, features):
@@ -376,11 +397,27 @@
             for turn in range(expert_count)
         ]
 
+    early = 1 if splits == 1 else 0
+    begun = kernel_call(
+        functools.partial(begin_kernel, early, blocks),
+        [
+            jax.ShapeDtypeStruct((home_rows, features), f32),
+            jax.ShapeDtypeStruct((expert_count - early, PADDED, home_rows), bf16),
+        ],
+        (grad_out, picked_tokens, *landed[:early]),
+        [pltpu.VMEM((PADDED, features), bf16)],
+    )
+    step = min(512, features)
     return kernel_call(
-        functools.partial(finish_kernel, blocks),
-        jax.ShapeDtypeStruct((home_rows, features), bf16),
-        (grad_out, picked_tokens, *landed),
-        [pltpu.VMEM((PADDED, features), bf16)],
+        finish_kernel,
+        pltpu.HBM((home_rows, features), bf16),
+        (*begun, *landed[early:]),
+        [
+            pltpu.VMEM((PADDED, step), bf16),
+            pltpu.VMEM((features // step, home_rows, step), bf16),
+            pltpu.SemaphoreType.DMA((features // step,)),
+        ],
+        out_left=True,
     )
 
 

time: 67.5 us -> 67.1 us (level)
    pallas_call x8 -> x9, Pallas kernels: 26.9 us -> 27 us  [kernel_call(): pl.pallas_call(body, out_shape=out_shape, in_specs=[LEFT] * left + [VMEM]...]
  transfers between devices with their start and end apart: 20 -> 20, of which waited for: 8 -> 8; matrix products, arithmetic and copies ran while one was open for 1% -> 1% of each run, Pallas kernels for 24% -> 25%
where the time goes in v5:
time: 67.1 us; the launch traced here: 66.9 us
  Pallas kernels  27 us (40%)
  starting transfers between devices  26.7 us (40%)
  waiting for transfers between devices  12.4 us (18%)
    pallas_call x9, Pallas kernels, kernel_call(): pl.pallas_call(body, out_shape=out_shape, in_specs=[LEFT] * left + [VMEM]...  27 us
    ppermute x15, starting transfers between devices, swap(): return lax.ppermute(values, 'loop', pairs)  11 us
    ppermute x15, waiting for transfers between devices, swap(): return lax.ppermute(values, 'loop', pairs)  7.05 us
    ppermute x2, starting transfers between devices, shards(): lax.ppermute(outgoing[turn], BOTH, routes[turn])  5.76 us
    ppermute x1, starting transfers between devices, shards(): before = after = [lax.ppermute(edge, 'tensor', [(0, 1), (1, 0)])]  4.22 us
    ppermute x1, waiting for transfers between devices, shards(): landed.append(lax.ppermute(sending, 'loop', pairs) if turn else sending)  3.9 us
    ppermute x1, starting transfers between devices, shards(): totals[turn] = lax.ppermute(totals[turn], 'tensor', pairs)  3.3 us
    ppermute x1, starting transfers between devices, shards(): landed.append(lax.ppermute(sending, 'loop', pairs) if turn else sending)  2.48 us
  transfers between devices with their start and end apart: 20, of which 8 were waited for; matrix products, arithmetic and copies ran while one was open for 1% of the time, Pallas kernels for 25%

profile of v5, /device:TPU:0, one launch (start us, length us, event | category | flops | bytes accessed | tf_op | source)
XLA Modules:
  0.0 66.9 jit_solution(592996800578773335)
XLA Ops:
  0.0 1.4 %shard_map.64 = (bf16[28,2048]{1,0:T(8,128)(2,1)S(1)}, bf16[28,2048]{1,0:T(8,128)(2,1)S(1)}, bf16[16,2048]{1,0:T(8,128)(2,1)S(1)}) custom-call(bf16[128,2048]{1,0:T(8,128)(2,1)} %grad.1, s32[2,416]{1,0:T(2,128)} %picked.3, f32[2,416]{1,0:T(2,128)} %gates_from.1, bf16[208,2048]{1,0:T(8,128)(2,1)} %refs_1_), custom_call_target="tpu_custom_call" | custom-call | bytes 1382912 | tf_op jit(solution)/shard_map/pallas_call | solution.py:38
  1.4 5.1 %collective-permute-start = (bf16[28,2048]{1,0:T(8,128)(2,1)S(1)}, bf16[28,2048]{1,0:T(8,128)(2,1)S(1)}, u32[]{:S(2)}, u32[]{:S(2)}) collective-permute-start(bf16[28,2048]{1,0:T(8,128)(2,1)S(1)} %get-tuple-element.29), channel_id=1, source_target_pairs={{0,24},{1,0},{2,26},{3,2},{4,28},{5,4},{6,30},{7,6},{8,16},{9,8},{... | collective-permute-start | bytes 344072 | tf_op jit(solution)/shard_map/ppermute | solution.py:309
  6.5 0.7 collective-permute-start.1
  7.2 5.9 %shard_map.65 = (bf16[1,2048,2048]{2,1,0:T(8,128)(2,1)S(1)}, bf16[1,2048,2048]{2,1,0:T(8,128)(2,1)S(1)}) custom-call(bf16[2048,4096]{1,0:T(8,128)(2,1)} %weight), custom_call_target="tpu_custom_call" | custom-call | bytes 16777216 | tf_op jit(solution)/shard_map/pallas_call | solution.py:38
  13.1 0.0 collective-permute-done.refs_0_
  13.1 0.0 collective-permute-done.1.refs_1_
  13.2 0.1 collective-permute-start.2
  13.3 1.6 %collective-permute-start.4 = (bf16[2,28,2048]{2,1,0:T(8,128)(2,1)S(1)}, bf16[2,28,2048]{2,1,0:T(8,128)(2,1)S(1)}, u32[]{:S(2)}, u32[]{:S(2)}) collective-permute-start(bf16[2,28,2048]{2,1,0:T(8,128)(2,1)S(1)} %shard_map.66.refs_4_), channel_id=1, source_target_pairs={{0,4},{2,6},{4,0},{6,2},{8,12},{10,14},{12,8},{14,10},{16,20},{18,... | collective-permute-start | bytes 688136 | tf_op jit(solution)/shard_map/ppermute | solution.py:56
  14.8 0.0 collective-permute-start.6
  14.8 2.0 %collective-permute-start.8 = (bf16[2,28,2048]{2,1,0:T(8,128)(2,1)S(1)}, bf16[2,28,2048]{2,1,0:T(8,128)(2,1)S(1)}, u32[]{:S(2)}, u32[]{:S(2)}) collective-permute-start(bf16[2,28,2048]{2,1,0:T(8,128)(2,1)S(1)} %shard_map.66.refs_4_), channel_id=1, source_target_pairs={{0,12},{2,14},{4,8},{6,10},{8,4},{10,6},{12,0},{14,2},{16,28},{18,... | collective-permute-start | bytes 688136 | tf_op jit(solution)/shard_map/ppermute | solution.py:56
  16.8 0.0 collective-permute-done.2.refs_5_
  16.8 0.0 copy-start
  16.8 0.0 copy-start.2
  16.8 4.2 %collective-permute-start.3 = (bf16[16,2048]{1,0:T(8,128)(2,1)S(1)}, bf16[16,2048]{1,0:T(8,128)(2,1)S(1)}, u32[]{:S(2)}, u32[]{:S(2)}) collective-permute-start(bf16[16,2048]{1,0:T(8,128)(2,1)S(1)} %get-tuple-element.38), channel_id=1, source_target_pairs={{0,1},{1,0},{2,3},{3,2},{4,5},{5,4},{6,7},{7,6},{8,9},{9,8},{10,11... | collective-permute-start | bytes 196616 | tf_op jit(solution)/shard_map/ppermute | solution.py:331
  21.0 5.9 %shard_map.67 = (bf16[1,2048,2048]{2,1,0:T(8,128)(2,1)S(1)}, bf16[1,2048,2048]{2,1,0:T(8,128)(2,1)S(1)}) custom-call(bf16[4096,2048]{1,0:T(8,128)(2,1)} %weight.1), custom_call_target="tpu_custom_call" | custom-call | bytes 16777216 | tf_op jit(solution)/shard_map/pallas_call | solution.py:38
  27.0 0.0 collective-permute-done.3.refs_0_.refs_2_
  27.0 0.0 copy-done
  27.0 0.0 copy-done.2
  27.0 2.0 %shard_map.68.refs_3_ = f32[224,2048]{1,0:T(8,128)S(1)} custom-call(s32[2,416]{1,0:T(2,128)S(1)} %copy-done.2, bf16[16,2048]{1,0:T(8,128)(2,1)S(1)} %collective-permute-done.3.refs_0_.refs_2_, bf16[208,2048]{1,0:T(8,128)(2,1)S(1)} %copy-done, bf16[16,2048]{1,0:T(8,128)(2,1)S(1)} %collective-permute-done.3.refs_0_.refs_2_), custom_call_target="tpu_custom_call" | custom-call | flops 220200960 | bytes 986368 | tf_op jit(solution)/shard_map/pallas_call | solution.py:38
  29.0 0.0 collective-permute-done.4.refs_6_
  29.0 0.1 collective-permute-start.5
  29.0 0.0 collective-permute-done.6.refs_8_
  29.1 0.5 collective-permute-start.7
  29.5 0.0 collective-permute-done.8.refs_10_
  29.5 0.1 collective-permute-start.9
  29.6 0.9 %collective-permute-done.5.refs_7_ = bf16[2,28,2048]{2,1,0:T(8,128)(2,1)S(1)} collective-permute-done((bf16[2,28,2048]{2,1,0:T(8,128)(2,1)S(1)}, bf16[2,28,2048]{2,1,0:T(8,128)(2,1)S(1)}, u32[]{:S(2)}, u32[]{:S(2)}) %collective-permute-start.5) | collective-permute-done | bytes 229408 | tf_op jit(solution)/shard_map/ppermute | solution.py:56
  30.6 0.4 collective-permute-done.7.refs_9_
  30.9 0.4 collective-permute-done.9.refs_11_
  31.3 7.6 %shard_map.69 = (bf16[224,2048]{1,0:T(8,128)(2,1)S(1)}, bf16[4,28,2048]{2,1,0:T(8,128)(2,1)S(1)}, bf16[4,28,2048]{2,1,0:T(8,128)(2,1)S(1)}) custom-call(bf16[1,2048,2048]{2,1,0:T(8,128)(2,1)S(1)} %get-tuple-element.31.refs_0_, bf16[1,2048,2048]{2,1,0:T(8,128)(2,1)S(1)} %get-tuple-element.32.refs_1_, bf16[1,2048,2048]{2,1,0:T(8,128)(2,1)S(1)} %get-tuple-element.37.refs_2_, ...), custom_call_target="tpu_custom_call" | custom-call | flops 5637144576 | bytes 28835840 | tf_op jit(solution)/shard_map/pallas_call | solution.py:38
  38.9 0.2 collective-permute-start.10
  39.1 0.0 copy-start.1
  39.1 2.6 %shard_map.70 = (bf16[4,28,2048]{2,1,0:T(8,128)(2,1)S(1)}, bf16[4,28,2048]{2,1,0:T(8,128)(2,1)S(1)}) custom-call(bf16[1,2048,2048]{2,1,0:T(8,128)(2,1)S(1)} %get-tuple-element.40.weight, bf16[224,2048]{1,0:T(8,128)(2,1)S(1)} %get-tuple-element.46.pre_grad), custom_call_target="tpu_custom_call" | custom-call | flops 1879048192 | bytes 9306112 | tf_op jit(solution)/shard_map/pallas_call | solution.py:38
  41.7 0.4 collective-permute-start.15
  42.1 0.0 collective-permute-done.10
  42.1 0.2 fusion.8
  42.3 0.2 collective-permute-start.13
  42.5 1.5 %collective-permute-start.12 = (bf16[28,2048]{1,0:T(8,128)(2,1)S(1)}, bf16[28,2048]{1,0:T(8,128)(2,1)S(1)}, u32[]{:S(2)}, u32[]{:S(2)}) collective-permute-start(bf16[28,2048]{1,0:T(8,128)(2,1)S(1)} %get-tuple-element.62), channel_id=1, source_target_pairs={{0,4},{2,6},{4,0},{6,2},{8,12},{10,14},{12,8},{14,10},{16,20},{18,... | collective-permute-start | bytes 344072 | tf_op jit(solution)/shard_map/ppermute | solution.py:56
  44.0 1.9 %collective-permute-start.11 = (bf16[28,2048]{1,0:T(8,128)(2,1)S(1)}, bf16[28,2048]{1,0:T(8,128)(2,1)S(1)}, u32[]{:S(2)}, u32[]{:S(2)}) collective-permute-start(bf16[28,2048]{1,0:T(8,128)(2,1)S(1)} %get-tuple-element.60), channel_id=1, source_target_pairs={{0,12},{2,14},{4,8},{6,10},{8,4},{10,6},{12,0},{14,2},{16,28},{18,... | collective-permute-start | bytes 344072 | tf_op jit(solution)/shard_map/ppermute | solution.py:56
  45.9 0.0 collective-permute-done.15
  45.9 0.2 convert_add_fusion
  46.1 0.2 collective-permute-start.18
  46.3 1.5 %collective-permute-start.17 = (bf16[28,2048]{1,0:T(8,128)(2,1)S(1)}, bf16[28,2048]{1,0:T(8,128)(2,1)S(1)}, u32[]{:S(2)}, u32[]{:S(2)}) collective-permute-start(bf16[28,2048]{1,0:T(8,128)(2,1)S(1)} %get-tuple-element.59), channel_id=1, source_target_pairs={{0,4},{2,6},{4,0},{6,2},{8,12},{10,14},{12,8},{14,10},{16,20},{18,... | collective-permute-start | bytes 344072 | tf_op jit(solution)/shard_map/ppermute | solution.py:56
  47.7 1.0 %collective-permute-done.13 = bf16[28,2048]{1,0:T(8,128)(2,1)S(1)} collective-permute-done((bf16[28,2048]{1,0:T(8,128)(2,1)S(1)}, bf16[28,2048]{1,0:T(8,128)(2,1)S(1)}, u32[]{:S(2)}, u32[]{:S(2)}) %collective-permute-start.13) | collective-permute-done | bytes 114720 | tf_op jit(solution)/shard_map/ppermute | solution.py:56
  48.8 0.9 %collective-permute-start.16 = (bf16[28,2048]{1,0:T(8,128)(2,1)S(1)}, bf16[28,2048]{1,0:T(8,128)(2,1)S(1)}, u32[]{:S(2)}, u32[]{:S(2)}) collective-permute-start(bf16[28,2048]{1,0:T(8,128)(2,1)S(1)} %get-tuple-element.57), channel_id=1, source_target_pairs={{0,12},{2,14},{4,8},{6,10},{8,4},{10,6},{12,0},{14,2},{16,28},{18,... | collective-permute-start | bytes 344072 | tf_op jit(solution)/shard_map/ppermute | solution.py:56
  49.7 0.0 collective-permute-done.12
  49.7 2.9 %collective-permute-done.11 = bf16[28,2048]{1,0:T(8,128)(2,1)S(1)} collective-permute-done((bf16[28,2048]{1,0:T(8,128)(2,1)S(1)}, bf16[28,2048]{1,0:T(8,128)(2,1)S(1)}, u32[]{:S(2)}, u32[]{:S(2)}) %collective-permute-start.11) | collective-permute-done | bytes 114720 | tf_op jit(solution)/shard_map/ppermute | solution.py:56
  52.5 0.1 fusion.7
  52.6 3.3 %collective-permute-start.14 = (bf16[28,2048]{1,0:T(8,128)(2,1)S(1)}, bf16[28,2048]{1,0:T(8,128)(2,1)S(1)}, u32[]{:S(2)}, u32[]{:S(2)}) collective-permute-start(bf16[28,2048]{1,0:T(8,128)(2,1)S(1)} %fusion.7), channel_id=1, source_target_pairs={{0,1},{1,0},{2,3},{3,2},{4,5},{5,4},{6,7},{7,6},{8,9},{9,8},{10,11... | collective-permute-start | bytes 344072 | tf_op jit(solution)/shard_map/ppermute | solution.py:379
  55.9 0.0 collective-permute-done.18
  55.9 0.0 collective-permute-done.17
  55.9 1.5 %collective-permute-done.16 = bf16[28,2048]{1,0:T(8,128)(2,1)S(1)} collective-permute-done((bf16[28,2048]{1,0:T(8,128)(2,1)S(1)}, bf16[28,2048]{1,0:T(8,128)(2,1)S(1)}, u32[]{:S(2)}, u32[]{:S(2)}) %collective-permute-start.16) | collective-permute-done | bytes 114720 | tf_op jit(solution)/shard_map/ppermute | solution.py:56
  57.3 1.5 %collective-permute-done.14 = bf16[28,2048]{1,0:T(8,128)(2,1)S(1)} collective-permute-done((bf16[28,2048]{1,0:T(8,128)(2,1)S(1)}, bf16[28,2048]{1,0:T(8,128)(2,1)S(1)}, u32[]{:S(2)}, u32[]{:S(2)}) %collective-permute-start.14) | collective-permute-done | bytes 114720 | tf_op jit(solution)/shard_map/ppermute | solution.py:379
  58.8 0.1 broadcast_select_fusion
  58.9 2.5 %collective-permute-start.19 = (bf16[28,2048]{1,0:T(8,128)(2,1)S(1)}, bf16[28,2048]{1,0:T(8,128)(2,1)S(1)}, u32[]{:S(2)}, u32[]{:S(2)}) collective-permute-start(bf16[28,2048]{1,0:T(8,128)(2,1)S(1)} %get-tuple-element.51), channel_id=1, source_target_pairs={{0,24},{2,26},{4,28},{6,30},{8,16},{10,18},{12,20},{14,22},{16,8},... | collective-permute-start | bytes 344072 | tf_op jit(solution)/shard_map/ppermute | solution.py:393
  61.4 0.0 copy-done.1
  61.4 0.5 shard_map.71
  62.0 3.9 %collective-permute-done.19.refs_0_ = bf16[28,2048]{1,0:T(8,128)(2,1)S(1)} collective-permute-done((bf16[28,2048]{1,0:T(8,128)(2,1)S(1)}, bf16[28,2048]{1,0:T(8,128)(2,1)S(1)}, u32[]{:S(2)}, u32[]{:S(2)}) %collective-permute-start.19) | collective-permute-done | bytes 114720 | tf_op jit(solution)/shard_map/ppermute | solution.py:393
  65.9 1.0 %shard_map.72 = bf16[128,2048]{1,0:T(8,128)(2,1)} custom-call(f32[128,2048]{1,0:T(8,128)S(1)} %get-tuple-element.49.total, bf16[1,32,128]{2,1,0:T(8,128)(2,1)S(1)} %get-tuple-element.50.chosen, bf16[28,2048]{1,0:T(8,128)(2,1)S(1)} %collective-permute-done.19.refs_0_), custom_call_target="tpu_custom_call" | custom-call | bytes 1171456 | tf_op jit(solution)/shard_map/pallas_call | solution.py:38
  (4 shorter events, 0.1 us)
Async XLA Ops:
  1.4 11.7 %collective-permute-start = (bf16[28,2048]{1,0:T(8,128)(2,1)S(1)}, bf16[28,2048]{1,0:T(8,128)(2,1)S(1)}, u32[]{:S(2)}, u32[]{:S(2)}) collective-permute-start(bf16[28,2048]{1,0:T(8,128)(2,1)S(1)} %get-tuple-element.29), channel_id=1, source_target_pairs={{0,24},{1,0},{2,26},{3,2},{4,28},{5,4},{6,30},{7,6},{8,16},{9,8},{... | collective-permute-start | bytes 344072 | tf_op jit(solution)/shard_map/ppermute | solution.py:309
  6.5 6.6 %collective-permute-start.1 = (bf16[28,2048]{1,0:T(8,128)(2,1)S(1)}, bf16[28,2048]{1,0:T(8,128)(2,1)S(1)}, u32[]{:S(2)}, u32[]{:S(2)}) collective-permute-start(bf16[28,2048]{1,0:T(8,128)(2,1)S(1)} %get-tuple-element.28), channel_id=1, source_target_pairs={{0,0},{1,24},{2,2},{3,26},{4,4},{5,28},{6,6},{7,30},{8,8},{9,16},{... | collective-permute-start | bytes 344072 | tf_op jit(solution)/shard_map/ppermute | solution.py:309
  13.2 3.6 %collective-permute-start.2 = (bf16[2,28,2048]{2,1,0:T(8,128)(2,1)S(1)}, bf16[2,28,2048]{2,1,0:T(8,128)(2,1)S(1)}, u32[]{:S(2)}, u32[]{:S(2)}) collective-permute-start(bf16[2,28,2048]{2,1,0:T(8,128)(2,1)S(1)} %shard_map.66.refs_4_), channel_id=1, source_target_pairs={{0,2},{2,0},{4,6},{6,4},{8,10},{10,8},{12,14},{14,12},{16,18},{18,... | collective-permute-start | bytes 688136 | tf_op jit(solution)/shard_map/ppermute | solution.py:56
  13.3 15.7 %collective-permute-start.4 = (bf16[2,28,2048]{2,1,0:T(8,128)(2,1)S(1)}, bf16[2,28,2048]{2,1,0:T(8,128)(2,1)S(1)}, u32[]{:S(2)}, u32[]{:S(2)}) collective-permute-start(bf16[2,28,2048]{2,1,0:T(8,128)(2,1)S(1)} %shard_map.66.refs_4_), channel_id=1, source_target_pairs={{0,4},{2,6},{4,0},{6,2},{8,12},{10,14},{12,8},{14,10},{16,20},{18,... | collective-permute-start | bytes 688136 | tf_op jit(solution)/shard_map/ppermute | solution.py:56
  14.8 14.2 %collective-permute-start.6 = (bf16[2,28,2048]{2,1,0:T(8,128)(2,1)S(1)}, bf16[2,28,2048]{2,1,0:T(8,128)(2,1)S(1)}, u32[]{:S(2)}, u32[]{:S(2)}) collective-permute-start(bf16[2,28,2048]{2,1,0:T(8,128)(2,1)S(1)} %shard_map.66.refs_4_), channel_id=1, source_target_pairs={{0,8},{2,10},{4,12},{6,14},{8,0},{10,2},{12,4},{14,6},{16,24},{18,... | collective-permute-start | bytes 688136 | tf_op jit(solution)/shard_map/ppermute | solution.py:56
  14.8 14.7 %collective-permute-start.8 = (bf16[2,28,2048]{2,1,0:T(8,128)(2,1)S(1)}, bf16[2,28,2048]{2,1,0:T(8,128)(2,1)S(1)}, u32[]{:S(2)}, u32[]{:S(2)}) collective-permute-start(bf16[2,28,2048]{2,1,0:T(8,128)(2,1)S(1)} %shard_map.66.refs_4_), channel_id=1, source_target_pairs={{0,12},{2,14},{4,8},{6,10},{8,4},{10,6},{12,0},{14,2},{16,28},{18,... | collective-permute-start | bytes 688136 | tf_op jit(solution)/shard_map/ppermute | solution.py:56
  16.8 10.2 %copy-start = (bf16[208,2048]{1,0:T(8,128)(2,1)S(1)}, bf16[208,2048]{1,0:T(8,128)(2,1)}, u32[]{:S(2)}) copy-start(bf16[208,2048]{1,0:T(8,128)(2,1)} %refs_1_) | copy-start | bytes 2555908
  16.8 10.2 %copy-start.2 = (s32[2,416]{1,0:T(2,128)S(1)}, s32[2,416]{1,0:T(2,128)}, u32[]{:S(2)}) copy-start(s32[2,416]{1,0:T(2,128)} %picked.3) | copy-start | bytes 9988
  16.8 10.2 %collective-permute-start.3 = (bf16[16,2048]{1,0:T(8,128)(2,1)S(1)}, bf16[16,2048]{1,0:T(8,128)(2,1)S(1)}, u32[]{:S(2)}, u32[]{:S(2)}) collective-permute-start(bf16[16,2048]{1,0:T(8,128)(2,1)S(1)} %get-tuple-element.38), channel_id=1, source_target_pairs={{0,1},{1,0},{2,3},{3,2},{4,5},{5,4},{6,7},{7,6},{8,9},{9,8},{10,11... | collective-permute-start | bytes 196616 | tf_op jit(solution)/shard_map/ppermute | solution.py:331
  29.0 1.6 %collective-permute-start.5 = (bf16[2,28,2048]{2,1,0:T(8,128)(2,1)S(1)}, bf16[2,28,2048]{2,1,0:T(8,128)(2,1)S(1)}, u32[]{:S(2)}, u32[]{:S(2)}) collective-permute-start(bf16[2,28,2048]{2,1,0:T(8,128)(2,1)S(1)} %collective-permute-done.4.refs_6_), channel_id=1, source_target_pairs={{0,2},{2,0},{4,6},{6,4},{8,10},{10,8},{12,14},{14,12},{16,18},{18,... | collective-permute-start | bytes 688136 | tf_op jit(solution)/shard_map/ppermute | solution.py:56
  29.1 1.9 %collective-permute-start.7 = (bf16[2,28,2048]{2,1,0:T(8,128)(2,1)S(1)}, bf16[2,28,2048]{2,1,0:T(8,128)(2,1)S(1)}, u32[]{:S(2)}, u32[]{:S(2)}) collective-permute-start(bf16[2,28,2048]{2,1,0:T(8,128)(2,1)S(1)} %collective-permute-done.6.refs_8_), channel_id=1, source_target_pairs={{0,2},{2,0},{4,6},{6,4},{8,10},{10,8},{12,14},{14,12},{16,18},{18,... | collective-permute-start | bytes 688136 | tf_op jit(solution)/shard_map/ppermute | solution.py:56
  29.5 1.8 %collective-permute-start.9 = (bf16[2,28,2048]{2,1,0:T(8,128)(2,1)S(1)}, bf16[2,28,2048]{2,1,0:T(8,128)(2,1)S(1)}, u32[]{:S(2)}, u32[]{:S(2)}) collective-permute-start(bf16[2,28,2048]{2,1,0:T(8,128)(2,1)S(1)} %collective-permute-done.8.refs_10_), channel_id=1, source_target_pairs={{0,2},{2,0},{4,6},{6,4},{8,10},{10,8},{12,14},{14,12},{16,18},{18,... | collective-permute-start | bytes 688136 | tf_op jit(solution)/shard_map/ppermute | solution.py:56
  38.9 3.2 %collective-permute-start.10 = (bf16[4,28,2048]{2,1,0:T(8,128)(2,1)S(1)}, bf16[4,28,2048]{2,1,0:T(8,128)(2,1)S(1)}, u32[]{:S(2)}, u32[]{:S(2)}) collective-permute-start(bf16[4,28,2048]{2,1,0:T(8,128)(2,1)S(1)} %get-tuple-element.45), channel_id=1, source_target_pairs={{0,2},{2,0},{4,6},{6,4},{8,10},{10,8},{12,14},{14,12},{16,18},{18,... | collective-permute-start | bytes 1376264 | tf_op jit(solution)/shard_map/ppermute | solution.py:56
  39.1 22.3 %copy-start.1 = (bf16[128,2048]{1,0:T(8,128)(2,1)S(1)}, bf16[128,2048]{1,0:T(8,128)(2,1)}, u32[]{:S(2)}) copy-start(bf16[128,2048]{1,0:T(8,128)(2,1)} %grad.1) | copy-start | bytes 1572868
  41.7 4.2 %collective-permute-start.15 = (bf16[4,28,2048]{2,1,0:T(8,128)(2,1)S(1)}, bf16[4,28,2048]{2,1,0:T(8,128)(2,1)S(1)}, u32[]{:S(2)}, u32[]{:S(2)}) collective-permute-start(bf16[4,28,2048]{2,1,0:T(8,128)(2,1)S(1)} %get-tuple-element.48), channel_id=1, source_target_pairs={{0,2},{2,0},{4,6},{6,4},{8,10},{10,8},{12,14},{14,12},{16,18},{18,... | collective-permute-start | bytes 1376264 | tf_op jit(solution)/shard_map/ppermute | solution.py:56
  42.3 6.4 %collective-permute-start.13 = (bf16[28,2048]{1,0:T(8,128)(2,1)S(1)}, bf16[28,2048]{1,0:T(8,128)(2,1)S(1)}, u32[]{:S(2)}, u32[]{:S(2)}) collective-permute-start(bf16[28,2048]{1,0:T(8,128)(2,1)S(1)} %get-tuple-element.61), channel_id=1, source_target_pairs={{0,8},{2,10},{4,12},{6,14},{8,0},{10,2},{12,4},{14,6},{16,24},{18,... | collective-permute-start | bytes 344072 | tf_op jit(solution)/shard_map/ppermute | solution.py:56
  42.5 7.2 %collective-permute-start.12 = (bf16[28,2048]{1,0:T(8,128)(2,1)S(1)}, bf16[28,2048]{1,0:T(8,128)(2,1)S(1)}, u32[]{:S(2)}, u32[]{:S(2)}) collective-permute-start(bf16[28,2048]{1,0:T(8,128)(2,1)S(1)} %get-tuple-element.62), channel_id=1, source_target_pairs={{0,4},{2,6},{4,0},{6,2},{8,12},{10,14},{12,8},{14,10},{16,20},{18,... | collective-permute-start | bytes 344072 | tf_op jit(solution)/shard_map/ppermute | solution.py:56
  44.0 8.6 %collective-permute-start.11 = (bf16[28,2048]{1,0:T(8,128)(2,1)S(1)}, bf16[28,2048]{1,0:T(8,128)(2,1)S(1)}, u32[]{:S(2)}, u32[]{:S(2)}) collective-permute-start(bf16[28,2048]{1,0:T(8,128)(2,1)S(1)} %get-tuple-element.60), channel_id=1, source_target_pairs={{0,12},{2,14},{4,8},{6,10},{8,4},{10,6},{12,0},{14,2},{16,28},{18,... | collective-permute-start | bytes 344072 | tf_op jit(solution)/shard_map/ppermute | solution.py:56
  46.1 9.8 %collective-permute-start.18 = (bf16[28,2048]{1,0:T(8,128)(2,1)S(1)}, bf16[28,2048]{1,0:T(8,128)(2,1)S(1)}, u32[]{:S(2)}, u32[]{:S(2)}) collective-permute-start(bf16[28,2048]{1,0:T(8,128)(2,1)S(1)} %get-tuple-element.58), channel_id=1, source_target_pairs={{0,8},{2,10},{4,12},{6,14},{8,0},{10,2},{12,4},{14,6},{16,24},{18,... | collective-permute-start | bytes 344072 | tf_op jit(solution)/shard_map/ppermute | solution.py:56
  46.3 9.6 %collective-permute-start.17 = (bf16[28,2048]{1,0:T(8,128)(2,1)S(1)}, bf16[28,2048]{1,0:T(8,128)(2,1)S(1)}, u32[]{:S(2)}, u32[]{:S(2)}) collective-permute-start(bf16[28,2048]{1,0:T(8,128)(2,1)S(1)} %get-tuple-element.59), channel_id=1, source_target_pairs={{0,4},{2,6},{4,0},{6,2},{8,12},{10,14},{12,8},{14,10},{16,20},{18,... | collective-permute-start | bytes 344072 | tf_op jit(solution)/shard_map/ppermute | solution.py:56
  48.8 8.6 %collective-permute-start.16 = (bf16[28,2048]{1,0:T(8,128)(2,1)S(1)}, bf16[28,2048]{1,0:T(8,128)(2,1)S(1)}, u32[]{:S(2)}, u32[]{:S(2)}) collective-permute-start(bf16[28,2048]{1,0:T(8,128)(2,1)S(1)} %get-tuple-element.57), channel_id=1, source_target_pairs={{0,12},{2,14},{4,8},{6,10},{8,4},{10,6},{12,0},{14,2},{16,28},{18,... | collective-permute-start | bytes 344072 | tf_op jit(solution)/shard_map/ppermute | solution.py:56
  52.6 6.2 %collective-permute-start.14 = (bf16[28,2048]{1,0:T(8,128)(2,1)S(1)}, bf16[28,2048]{1,0:T(8,128)(2,1)S(1)}, u32[]{:S(2)}, u32[]{:S(2)}) collective-permute-start(bf16[28,2048]{1,0:T(8,128)(2,1)S(1)} %fusion.7), channel_id=1, source_target_pairs={{0,1},{1,0},{2,3},{3,2},{4,5},{5,4},{6,7},{7,6},{8,9},{9,8},{10,11... | collective-permute-start | bytes 344072 | tf_op jit(solution)/shard_map/ppermute | solution.py:379
  58.9 6.9 %collective-permute-start.19 = (bf16[28,2048]{1,0:T(8,128)(2,1)S(1)}, bf16[28,2048]{1,0:T(8,128)(2,1)S(1)}, u32[]{:S(2)}, u32[]{:S(2)}) collective-permute-start(bf16[28,2048]{1,0:T(8,128)(2,1)S(1)} %get-tuple-element.51), channel_id=1, source_target_pairs={{0,24},{2,26},{4,28},{6,30},{8,16},{10,18},{12,20},{14,22},{16,8},... | collective-permute-start | bytes 344072 | tf_op jit(solution)/shard_map/ppermute | solution.py:393

commit v6 on v5

--- a/solution.py
+++ b/solution.py
@@ -89,7 +89,7 @@
 def prepare_kernel(grad_from, picked_from, gates_from, saved_from, *refs):
     outs, edge, (grad, picked, gates, arrived) = refs[:-5], refs[-5], refs[-4:]
     expert_count = len(outs)
-    spare = saved_from.shape[0] - edge.shape[0]
+    spare = (saved_from.shape[0] - edge.shape[0]) // 16 * 16
     first = jnp.where(lax.axis_index("tensor") == 0, spare, 0)
     saved_rows = saved_from.at[pl.ds(pl.multiple_of(first, 16), edge.shape[0]), :]
     copies = [
@@ -327,7 +327,7 @@
 
     saved, edge, down_source = after_all((saved_hidden, edge, in_weight), [beside])
     before, after = [], []
-    if tensor_size == 2 and halo <= per_tensor:
+    if tensor_size == 2 and halo <= per_tensor and per_tensor % 16 == 0:
         before = after = [lax.ppermute(edge, "tensor", [(0, 1), (1, 0)])]
     else:
         for hop in range(1, -(-halo // per_tensor) + 1):

time: 67.1 us -> 67.1 us (level)
  no operation moved by 1% of the time
where the time goes in v6:
time: 67.1 us; the launch traced here: 66.9 us
  Pallas kernels  27 us (40%)
  starting transfers between devices  26.7 us (40%)
  waiting for transfers between devices  12.4 us (18%)
    pallas_call x9, Pallas kernels, kernel_call(): pl.pallas_call(body, out_shape=out_shape, in_specs=[LEFT] * left + [VMEM]...  27 us
    ppermute x15, starting transfers between devices, swap(): return lax.ppermute(values, 'loop', pairs)  11 us
    ppermute x15, waiting for transfers between devices, swap(): return lax.ppermute(values, 'loop', pairs)  7.05 us
    ppermute x2, starting transfers between devices, shards(): lax.ppermute(outgoing[turn], BOTH, routes[turn])  5.76 us
    ppermute x1, starting transfers between devices, shards(): before = after = [lax.ppermute(edge, 'tensor', [(0, 1), (1, 0)])]  4.22 us
    ppermute x1, waiting for transfers between devices, shards(): landed.append(lax.ppermute(sending, 'loop', pairs) if turn else sending)  3.9 us
    ppermute x1, starting transfers between devices, shards(): totals[turn] = lax.ppermute(totals[turn], 'tensor', pairs)  3.3 us
    ppermute x1, starting transfers between devices, shards(): landed.append(lax.ppermute(sending, 'loop', pairs) if turn else sending)  2.48 us
  transfers between devices with their start and end apart: 20, of which 8 were waited for; matrix products, arithmetic and copies ran while one was open for 1% of the time, Pallas kernels for 25%

profile of v6, /device:TPU:0, one launch (start us, length us, event | category | flops | bytes accessed | tf_op | source)
XLA Modules:
  0.0 66.9 jit_solution(592996800578773335)
XLA Ops:
  0.0 1.4 %shard_map.64 = (bf16[28,2048]{1,0:T(8,128)(2,1)S(1)}, bf16[28,2048]{1,0:T(8,128)(2,1)S(1)}, bf16[16,2048]{1,0:T(8,128)(2,1)S(1)}) custom-call(bf16[128,2048]{1,0:T(8,128)(2,1)} %grad.1, s32[2,416]{1,0:T(2,128)} %picked.3, f32[2,416]{1,0:T(2,128)} %gates_from.1, bf16[208,2048]{1,0:T(8,128)(2,1)} %refs_1_), custom_call_target="tpu_custom_call" | custom-call | bytes 1382912 | tf_op jit(solution)/shard_map/pallas_call | solution.py:38
  1.4 5.1 %collective-permute-start = (bf16[28,2048]{1,0:T(8,128)(2,1)S(1)}, bf16[28,2048]{1,0:T(8,128)(2,1)S(1)}, u32[]{:S(2)}, u32[]{:S(2)}) collective-permute-start(bf16[28,2048]{1,0:T(8,128)(2,1)S(1)} %get-tuple-element.29), channel_id=1, source_target_pairs={{0,24},{1,0},{2,26},{3,2},{4,28},{5,4},{6,30},{7,6},{8,16},{9,8},{... | collective-permute-start | bytes 344072 | tf_op jit(solution)/shard_map/ppermute | solution.py:309
  6.5 0.7 collective-permute-start.1
  7.2 5.9 %shard_map.65 = (bf16[1,2048,2048]{2,1,0:T(8,128)(2,1)S(1)}, bf16[1,2048,2048]{2,1,0:T(8,128)(2,1)S(1)}) custom-call(bf16[2048,4096]{1,0:T(8,128)(2,1)} %weight), custom_call_target="tpu_custom_call" | custom-call | bytes 16777216 | tf_op jit(solution)/shard_map/pallas_call | solution.py:38
  13.1 0.0 collective-permute-done.refs_0_
  13.1 0.0 collective-permute-done.1.refs_1_
  13.2 0.1 collective-permute-start.2
  13.3 1.6 %collective-permute-start.4 = (bf16[2,28,2048]{2,1,0:T(8,128)(2,1)S(1)}, bf16[2,28,2048]{2,1,0:T(8,128)(2,1)S(1)}, u32[]{:S(2)}, u32[]{:S(2)}) collective-permute-start(bf16[2,28,2048]{2,1,0:T(8,128)(2,1)S(1)} %shard_map.66.refs_4_), channel_id=1, source_target_pairs={{0,4},{2,6},{4,0},{6,2},{8,12},{10,14},{12,8},{14,10},{16,20},{18,... | collective-permute-start | bytes 688136 | tf_op jit(solution)/shard_map/ppermute | solution.py:56
  14.8 0.0 collective-permute-start.6
  14.8 2.0 %collective-permute-start.8 = (bf16[2,28,2048]{2,1,0:T(8,128)(2,1)S(1)}, bf16[2,28,2048]{2,1,0:T(8,128)(2,1)S(1)}, u32[]{:S(2)}, u32[]{:S(2)}) collective-permute-start(bf16[2,28,2048]{2,1,0:T(8,128)(2,1)S(1)} %shard_map.66.refs_4_), channel_id=1, source_target_pairs={{0,12},{2,14},{4,8},{6,10},{8,4},{10,6},{12,0},{14,2},{16,28},{18,... | collective-permute-start | bytes 688136 | tf_op jit(solution)/shard_map/ppermute | solution.py:56
  16.8 0.0 collective-permute-done.2.refs_5_
  16.8 0.0 copy-start
  16.8 0.0 copy-start.2
  16.8 4.2 %collective-permute-start.3 = (bf16[16,2048]{1,0:T(8,128)(2,1)S(1)}, bf16[16,2048]{1,0:T(8,128)(2,1)S(1)}, u32[]{:S(2)}, u32[]{:S(2)}) collective-permute-start(bf16[16,2048]{1,0:T(8,128)(2,1)S(1)} %get-tuple-element.38), channel_id=1, source_target_pairs={{0,1},{1,0},{2,3},{3,2},{4,5},{5,4},{6,7},{7,6},{8,9},{9,8},{10,11... | collective-permute-start | bytes 196616 | tf_op jit(solution)/shard_map/ppermute | solution.py:331
  21.0 5.9 %shard_map.67 = (bf16[1,2048,2048]{2,1,0:T(8,128)(2,1)S(1)}, bf16[1,2048,2048]{2,1,0:T(8,128)(2,1)S(1)}) custom-call(bf16[4096,2048]{1,0:T(8,128)(2,1)} %weight.1), custom_call_target="tpu_custom_call" | custom-call | bytes 16777216 | tf_op jit(solution)/shard_map/pallas_call | solution.py:38
  27.0 0.0 collective-permute-done.3.refs_0_.refs_2_
  27.0 0.0 copy-done
  27.0 0.0 copy-done.2
  27.0 2.0 %shard_map.68.refs_3_ = f32[224,2048]{1,0:T(8,128)S(1)} custom-call(s32[2,416]{1,0:T(2,128)S(1)} %copy-done.2, bf16[16,2048]{1,0:T(8,128)(2,1)S(1)} %collective-permute-done.3.refs_0_.refs_2_, bf16[208,2048]{1,0:T(8,128)(2,1)S(1)} %copy-done, bf16[16,2048]{1,0:T(8,128)(2,1)S(1)} %collective-permute-done.3.refs_0_.refs_2_), custom_call_target="tpu_custom_call" | custom-call | flops 220200960 | bytes 986368 | tf_op jit(solution)/shard_map/pallas_call | solution.py:38
  29.0 0.0 collective-permute-done.4.refs_6_
  29.0 0.1 collective-permute-start.5
  29.0 0.0 collective-permute-done.6.refs_8_
  29.1 0.5 collective-permute-start.7
  29.5 0.0 collective-permute-done.8.refs_10_
  29.5 0.1 collective-permute-start.9
  29.6 0.9 %collective-permute-done.5.refs_7_ = bf16[2,28,2048]{2,1,0:T(8,128)(2,1)S(1)} collective-permute-done((bf16[2,28,2048]{2,1,0:T(8,128)(2,1)S(1)}, bf16[2,28,2048]{2,1,0:T(8,128)(2,1)S(1)}, u32[]{:S(2)}, u32[]{:S(2)}) %collective-permute-start.5) | collective-permute-done | bytes 229408 | tf_op jit(solution)/shard_map/ppermute | solution.py:56
  30.6 0.4 collective-permute-done.7.refs_9_
  30.9 0.4 collective-permute-done.9.refs_11_
  31.3 7.6 %shard_map.69 = (bf16[224,2048]{1,0:T(8,128)(2,1)S(1)}, bf16[4,28,2048]{2,1,0:T(8,128)(2,1)S(1)}, bf16[4,28,2048]{2,1,0:T(8,128)(2,1)S(1)}) custom-call(bf16[1,2048,2048]{2,1,0:T(8,128)(2,1)S(1)} %get-tuple-element.31.refs_0_, bf16[1,2048,2048]{2,1,0:T(8,128)(2,1)S(1)} %get-tuple-element.32.refs_1_, bf16[1,2048,2048]{2,1,0:T(8,128)(2,1)S(1)} %get-tuple-element.37.refs_2_, ...), custom_call_target="tpu_custom_call" | custom-call | flops 5637144576 | bytes 28835840 | tf_op jit(solution)/shard_map/pallas_call | solution.py:38
  38.9 0.2 collective-permute-start.10
  39.1 0.0 copy-start.1
  39.1 2.6 %shard_map.70 = (bf16[4,28,2048]{2,1,0:T(8,128)(2,1)S(1)}, bf16[4,28,2048]{2,1,0:T(8,128)(2,1)S(1)}) custom-call(bf16[1,2048,2048]{2,1,0:T(8,128)(2,1)S(1)} %get-tuple-element.40.weight, bf16[224,2048]{1,0:T(8,128)(2,1)S(1)} %get-tuple-element.46.pre_grad), custom_call_target="tpu_custom_call" | custom-call | flops 1879048192 | bytes 9306112 | tf_op jit(solution)/shard_map/pallas_call | solution.py:38
  41.7 0.4 collective-permute-start.15
  42.1 0.0 collective-permute-done.10
  42.1 0.2 fusion.8
  42.3 0.2 collective-permute-start.13
  42.5 1.5 %collective-permute-start.12 = (bf16[28,2048]{1,0:T(8,128)(2,1)S(1)}, bf16[28,2048]{1,0:T(8,128)(2,1)S(1)}, u32[]{:S(2)}, u32[]{:S(2)}) collective-permute-start(bf16[28,2048]{1,0:T(8,128)(2,1)S(1)} %get-tuple-element.62), channel_id=1, source_target_pairs={{0,4},{2,6},{4,0},{6,2},{8,12},{10,14},{12,8},{14,10},{16,20},{18,... | collective-permute-start | bytes 344072 | tf_op jit(solution)/shard_map/ppermute | solution.py:56
  44.0 1.9 %collective-permute-start.11 = (bf16[28,2048]{1,0:T(8,128)(2,1)S(1)}, bf16[28,2048]{1,0:T(8,128)(2,1)S(1)}, u32[]{:S(2)}, u32[]{:S(2)}) collective-permute-start(bf16[28,2048]{1,0:T(8,128)(2,1)S(1)} %get-tuple-element.60), channel_id=1, source_target_pairs={{0,12},{2,14},{4,8},{6,10},{8,4},{10,6},{12,0},{14,2},{16,28},{18,... | collective-permute-start | bytes 344072 | tf_op jit(solution)/shard_map/ppermute | solution.py:56
  45.9 0.0 collective-permute-done.15
  45.9 0.2 convert_add_fusion
  46.1 0.2 collective-permute-start.18
  46.3 1.5 %collective-permute-start.17 = (bf16[28,2048]{1,0:T(8,128)(2,1)S(1)}, bf16[28,2048]{1,0:T(8,128)(2,1)S(1)}, u32[]{:S(2)}, u32[]{:S(2)}) collective-permute-start(bf16[28,2048]{1,0:T(8,128)(2,1)S(1)} %get-tuple-element.59), channel_id=1, source_target_pairs={{0,4},{2,6},{4,0},{6,2},{8,12},{10,14},{12,8},{14,10},{16,20},{18,... | collective-permute-start | bytes 344072 | tf_op jit(solution)/shard_map/ppermute | solution.py:56
  47.7 1.0 %collective-permute-done.13 = bf16[28,2048]{1,0:T(8,128)(2,1)S(1)} collective-permute-done((bf16[28,2048]{1,0:T(8,128)(2,1)S(1)}, bf16[28,2048]{1,0:T(8,128)(2,1)S(1)}, u32[]{:S(2)}, u32[]{:S(2)}) %collective-permute-start.13) | collective-permute-done | bytes 114720 | tf_op jit(solution)/shard_map/ppermute | solution.py:56
  48.8 0.9 %collective-permute-start.16 = (bf16[28,2048]{1,0:T(8,128)(2,1)S(1)}, bf16[28,2048]{1,0:T(8,128)(2,1)S(1)}, u32[]{:S(2)}, u32[]{:S(2)}) collective-permute-start(bf16[28,2048]{1,0:T(8,128)(2,1)S(1)} %get-tuple-element.57), channel_id=1, source_target_pairs={{0,12},{2,14},{4,8},{6,10},{8,4},{10,6},{12,0},{14,2},{16,28},{18,... | collective-permute-start | bytes 344072 | tf_op jit(solution)/shard_map/ppermute | solution.py:56
  49.7 0.0 collective-permute-done.12
  49.7 2.9 %collective-permute-done.11 = bf16[28,2048]{1,0:T(8,128)(2,1)S(1)} collective-permute-done((bf16[28,2048]{1,0:T(8,128)(2,1)S(1)}, bf16[28,2048]{1,0:T(8,128)(2,1)S(1)}, u32[]{:S(2)}, u32[]{:S(2)}) %collective-permute-start.11) | collective-permute-done | bytes 114720 | tf_op jit(solution)/shard_map/ppermute | solution.py:56
  52.5 0.1 fusion.7
  52.6 3.3 %collective-permute-start.14 = (bf16[28,2048]{1,0:T(8,128)(2,1)S(1)}, bf16[28,2048]{1,0:T(8,128)(2,1)S(1)}, u32[]{:S(2)}, u32[]{:S(2)}) collective-permute-start(bf16[28,2048]{1,0:T(8,128)(2,1)S(1)} %fusion.7), channel_id=1, source_target_pairs={{0,1},{1,0},{2,3},{3,2},{4,5},{5,4},{6,7},{7,6},{8,9},{9,8},{10,11... | collective-permute-start | bytes 344072 | tf_op jit(solution)/shard_map/ppermute | solution.py:379
  55.9 0.0 collective-permute-done.18
  55.9 0.0 collective-permute-done.17
  55.9 1.5 %collective-permute-done.16 = bf16[28,2048]{1,0:T(8,128)(2,1)S(1)} collective-permute-done((bf16[28,2048]{1,0:T(8,128)(2,1)S(1)}, bf16[28,2048]{1,0:T(8,128)(2,1)S(1)}, u32[]{:S(2)}, u32[]{:S(2)}) %collective-permute-start.16) | collective-permute-done | bytes 114720 | tf_op jit(solution)/shard_map/ppermute | solution.py:56
  57.3 1.5 %collective-permute-done.14 = bf16[28,2048]{1,0:T(8,128)(2,1)S(1)} collective-permute-done((bf16[28,2048]{1,0:T(8,128)(2,1)S(1)}, bf16[28,2048]{1,0:T(8,128)(2,1)S(1)}, u32[]{:S(2)}, u32[]{:S(2)}) %collective-permute-start.14) | collective-permute-done | bytes 114720 | tf_op jit(solution)/shard_map/ppermute | solution.py:379
  58.8 0.1 broadcast_select_fusion
  58.9 2.5 %collective-permute-start.19 = (bf16[28,2048]{1,0:T(8,128)(2,1)S(1)}, bf16[28,2048]{1,0:T(8,128)(2,1)S(1)}, u32[]{:S(2)}, u32[]{:S(2)}) collective-permute-start(bf16[28,2048]{1,0:T(8,128)(2,1)S(1)} %get-tuple-element.51), channel_id=1, source_target_pairs={{0,24},{2,26},{4,28},{6,30},{8,16},{10,18},{12,20},{14,22},{16,8},... | collective-permute-start | bytes 344072 | tf_op jit(solution)/shard_map/ppermute | solution.py:393
  61.4 0.0 copy-done.1
  61.4 0.5 shard_map.71
  62.0 3.9 %collective-permute-done.19.refs_0_ = bf16[28,2048]{1,0:T(8,128)(2,1)S(1)} collective-permute-done((bf16[28,2048]{1,0:T(8,128)(2,1)S(1)}, bf16[28,2048]{1,0:T(8,128)(2,1)S(1)}, u32[]{:S(2)}, u32[]{:S(2)}) %collective-permute-start.19) | collective-permute-done | bytes 114720 | tf_op jit(solution)/shard_map/ppermute | solution.py:393
  65.9 1.0 %shard_map.72 = bf16[128,2048]{1,0:T(8,128)(2,1)} custom-call(f32[128,2048]{1,0:T(8,128)S(1)} %get-tuple-element.49.total, bf16[1,32,128]{2,1,0:T(8,128)(2,1)S(1)} %get-tuple-element.50.chosen, bf16[28,2048]{1,0:T(8,128)(2,1)S(1)} %collective-permute-done.19.refs_0_), custom_call_target="tpu_custom_call" | custom-call | bytes 1171456 | tf_op jit(solution)/shard_map/pallas_call | solution.py:38
  (4 shorter events, 0.1 us)
Async XLA Ops:
  1.4 11.7 %collective-permute-start = (bf16[28,2048]{1,0:T(8,128)(2,1)S(1)}, bf16[28,2048]{1,0:T(8,128)(2,1)S(1)}, u32[]{:S(2)}, u32[]{:S(2)}) collective-permute-start(bf16[28,2048]{1,0:T(8,128)(2,1)S(1)} %get-tuple-element.29), channel_id=1, source_target_pairs={{0,24},{1,0},{2,26},{3,2},{4,28},{5,4},{6,30},{7,6},{8,16},{9,8},{... | collective-permute-start | bytes 344072 | tf_op jit(solution)/shard_map/ppermute | solution.py:309
  6.5 6.6 %collective-permute-start.1 = (bf16[28,2048]{1,0:T(8,128)(2,1)S(1)}, bf16[28,2048]{1,0:T(8,128)(2,1)S(1)}, u32[]{:S(2)}, u32[]{:S(2)}) collective-permute-start(bf16[28,2048]{1,0:T(8,128)(2,1)S(1)} %get-tuple-element.28), channel_id=1, source_target_pairs={{0,0},{1,24},{2,2},{3,26},{4,4},{5,28},{6,6},{7,30},{8,8},{9,16},{... | collective-permute-start | bytes 344072 | tf_op jit(solution)/shard_map/ppermute | solution.py:309
  13.2 3.6 %collective-permute-start.2 = (bf16[2,28,2048]{2,1,0:T(8,128)(2,1)S(1)}, bf16[2,28,2048]{2,1,0:T(8,128)(2,1)S(1)}, u32[]{:S(2)}, u32[]{:S(2)}) collective-permute-start(bf16[2,28,2048]{2,1,0:T(8,128)(2,1)S(1)} %shard_map.66.refs_4_), channel_id=1, source_target_pairs={{0,2},{2,0},{4,6},{6,4},{8,10},{10,8},{12,14},{14,12},{16,18},{18,... | collective-permute-start | bytes 688136 | tf_op jit(solution)/shard_map/ppermute | solution.py:56
  13.3 15.7 %collective-permute-start.4 = (bf16[2,28,2048]{2,1,0:T(8,128)(2,1)S(1)}, bf16[2,28,2048]{2,1,0:T(8,128)(2,1)S(1)}, u32[]{:S(2)}, u32[]{:S(2)}) collective-permute-start(bf16[2,28,2048]{2,1,0:T(8,128)(2,1)S(1)} %shard_map.66.refs_4_), channel_id=1, source_target_pairs={{0,4},{2,6},{4,0},{6,2},{8,12},{10,14},{12,8},{14,10},{16,20},{18,... | collective-permute-start | bytes 688136 | tf_op jit(solution)/shard_map/ppermute | solution.py:56
  14.8 14.2 %collective-permute-start.6 = (bf16[2,28,2048]{2,1,0:T(8,128)(2,1)S(1)}, bf16[2,28,2048]{2,1,0:T(8,128)(2,1)S(1)}, u32[]{:S(2)}, u32[]{:S(2)}) collective-permute-start(bf16[2,28,2048]{2,1,0:T(8,128)(2,1)S(1)} %shard_map.66.refs_4_), channel_id=1, source_target_pairs={{0,8},{2,10},{4,12},{6,14},{8,0},{10,2},{12,4},{14,6},{16,24},{18,... | collective-permute-start | bytes 688136 | tf_op jit(solution)/shard_map/ppermute | solution.py:56
  14.8 14.7 %collective-permute-start.8 = (bf16[2,28,2048]{2,1,0:T(8,128)(2,1)S(1)}, bf16[2,28,2048]{2,1,0:T(8,128)(2,1)S(1)}, u32[]{:S(2)}, u32[]{:S(2)}) collective-permute-start(bf16[2,28,2048]{2,1,0:T(8,128)(2,1)S(1)} %shard_map.66.refs_4_), channel_id=1, source_target_pairs={{0,12},{2,14},{4,8},{6,10},{8,4},{10,6},{12,0},{14,2},{16,28},{18,... | collective-permute-start | bytes 688136 | tf_op jit(solution)/shard_map/ppermute | solution.py:56
  16.8 10.2 %copy-start = (bf16[208,2048]{1,0:T(8,128)(2,1)S(1)}, bf16[208,2048]{1,0:T(8,128)(2,1)}, u32[]{:S(2)}) copy-start(bf16[208,2048]{1,0:T(8,128)(2,1)} %refs_1_) | copy-start | bytes 2555908
  16.8 10.2 %copy-start.2 = (s32[2,416]{1,0:T(2,128)S(1)}, s32[2,416]{1,0:T(2,128)}, u32[]{:S(2)}) copy-start(s32[2,416]{1,0:T(2,128)} %picked.3) | copy-start | bytes 9988
  16.8 10.2 %collective-permute-start.3 = (bf16[16,2048]{1,0:T(8,128)(2,1)S(1)}, bf16[16,2048]{1,0:T(8,128)(2,1)S(1)}, u32[]{:S(2)}, u32[]{:S(2)}) collective-permute-start(bf16[16,2048]{1,0:T(8,128)(2,1)S(1)} %get-tuple-element.38), channel_id=1, source_target_pairs={{0,1},{1,0},{2,3},{3,2},{4,5},{5,4},{6,7},{7,6},{8,9},{9,8},{10,11... | collective-permute-start | bytes 196616 | tf_op jit(solution)/shard_map/ppermute | solution.py:331
  29.0 1.6 %collective-permute-start.5 = (bf16[2,28,2048]{2,1,0:T(8,128)(2,1)S(1)}, bf16[2,28,2048]{2,1,0:T(8,128)(2,1)S(1)}, u32[]{:S(2)}, u32[]{:S(2)}) collective-permute-start(bf16[2,28,2048]{2,1,0:T(8,128)(2,1)S(1)} %collective-permute-done.4.refs_6_), channel_id=1, source_target_pairs={{0,2},{2,0},{4,6},{6,4},{8,10},{10,8},{12,14},{14,12},{16,18},{18,... | collective-permute-start | bytes 688136 | tf_op jit(solution)/shard_map/ppermute | solution.py:56
  29.1 1.9 %collective-permute-start.7 = (bf16[2,28,2048]{2,1,0:T(8,128)(2,1)S(1)}, bf16[2,28,2048]{2,1,0:T(8,128)(2,1)S(1)}, u32[]{:S(2)}, u32[]{:S(2)}) collective-permute-start(bf16[2,28,2048]{2,1,0:T(8,128)(2,1)S(1)} %collective-permute-done.6.refs_8_), channel_id=1, source_target_pairs={{0,2},{2,0},{4,6},{6,4},{8,10},{10,8},{12,14},{14,12},{16,18},{18,... | collective-permute-start | bytes 688136 | tf_op jit(solution)/shard_map/ppermute | solution.py:56
  29.5 1.8 %collective-permute-start.9 = (bf16[2,28,2048]{2,1,0:T(8,128)(2,1)S(1)}, bf16[2,28,2048]{2,1,0:T(8,128)(2,1)S(1)}, u32[]{:S(2)}, u32[]{:S(2)}) collective-permute-start(bf16[2,28,2048]{2,1,0:T(8,128)(2,1)S(1)} %collective-permute-done.8.refs_10_), channel_id=1, source_target_pairs={{0,2},{2,0},{4,6},{6,4},{8,10},{10,8},{12,14},{14,12},{16,18},{18,... | collective-permute-start | bytes 688136 | tf_op jit(solution)/shard_map/ppermute | solution.py:56
  38.9 3.2 %collective-permute-start.10 = (bf16[4,28,2048]{2,1,0:T(8,128)(2,1)S(1)}, bf16[4,28,2048]{2,1,0:T(8,128)(2,1)S(1)}, u32[]{:S(2)}, u32[]{:S(2)}) collective-permute-start(bf16[4,28,2048]{2,1,0:T(8,128)(2,1)S(1)} %get-tuple-element.45), channel_id=1, source_target_pairs={{0,2},{2,0},{4,6},{6,4},{8,10},{10,8},{12,14},{14,12},{16,18},{18,... | collective-permute-start | bytes 1376264 | tf_op jit(solution)/shard_map/ppermute | solution.py:56
  39.1 22.3 %copy-start.1 = (bf16[128,2048]{1,0:T(8,128)(2,1)S(1)}, bf16[128,2048]{1,0:T(8,128)(2,1)}, u32[]{:S(2)}) copy-start(bf16[128,2048]{1,0:T(8,128)(2,1)} %grad.1) | copy-start | bytes 1572868
  41.7 4.2 %collective-permute-start.15 = (bf16[4,28,2048]{2,1,0:T(8,128)(2,1)S(1)}, bf16[4,28,2048]{2,1,0:T(8,128)(2,1)S(1)}, u32[]{:S(2)}, u32[]{:S(2)}) collective-permute-start(bf16[4,28,2048]{2,1,0:T(8,128)(2,1)S(1)} %get-tuple-element.48), channel_id=1, source_target_pairs={{0,2},{2,0},{4,6},{6,4},{8,10},{10,8},{12,14},{14,12},{16,18},{18,... | collective-permute-start | bytes 1376264 | tf_op jit(solution)/shard_map/ppermute | solution.py:56
  42.3 6.4 %collective-permute-start.13 = (bf16[28,2048]{1,0:T(8,128)(2,1)S(1)}, bf16[28,2048]{1,0:T(8,128)(2,1)S(1)}, u32[]{:S(2)}, u32[]{:S(2)}) collective-permute-start(bf16[28,2048]{1,0:T(8,128)(2,1)S(1)} %get-tuple-element.61), channel_id=1, source_target_pairs={{0,8},{2,10},{4,12},{6,14},{8,0},{10,2},{12,4},{14,6},{16,24},{18,... | collective-permute-start | bytes 344072 | tf_op jit(solution)/shard_map/ppermute | solution.py:56
  42.5 7.2 %collective-permute-start.12 = (bf16[28,2048]{1,0:T(8,128)(2,1)S(1)}, bf16[28,2048]{1,0:T(8,128)(2,1)S(1)}, u32[]{:S(2)}, u32[]{:S(2)}) collective-permute-start(bf16[28,2048]{1,0:T(8,128)(2,1)S(1)} %get-tuple-element.62), channel_id=1, source_target_pairs={{0,4},{2,6},{4,0},{6,2},{8,12},{10,14},{12,8},{14,10},{16,20},{18,... | collective-permute-start | bytes 344072 | tf_op jit(solution)/shard_map/ppermute | solution.py:56
  44.0 8.6 %collective-permute-start.11 = (bf16[28,2048]{1,0:T(8,128)(2,1)S(1)}, bf16[28,2048]{1,0:T(8,128)(2,1)S(1)}, u32[]{:S(2)}, u32[]{:S(2)}) collective-permute-start(bf16[28,2048]{1,0:T(8,128)(2,1)S(1)} %get-tuple-element.60), channel_id=1, source_target_pairs={{0,12},{2,14},{4,8},{6,10},{8,4},{10,6},{12,0},{14,2},{16,28},{18,... | collective-permute-start | bytes 344072 | tf_op jit(solution)/shard_map/ppermute | solution.py:56
  46.1 9.8 %collective-permute-start.18 = (bf16[28,2048]{1,0:T(8,128)(2,1)S(1)}, bf16[28,2048]{1,0:T(8,128)(2,1)S(1)}, u32[]{:S(2)}, u32[]{:S(2)}) collective-permute-start(bf16[28,2048]{1,0:T(8,128)(2,1)S(1)} %get-tuple-element.58), channel_id=1, source_target_pairs={{0,8},{2,10},{4,12},{6,14},{8,0},{10,2},{12,4},{14,6},{16,24},{18,... | collective-permute-start | bytes 344072 | tf_op jit(solution)/shard_map/ppermute | solution.py:56
  46.3 9.6 %collective-permute-start.17 = (bf16[28,2048]{1,0:T(8,128)(2,1)S(1)}, bf16[28,2048]{1,0:T(8,128)(2,1)S(1)}, u32[]{:S(2)}, u32[]{:S(2)}) collective-permute-start(bf16[28,2048]{1,0:T(8,128)(2,1)S(1)} %get-tuple-element.59), channel_id=1, source_target_pairs={{0,4},{2,6},{4,0},{6,2},{8,12},{10,14},{12,8},{14,10},{16,20},{18,... | collective-permute-start | bytes 344072 | tf_op jit(solution)/shard_map/ppermute | solution.py:56
  48.8 8.6 %collective-permute-start.16 = (bf16[28,2048]{1,0:T(8,128)(2,1)S(1)}, bf16[28,2048]{1,0:T(8,128)(2,1)S(1)}, u32[]{:S(2)}, u32[]{:S(2)}) collective-permute-start(bf16[28,2048]{1,0:T(8,128)(2,1)S(1)} %get-tuple-element.57), channel_id=1, source_target_pairs={{0,12},{2,14},{4,8},{6,10},{8,4},{10,6},{12,0},{14,2},{16,28},{18,... | collective-permute-start | bytes 344072 | tf_op jit(solution)/shard_map/ppermute | solution.py:56
  52.6 6.2 %collective-permute-start.14 = (bf16[28,2048]{1,0:T(8,128)(2,1)S(1)}, bf16[28,2048]{1,0:T(8,128)(2,1)S(1)}, u32[]{:S(2)}, u32[]{:S(2)}) collective-permute-start(bf16[28,2048]{1,0:T(8,128)(2,1)S(1)} %fusion.7), channel_id=1, source_target_pairs={{0,1},{1,0},{2,3},{3,2},{4,5},{5,4},{6,7},{7,6},{8,9},{9,8},{10,11... | collective-permute-start | bytes 344072 | tf_op jit(solution)/shard_map/ppermute | solution.py:379
  58.9 6.9 %collective-permute-start.19 = (bf16[28,2048]{1,0:T(8,128)(2,1)S(1)}, bf16[28,2048]{1,0:T(8,128)(2,1)S(1)}, u32[]{:S(2)}, u32[]{:S(2)}) collective-permute-start(bf16[28,2048]{1,0:T(8,128)(2,1)S(1)} %get-tuple-element.51), channel_id=1, source_target_pairs={{0,24},{2,26},{4,28},{6,30},{8,16},{10,18},{12,20},{14,22},{16,8},... | collective-permute-start | bytes 344072 | tf_op jit(solution)/shard_map/ppermute | solution.py:393

commit v7 on v6

--- a/solution.py
+++ b/solution.py
@@ -124,7 +124,6 @@
 
 
 def place_rows(chosen, rows, held):
-    held[...] = jnp.zeros_like(held)
     held[:MOST, :] = rows[...]
     return lax.dot_general(chosen, held[...], (((0,), (0,)), ((), ())), preferred_element_type=jnp.float32)
 
@@ -135,6 +134,7 @@
     home_rows = grad.shape[0]
     start = lax.axis_index("loop") * home_rows
     total[...] = grad[...].astype(jnp.float32)
+    held[...] = jnp.zeros_like(held)
     for turn in range(expert_count):
         expert = landed_expert(turn, blocks, expert_count)
         _, tokens = home_slots(picked[pl.ds(expert, 1), :], start, home_rows)
@@ -147,6 +147,7 @@
 def finish_kernel(total, chosen, *refs):
     landed, (out, held, ready, sent) = refs[:-4], refs[-4:]
     parts, _, step = ready.shape
+    held[...] = jnp.zeros_like(held)
     copies = []
     for part in range(parts):
         columns = pl.ds(part * step, step)
@@ -228,7 +229,7 @@
 def up_product(sizes, slope, weights, pieces, gathered, pre_grad):
     blocks, splits = sizes[:2]
     hidden = slope.shape[1]
-    step = min(512, hidden)
+    step = min(256, hidden)
     for turn in range(len(weights)):
         for split in range(splits):
             for at in range(blocks):

time: 67.1 us -> 67.1 us (level)
  no operation moved by 1% of the time
where the time goes in v7:
time: 67.1 us; the launch traced here: 66.9 us
  Pallas kernels  27 us (40%)
  starting transfers between devices  26.7 us (40%)
  waiting for transfers between devices  12.4 us (18%)
    pallas_call x9, Pallas kernels, kernel_call(): pl.pallas_call(body, out_shape=out_shape, in_specs=[LEFT] * left + [VMEM]...  27 us
    ppermute x15, starting transfers between devices, swap(): return lax.ppermute(values, 'loop', pairs)  11 us
    ppermute x15, waiting for transfers between devices, swap(): return lax.ppermute(values, 'loop', pairs)  7.05 us
    ppermute x2, starting transfers between devices, shards(): lax.ppermute(outgoing[turn], BOTH, routes[turn])  5.76 us
    ppermute x1, starting transfers between devices, shards(): before = after = [lax.ppermute(edge, 'tensor', [(0, 1), (1, 0)])]  4.22 us
    ppermute x1, waiting for transfers between devices, shards(): landed.append(lax.ppermute(sending, 'loop', pairs) if turn else sending)  3.9 us
    ppermute x1, starting transfers between devices, shards(): totals[turn] = lax.ppermute(totals[turn], 'tensor', pairs)  3.3 us
    ppermute x1, starting transfers between devices, shards(): landed.append(lax.ppermute(sending, 'loop', pairs) if turn else sending)  2.48 us
  transfers between devices with their start and end apart: 20, of which 8 were waited for; matrix products, arithmetic and copies ran while one was open for 1% of the time, Pallas kernels for 25%

profile of v7, /device:TPU:0, one launch (start us, length us, event | category | flops | bytes accessed | tf_op | source)
XLA Modules:
  0.0 66.9 jit_solution(9576136187027099082)
XLA Ops:
  0.0 1.4 %shard_map.64 = (bf16[28,2048]{1,0:T(8,128)(2,1)S(1)}, bf16[28,2048]{1,0:T(8,128)(2,1)S(1)}, bf16[16,2048]{1,0:T(8,128)(2,1)S(1)}) custom-call(bf16[128,2048]{1,0:T(8,128)(2,1)} %grad.1, s32[2,416]{1,0:T(2,128)} %picked.3, f32[2,416]{1,0:T(2,128)} %gates_from.1, bf16[208,2048]{1,0:T(8,128)(2,1)} %refs_1_), custom_call_target="tpu_custom_call" | custom-call | bytes 1382912 | tf_op jit(solution)/shard_map/pallas_call | solution.py:38
  1.4 5.1 %collective-permute-start = (bf16[28,2048]{1,0:T(8,128)(2,1)S(1)}, bf16[28,2048]{1,0:T(8,128)(2,1)S(1)}, u32[]{:S(2)}, u32[]{:S(2)}) collective-permute-start(bf16[28,2048]{1,0:T(8,128)(2,1)S(1)} %get-tuple-element.29), channel_id=1, source_target_pairs={{0,24},{1,0},{2,26},{3,2},{4,28},{5,4},{6,30},{7,6},{8,16},{9,8},{... | collective-permute-start | bytes 344072 | tf_op jit(solution)/shard_map/ppermute | solution.py:310
  6.5 0.7 collective-permute-start.1
  7.2 5.9 %shard_map.65 = (bf16[1,2048,2048]{2,1,0:T(8,128)(2,1)S(1)}, bf16[1,2048,2048]{2,1,0:T(8,128)(2,1)S(1)}) custom-call(bf16[2048,4096]{1,0:T(8,128)(2,1)} %weight), custom_call_target="tpu_custom_call" | custom-call | bytes 16777216 | tf_op jit(solution)/shard_map/pallas_call | solution.py:38
  13.1 0.0 collective-permute-done.refs_0_
  13.1 0.0 collective-permute-done.1.refs_1_
  13.2 0.1 collective-permute-start.2
  13.3 1.6 %collective-permute-start.4 = (bf16[2,28,2048]{2,1,0:T(8,128)(2,1)S(1)}, bf16[2,28,2048]{2,1,0:T(8,128)(2,1)S(1)}, u32[]{:S(2)}, u32[]{:S(2)}) collective-permute-start(bf16[2,28,2048]{2,1,0:T(8,128)(2,1)S(1)} %shard_map.66.refs_4_), channel_id=1, source_target_pairs={{0,4},{2,6},{4,0},{6,2},{8,12},{10,14},{12,8},{14,10},{16,20},{18,... | collective-permute-start | bytes 688136 | tf_op jit(solution)/shard_map/ppermute | solution.py:56
  14.8 0.0 collective-permute-start.6
  14.8 2.0 %collective-permute-start.8 = (bf16[2,28,2048]{2,1,0:T(8,128)(2,1)S(1)}, bf16[2,28,2048]{2,1,0:T(8,128)(2,1)S(1)}, u32[]{:S(2)}, u32[]{:S(2)}) collective-permute-start(bf16[2,28,2048]{2,1,0:T(8,128)(2,1)S(1)} %shard_map.66.refs_4_), channel_id=1, source_target_pairs={{0,12},{2,14},{4,8},{6,10},{8,4},{10,6},{12,0},{14,2},{16,28},{18,... | collective-permute-start | bytes 688136 | tf_op jit(solution)/shard_map/ppermute | solution.py:56
  16.8 0.0 collective-permute-done.2.refs_5_
  16.8 0.0 copy-start
  16.8 0.0 copy-start.2
  16.8 4.2 %collective-permute-start.3 = (bf16[16,2048]{1,0:T(8,128)(2,1)S(1)}, bf16[16,2048]{1,0:T(8,128)(2,1)S(1)}, u32[]{:S(2)}, u32[]{:S(2)}) collective-permute-start(bf16[16,2048]{1,0:T(8,128)(2,1)S(1)} %get-tuple-element.38), channel_id=1, source_target_pairs={{0,1},{1,0},{2,3},{3,2},{4,5},{5,4},{6,7},{7,6},{8,9},{9,8},{10,11... | collective-permute-start | bytes 196616 | tf_op jit(solution)/shard_map/ppermute | solution.py:332
  21.0 5.9 %shard_map.67 = (bf16[1,2048,2048]{2,1,0:T(8,128)(2,1)S(1)}, bf16[1,2048,2048]{2,1,0:T(8,128)(2,1)S(1)}) custom-call(bf16[4096,2048]{1,0:T(8,128)(2,1)} %weight.1), custom_call_target="tpu_custom_call" | custom-call | bytes 16777216 | tf_op jit(solution)/shard_map/pallas_call | solution.py:38
  27.0 0.0 collective-permute-done.3.refs_0_.refs_2_
  27.0 0.0 copy-done
  27.0 0.0 copy-done.2
  27.0 2.0 %shard_map.68.refs_3_ = f32[224,2048]{1,0:T(8,128)S(1)} custom-call(s32[2,416]{1,0:T(2,128)S(1)} %copy-done.2, bf16[16,2048]{1,0:T(8,128)(2,1)S(1)} %collective-permute-done.3.refs_0_.refs_2_, bf16[208,2048]{1,0:T(8,128)(2,1)S(1)} %copy-done, bf16[16,2048]{1,0:T(8,128)(2,1)S(1)} %collective-permute-done.3.refs_0_.refs_2_), custom_call_target="tpu_custom_call" | custom-call | flops 220200960 | bytes 986368 | tf_op jit(solution)/shard_map/pallas_call | solution.py:38
  29.0 0.0 collective-permute-done.4.refs_6_
  29.0 0.1 collective-permute-start.5
  29.0 0.0 collective-permute-done.6.refs_8_
  29.1 0.5 collective-permute-start.7
  29.5 0.0 collective-permute-done.8.refs_10_
  29.5 0.1 collective-permute-start.9
  29.6 0.9 %collective-permute-done.5.refs_7_ = bf16[2,28,2048]{2,1,0:T(8,128)(2,1)S(1)} collective-permute-done((bf16[2,28,2048]{2,1,0:T(8,128)(2,1)S(1)}, bf16[2,28,2048]{2,1,0:T(8,128)(2,1)S(1)}, u32[]{:S(2)}, u32[]{:S(2)}) %collective-permute-start.5) | collective-permute-done | bytes 229408 | tf_op jit(solution)/shard_map/ppermute | solution.py:56
  30.6 0.4 collective-permute-done.7.refs_9_
  30.9 0.4 collective-permute-done.9.refs_11_
  31.3 7.6 %shard_map.69 = (bf16[224,2048]{1,0:T(8,128)(2,1)S(1)}, bf16[4,28,2048]{2,1,0:T(8,128)(2,1)S(1)}, bf16[4,28,2048]{2,1,0:T(8,128)(2,1)S(1)}) custom-call(bf16[1,2048,2048]{2,1,0:T(8,128)(2,1)S(1)} %get-tuple-element.31.refs_0_, bf16[1,2048,2048]{2,1,0:T(8,128)(2,1)S(1)} %get-tuple-element.32.refs_1_, bf16[1,2048,2048]{2,1,0:T(8,128)(2,1)S(1)} %get-tuple-element.37.refs_2_, ...), custom_call_target="tpu_custom_call" | custom-call | flops 5637144576 | bytes 28835840 | tf_op jit(solution)/shard_map/pallas_call | solution.py:38
  38.9 0.2 collective-permute-start.10
  39.1 0.0 copy-start.1
  39.1 2.6 %shard_map.70 = (bf16[4,28,2048]{2,1,0:T(8,128)(2,1)S(1)}, bf16[4,28,2048]{2,1,0:T(8,128)(2,1)S(1)}) custom-call(bf16[1,2048,2048]{2,1,0:T(8,128)(2,1)S(1)} %get-tuple-element.40.weight, bf16[224,2048]{1,0:T(8,128)(2,1)S(1)} %get-tuple-element.46.pre_grad), custom_call_target="tpu_custom_call" | custom-call | flops 1879048192 | bytes 9306112 | tf_op jit(solution)/shard_map/pallas_call | solution.py:38
  41.7 0.4 collective-permute-start.15
  42.1 0.0 collective-permute-done.10
  42.1 0.2 fusion.8
  42.3 0.2 collective-permute-start.13
  42.5 1.5 %collective-permute-start.12 = (bf16[28,2048]{1,0:T(8,128)(2,1)S(1)}, bf16[28,2048]{1,0:T(8,128)(2,1)S(1)}, u32[]{:S(2)}, u32[]{:S(2)}) collective-permute-start(bf16[28,2048]{1,0:T(8,128)(2,1)S(1)} %get-tuple-element.62), channel_id=1, source_target_pairs={{0,4},{2,6},{4,0},{6,2},{8,12},{10,14},{12,8},{14,10},{16,20},{18,... | collective-permute-start | bytes 344072 | tf_op jit(solution)/shard_map/ppermute | solution.py:56
  44.0 1.9 %collective-permute-start.11 = (bf16[28,2048]{1,0:T(8,128)(2,1)S(1)}, bf16[28,2048]{1,0:T(8,128)(2,1)S(1)}, u32[]{:S(2)}, u32[]{:S(2)}) collective-permute-start(bf16[28,2048]{1,0:T(8,128)(2,1)S(1)} %get-tuple-element.60), channel_id=1, source_target_pairs={{0,12},{2,14},{4,8},{6,10},{8,4},{10,6},{12,0},{14,2},{16,28},{18,... | collective-permute-start | bytes 344072 | tf_op jit(solution)/shard_map/ppermute | solution.py:56
  45.9 0.0 collective-permute-done.15
  45.9 0.2 convert_add_fusion
  46.1 0.2 collective-permute-start.18
  46.3 1.5 %collective-permute-start.17 = (bf16[28,2048]{1,0:T(8,128)(2,1)S(1)}, bf16[28,2048]{1,0:T(8,128)(2,1)S(1)}, u32[]{:S(2)}, u32[]{:S(2)}) collective-permute-start(bf16[28,2048]{1,0:T(8,128)(2,1)S(1)} %get-tuple-element.59), channel_id=1, source_target_pairs={{0,4},{2,6},{4,0},{6,2},{8,12},{10,14},{12,8},{14,10},{16,20},{18,... | collective-permute-start | bytes 344072 | tf_op jit(solution)/shard_map/ppermute | solution.py:56
  47.7 1.0 %collective-permute-done.13 = bf16[28,2048]{1,0:T(8,128)(2,1)S(1)} collective-permute-done((bf16[28,2048]{1,0:T(8,128)(2,1)S(1)}, bf16[28,2048]{1,0:T(8,128)(2,1)S(1)}, u32[]{:S(2)}, u32[]{:S(2)}) %collective-permute-start.13) | collective-permute-done | bytes 114720 | tf_op jit(solution)/shard_map/ppermute | solution.py:56
  48.8 0.9 %collective-permute-start.16 = (bf16[28,2048]{1,0:T(8,128)(2,1)S(1)}, bf16[28,2048]{1,0:T(8,128)(2,1)S(1)}, u32[]{:S(2)}, u32[]{:S(2)}) collective-permute-start(bf16[28,2048]{1,0:T(8,128)(2,1)S(1)} %get-tuple-element.57), channel_id=1, source_target_pairs={{0,12},{2,14},{4,8},{6,10},{8,4},{10,6},{12,0},{14,2},{16,28},{18,... | collective-permute-start | bytes 344072 | tf_op jit(solution)/shard_map/ppermute | solution.py:56
  49.7 0.0 collective-permute-done.12
  49.7 2.9 %collective-permute-done.11 = bf16[28,2048]{1,0:T(8,128)(2,1)S(1)} collective-permute-done((bf16[28,2048]{1,0:T(8,128)(2,1)S(1)}, bf16[28,2048]{1,0:T(8,128)(2,1)S(1)}, u32[]{:S(2)}, u32[]{:S(2)}) %collective-permute-start.11) | collective-permute-done | bytes 114720 | tf_op jit(solution)/shard_map/ppermute | solution.py:56
  52.5 0.1 fusion.7
  52.6 3.3 %collective-permute-start.14 = (bf16[28,2048]{1,0:T(8,128)(2,1)S(1)}, bf16[28,2048]{1,0:T(8,128)(2,1)S(1)}, u32[]{:S(2)}, u32[]{:S(2)}) collective-permute-start(bf16[28,2048]{1,0:T(8,128)(2,1)S(1)} %fusion.7), channel_id=1, source_target_pairs={{0,1},{1,0},{2,3},{3,2},{4,5},{5,4},{6,7},{7,6},{8,9},{9,8},{10,11... | collective-permute-start | bytes 344072 | tf_op jit(solution)/shard_map/ppermute | solution.py:380
  55.9 0.0 collective-permute-done.18
  55.9 0.0 collective-permute-done.17
  55.9 1.5 %collective-permute-done.16 = bf16[28,2048]{1,0:T(8,128)(2,1)S(1)} collective-permute-done((bf16[28,2048]{1,0:T(8,128)(2,1)S(1)}, bf16[28,2048]{1,0:T(8,128)(2,1)S(1)}, u32[]{:S(2)}, u32[]{:S(2)}) %collective-permute-start.16) | collective-permute-done | bytes 114720 | tf_op jit(solution)/shard_map/ppermute | solution.py:56
  57.3 1.5 %collective-permute-done.14 = bf16[28,2048]{1,0:T(8,128)(2,1)S(1)} collective-permute-done((bf16[28,2048]{1,0:T(8,128)(2,1)S(1)}, bf16[28,2048]{1,0:T(8,128)(2,1)S(1)}, u32[]{:S(2)}, u32[]{:S(2)}) %collective-permute-start.14) | collective-permute-done | bytes 114720 | tf_op jit(solution)/shard_map/ppermute | solution.py:380
  58.8 0.1 broadcast_select_fusion
  58.9 2.5 %collective-permute-start.19 = (bf16[28,2048]{1,0:T(8,128)(2,1)S(1)}, bf16[28,2048]{1,0:T(8,128)(2,1)S(1)}, u32[]{:S(2)}, u32[]{:S(2)}) collective-permute-start(bf16[28,2048]{1,0:T(8,128)(2,1)S(1)} %get-tuple-element.51), channel_id=1, source_target_pairs={{0,24},{2,26},{4,28},{6,30},{8,16},{10,18},{12,20},{14,22},{16,8},... | collective-permute-start | bytes 344072 | tf_op jit(solution)/shard_map/ppermute | solution.py:394
  61.4 0.0 copy-done.1
  61.4 0.5 shard_map.71
  62.0 3.9 %collective-permute-done.19.refs_0_ = bf16[28,2048]{1,0:T(8,128)(2,1)S(1)} collective-permute-done((bf16[28,2048]{1,0:T(8,128)(2,1)S(1)}, bf16[28,2048]{1,0:T(8,128)(2,1)S(1)}, u32[]{:S(2)}, u32[]{:S(2)}) %collective-permute-start.19) | collective-permute-done | bytes 114720 | tf_op jit(solution)/shard_map/ppermute | solution.py:394
  65.9 1.0 %shard_map.72 = bf16[128,2048]{1,0:T(8,128)(2,1)} custom-call(f32[128,2048]{1,0:T(8,128)S(1)} %get-tuple-element.49.total, bf16[1,32,128]{2,1,0:T(8,128)(2,1)S(1)} %get-tuple-element.50.chosen, bf16[28,2048]{1,0:T(8,128)(2,1)S(1)} %collective-permute-done.19.refs_0_), custom_call_target="tpu_custom_call" | custom-call | bytes 1171456 | tf_op jit(solution)/shard_map/pallas_call | solution.py:38
  (4 shorter events, 0.1 us)
Async XLA Ops:
  1.4 11.7 %collective-permute-start = (bf16[28,2048]{1,0:T(8,128)(2,1)S(1)}, bf16[28,2048]{1,0:T(8,128)(2,1)S(1)}, u32[]{:S(2)}, u32[]{:S(2)}) collective-permute-start(bf16[28,2048]{1,0:T(8,128)(2,1)S(1)} %get-tuple-element.29), channel_id=1, source_target_pairs={{0,24},{1,0},{2,26},{3,2},{4,28},{5,4},{6,30},{7,6},{8,16},{9,8},{... | collective-permute-start | bytes 344072 | tf_op jit(solution)/shard_map/ppermute | solution.py:310
  6.5 6.6 %collective-permute-start.1 = (bf16[28,2048]{1,0:T(8,128)(2,1)S(1)}, bf16[28,2048]{1,0:T(8,128)(2,1)S(1)}, u32[]{:S(2)}, u32[]{:S(2)}) collective-permute-start(bf16[28,2048]{1,0:T(8,128)(2,1)S(1)} %get-tuple-element.28), channel_id=1, source_target_pairs={{0,0},{1,24},{2,2},{3,26},{4,4},{5,28},{6,6},{7,30},{8,8},{9,16},{... | collective-permute-start | bytes 344072 | tf_op jit(solution)/shard_map/ppermute | solution.py:310
  13.2 3.6 %collective-permute-start.2 = (bf16[2,28,2048]{2,1,0:T(8,128)(2,1)S(1)}, bf16[2,28,2048]{2,1,0:T(8,128)(2,1)S(1)}, u32[]{:S(2)}, u32[]{:S(2)}) collective-permute-start(bf16[2,28,2048]{2,1,0:T(8,128)(2,1)S(1)} %shard_map.66.refs_4_), channel_id=1, source_target_pairs={{0,2},{2,0},{4,6},{6,4},{8,10},{10,8},{12,14},{14,12},{16,18},{18,... | collective-permute-start | bytes 688136 | tf_op jit(solution)/shard_map/ppermute | solution.py:56
  13.3 15.7 %collective-permute-start.4 = (bf16[2,28,2048]{2,1,0:T(8,128)(2,1)S(1)}, bf16[2,28,2048]{2,1,0:T(8,128)(2,1)S(1)}, u32[]{:S(2)}, u32[]{:S(2)}) collective-permute-start(bf16[2,28,2048]{2,1,0:T(8,128)(2,1)S(1)} %shard_map.66.refs_4_), channel_id=1, source_target_pairs={{0,4},{2,6},{4,0},{6,2},{8,12},{10,14},{12,8},{14,10},{16,20},{18,... | collective-permute-start | bytes 688136 | tf_op jit(solution)/shard_map/ppermute | solution.py:56
  14.8 14.2 %collective-permute-start.6 = (bf16[2,28,2048]{2,1,0:T(8,128)(2,1)S(1)}, bf16[2,28,2048]{2,1,0:T(8,128)(2,1)S(1)}, u32[]{:S(2)}, u32[]{:S(2)}) collective-permute-start(bf16[2,28,2048]{2,1,0:T(8,128)(2,1)S(1)} %shard_map.66.refs_4_), channel_id=1, source_target_pairs={{0,8},{2,10},{4,12},{6,14},{8,0},{10,2},{12,4},{14,6},{16,24},{18,... | collective-permute-start | bytes 688136 | tf_op jit(solution)/shard_map/ppermute | solution.py:56
  14.8 14.7 %collective-permute-start.8 = (bf16[2,28,2048]{2,1,0:T(8,128)(2,1)S(1)}, bf16[2,28,2048]{2,1,0:T(8,128)(2,1)S(1)}, u32[]{:S(2)}, u32[]{:S(2)}) collective-permute-start(bf16[2,28,2048]{2,1,0:T(8,128)(2,1)S(1)} %shard_map.66.refs_4_), channel_id=1, source_target_pairs={{0,12},{2,14},{4,8},{6,10},{8,4},{10,6},{12,0},{14,2},{16,28},{18,... | collective-permute-start | bytes 688136 | tf_op jit(solution)/shard_map/ppermute | solution.py:56
  16.8 10.2 %copy-start = (bf16[208,2048]{1,0:T(8,128)(2,1)S(1)}, bf16[208,2048]{1,0:T(8,128)(2,1)}, u32[]{:S(2)}) copy-start(bf16[208,2048]{1,0:T(8,128)(2,1)} %refs_1_) | copy-start | bytes 2555908
  16.8 10.2 %copy-start.2 = (s32[2,416]{1,0:T(2,128)S(1)}, s32[2,416]{1,0:T(2,128)}, u32[]{:S(2)}) copy-start(s32[2,416]{1,0:T(2,128)} %picked.3) | copy-start | bytes 9988
  16.8 10.2 %collective-permute-start.3 = (bf16[16,2048]{1,0:T(8,128)(2,1)S(1)}, bf16[16,2048]{1,0:T(8,128)(2,1)S(1)}, u32[]{:S(2)}, u32[]{:S(2)}) collective-permute-start(bf16[16,2048]{1,0:T(8,128)(2,1)S(1)} %get-tuple-element.38), channel_id=1, source_target_pairs={{0,1},{1,0},{2,3},{3,2},{4,5},{5,4},{6,7},{7,6},{8,9},{9,8},{10,11... | collective-permute-start | bytes 196616 | tf_op jit(solution)/shard_map/ppermute | solution.py:332
  29.0 1.6 %collective-permute-start.5 = (bf16[2,28,2048]{2,1,0:T(8,128)(2,1)S(1)}, bf16[2,28,2048]{2,1,0:T(8,128)(2,1)S(1)}, u32[]{:S(2)}, u32[]{:S(2)}) collective-permute-start(bf16[2,28,2048]{2,1,0:T(8,128)(2,1)S(1)} %collective-permute-done.4.refs_6_), channel_id=1, source_target_pairs={{0,2},{2,0},{4,6},{6,4},{8,10},{10,8},{12,14},{14,12},{16,18},{18,... | collective-permute-start | bytes 688136 | tf_op jit(solution)/shard_map/ppermute | solution.py:56
  29.1 1.9 %collective-permute-start.7 = (bf16[2,28,2048]{2,1,0:T(8,128)(2,1)S(1)}, bf16[2,28,2048]{2,1,0:T(8,128)(2,1)S(1)}, u32[]{:S(2)}, u32[]{:S(2)}) collective-permute-start(bf16[2,28,2048]{2,1,0:T(8,128)(2,1)S(1)} %collective-permute-done.6.refs_8_), channel_id=1, source_target_pairs={{0,2},{2,0},{4,6},{6,4},{8,10},{10,8},{12,14},{14,12},{16,18},{18,... | collective-permute-start | bytes 688136 | tf_op jit(solution)/shard_map/ppermute | solution.py:56
  29.5 1.8 %collective-permute-start.9 = (bf16[2,28,2048]{2,1,0:T(8,128)(2,1)S(1)}, bf16[2,28,2048]{2,1,0:T(8,128)(2,1)S(1)}, u32[]{:S(2)}, u32[]{:S(2)}) collective-permute-start(bf16[2,28,2048]{2,1,0:T(8,128)(2,1)S(1)} %collective-permute-done.8.refs_10_), channel_id=1, source_target_pairs={{0,2},{2,0},{4,6},{6,4},{8,10},{10,8},{12,14},{14,12},{16,18},{18,... | collective-permute-start | bytes 688136 | tf_op jit(solution)/shard_map/ppermute | solution.py:56
  38.9 3.2 %collective-permute-start.10 = (bf16[4,28,2048]{2,1,0:T(8,128)(2,1)S(1)}, bf16[4,28,2048]{2,1,0:T(8,128)(2,1)S(1)}, u32[]{:S(2)}, u32[]{:S(2)}) collective-permute-start(bf16[4,28,2048]{2,1,0:T(8,128)(2,1)S(1)} %get-tuple-element.45), channel_id=1, source_target_pairs={{0,2},{2,0},{4,6},{6,4},{8,10},{10,8},{12,14},{14,12},{16,18},{18,... | collective-permute-start | bytes 1376264 | tf_op jit(solution)/shard_map/ppermute | solution.py:56
  39.1 22.3 %copy-start.1 = (bf16[128,2048]{1,0:T(8,128)(2,1)S(1)}, bf16[128,2048]{1,0:T(8,128)(2,1)}, u32[]{:S(2)}) copy-start(bf16[128,2048]{1,0:T(8,128)(2,1)} %grad.1) | copy-start | bytes 1572868
  41.7 4.2 %collective-permute-start.15 = (bf16[4,28,2048]{2,1,0:T(8,128)(2,1)S(1)}, bf16[4,28,2048]{2,1,0:T(8,128)(2,1)S(1)}, u32[]{:S(2)}, u32[]{:S(2)}) collective-permute-start(bf16[4,28,2048]{2,1,0:T(8,128)(2,1)S(1)} %get-tuple-element.48), channel_id=1, source_target_pairs={{0,2},{2,0},{4,6},{6,4},{8,10},{10,8},{12,14},{14,12},{16,18},{18,... | collective-permute-start | bytes 1376264 | tf_op jit(solution)/shard_map/ppermute | solution.py:56
  42.3 6.4 %collective-permute-start.13 = (bf16[28,2048]{1,0:T(8,128)(2,1)S(1)}, bf16[28,2048]{1,0:T(8,128)(2,1)S(1)}, u32[]{:S(2)}, u32[]{:S(2)}) collective-permute-start(bf16[28,2048]{1,0:T(8,128)(2,1)S(1)} %get-tuple-element.61), channel_id=1, source_target_pairs={{0,8},{2,10},{4,12},{6,14},{8,0},{10,2},{12,4},{14,6},{16,24},{18,... | collective-permute-start | bytes 344072 | tf_op jit(solution)/shard_map/ppermute | solution.py:56
  42.5 7.2 %collective-permute-start.12 = (bf16[28,2048]{1,0:T(8,128)(2,1)S(1)}, bf16[28,2048]{1,0:T(8,128)(2,1)S(1)}, u32[]{:S(2)}, u32[]{:S(2)}) collective-permute-start(bf16[28,2048]{1,0:T(8,128)(2,1)S(1)} %get-tuple-element.62), channel_id=1, source_target_pairs={{0,4},{2,6},{4,0},{6,2},{8,12},{10,14},{12,8},{14,10},{16,20},{18,... | collective-permute-start | bytes 344072 | tf_op jit(solution)/shard_map/ppermute | solution.py:56
  44.0 8.6 %collective-permute-start.11 = (bf16[28,2048]{1,0:T(8,128)(2,1)S(1)}, bf16[28,2048]{1,0:T(8,128)(2,1)S(1)}, u32[]{:S(2)}, u32[]{:S(2)}) collective-permute-start(bf16[28,2048]{1,0:T(8,128)(2,1)S(1)} %get-tuple-element.60), channel_id=1, source_target_pairs={{0,12},{2,14},{4,8},{6,10},{8,4},{10,6},{12,0},{14,2},{16,28},{18,... | collective-permute-start | bytes 344072 | tf_op jit(solution)/shard_map/ppermute | solution.py:56
  46.1 9.8 %collective-permute-start.18 = (bf16[28,2048]{1,0:T(8,128)(2,1)S(1)}, bf16[28,2048]{1,0:T(8,128)(2,1)S(1)}, u32[]{:S(2)}, u32[]{:S(2)}) collective-permute-start(bf16[28,2048]{1,0:T(8,128)(2,1)S(1)} %get-tuple-element.58), channel_id=1, source_target_pairs={{0,8},{2,10},{4,12},{6,14},{8,0},{10,2},{12,4},{14,6},{16,24},{18,... | collective-permute-start | bytes 344072 | tf_op jit(solution)/shard_map/ppermute | solution.py:56
  46.3 9.6 %collective-permute-start.17 = (bf16[28,2048]{1,0:T(8,128)(2,1)S(1)}, bf16[28,2048]{1,0:T(8,128)(2,1)S(1)}, u32[]{:S(2)}, u32[]{:S(2)}) collective-permute-start(bf16[28,2048]{1,0:T(8,128)(2,1)S(1)} %get-tuple-element.59), channel_id=1, source_target_pairs={{0,4},{2,6},{4,0},{6,2},{8,12},{10,14},{12,8},{14,10},{16,20},{18,... | collective-permute-start | bytes 344072 | tf_op jit(solution)/shard_map/ppermute | solution.py:56
  48.8 8.6 %collective-permute-start.16 = (bf16[28,2048]{1,0:T(8,128)(2,1)S(1)}, bf16[28,2048]{1,0:T(8,128)(2,1)S(1)}, u32[]{:S(2)}, u32[]{:S(2)}) collective-permute-start(bf16[28,2048]{1,0:T(8,128)(2,1)S(1)} %get-tuple-element.57), channel_id=1, source_target_pairs={{0,12},{2,14},{4,8},{6,10},{8,4},{10,6},{12,0},{14,2},{16,28},{18,... | collective-permute-start | bytes 344072 | tf_op jit(solution)/shard_map/ppermute | solution.py:56
  52.6 6.2 %collective-permute-start.14 = (bf16[28,2048]{1,0:T(8,128)(2,1)S(1)}, bf16[28,2048]{1,0:T(8,128)(2,1)S(1)}, u32[]{:S(2)}, u32[]{:S(2)}) collective-permute-start(bf16[28,2048]{1,0:T(8,128)(2,1)S(1)} %fusion.7), channel_id=1, source_target_pairs={{0,1},{1,0},{2,3},{3,2},{4,5},{5,4},{6,7},{7,6},{8,9},{9,8},{10,11... | collective-permute-start | bytes 344072 | tf_op jit(solution)/shard_map/ppermute | solution.py:380
  58.9 6.9 %collective-permute-start.19 = (bf16[28,2048]{1,0:T(8,128)(2,1)S(1)}, bf16[28,2048]{1,0:T(8,128)(2,1)S(1)}, u32[]{:S(2)}, u32[]{:S(2)}) collective-permute-start(bf16[28,2048]{1,0:T(8,128)(2,1)S(1)} %get-tuple-element.51), channel_id=1, source_target_pairs={{0,24},{2,26},{4,28},{6,30},{8,16},{10,18},{12,20},{14,22},{16,8},... | collective-permute-start | bytes 344072 | tf_op jit(solution)/shard_map/ppermute | solution.py:394
